TPU v7x, 128 devices: a whole 4x4x4 slice. The times are simulated.
128 devices in a mesh: dp: 16 (over y, x_hi, core), mp: 8 (over z, x_lo).
Axes of the slice: x: 4 (x_hi: 2, x_lo: 2; x = x_hi * 2 + x_lo), y: 4, z: 4, core: 2. Of those that a mesh axis runs over, the one named last changes fastest.
Arguments:
- tokens: bfloat16 [2, 8192, 1024], P(None, ('dp', 'mp')), may hold values from -6 to 6
- segment_ids: int32 [2, 8192], P(None, 'dp'), may hold values from 0 to 3, as said below
- cotangent: bfloat16 [2, 8192, 1024], P(None, ('dp', 'mp')), may hold values from -6 to 6
- w_query: bfloat16 [1024, 1024], P('dp', 'mp'), may hold values from -0.1875 to 0.1875
- w_key: bfloat16 [1024, 512], P('dp', 'mp'), may hold values from -0.1875 to 0.1875
- w_value: bfloat16 [1024, 512], P('dp', 'mp'), may hold values from -0.1875 to 0.1875
- w_out: bfloat16 [1024, 1024], P('mp', 'dp'), may hold values from -1.5 to 1.5
- w_gate: bfloat16 [1024, 4608], P('dp', 'mp'), may hold values from -0.1875 to 0.1875
- w_up: bfloat16 [1024, 4608], P('dp', 'mp'), may hold values from -0.1875 to 0.1875
- w_down: bfloat16 [4608, 1024], P('mp', 'dp'), may hold values from -0.09375 to 0.09375
- norm_gain: float32 [1024], replicated, may hold values from 0.5 to 1.5
- ffn_gain: float32 [1024], replicated, may hold values from 0.5 to 1.5
- query_gain: float32 [64], replicated, may hold values from 0.1 to 1.9
- key_gain: float32 [64], replicated, may hold values from 0.1 to 1.9
Outputs:
- output: bfloat16 [2, 8192, 1024], P(None, ('dp', 'mp'))
- input_grad: bfloat16 [2, 8192, 1024], P(None, ('dp', 'mp'))
- grad_query: float32 [1024, 1024], P('dp', 'mp')
- grad_key: float32 [1024, 512], P('dp', 'mp')
- grad_value: float32 [1024, 512], P('dp', 'mp')
- grad_out: float32 [1024, 1024], P('mp', 'dp')
- grad_gate: float32 [1024, 4608], P('dp', 'mp')
- grad_up: float32 [1024, 4608], P('dp', 'mp')
- grad_down: float32 [4608, 1024], P('mp', 'dp')
- grad_norm: float32 [1024], replicated
- grad_ffn_norm: float32 [1024], replicated
- grad_query_gain: float32 [64], replicated
- grad_key_gain: float32 [64], replicated
Inputs may be any that keep to these rules, and one draw needn't show every extreme that they name: `segment_ids`: in each micro-batch each data group's 512 tokens hold 1 to 4 whole sequences, numbered 0, 1, ... in order; in each micro-batch some group holds a single sequence and some group holds four.
All inputs are finite; a program needn't handle non-finite values.
Results may differ from a plain program's by a relative error of at most 0.025.
Values may be sent and summed in bfloat16 or wider, within the bound.
No kernel may reach another device: no remote copies, remote signals or barrier semaphores. Data moves between devices by JAX's collectives and lax.ppermute only.
A program may use at most 128 MiB of HBM per device.

v0:
```python
import jax
import jax.numpy as jnp
from jax import lax
from jax.experimental import pallas as pl
from jax.experimental.pallas import tpu as pltpu
from jax.sharding import Mesh, PartitionSpec as P

eps = 1e-05
rope_base = 1000000.0
axes = ("y", "xh", "core", "z", "xl")
plane = ("y", "xh", "xl")
CORE = [(0, 1), (1, 0)]
bf16 = jnp.bfloat16
f32 = jnp.float32
VMEM = 60 * 2**20


def product(left, right):
    return jnp.dot(left, right, preferred_element_type=jnp.float32)


def product_nt(left, right):
    return lax.dot_general(
        left, right, (((1,), (1,)), ((), ())), preferred_element_type=jnp.float32
    )


def product_tn(left, right):
    return lax.dot_general(
        left, right, (((0,), (0,)), ((), ())), preferred_element_type=jnp.float32
    )


def rms_scale(value):
    return lax.rsqrt(jnp.mean(value * value, axis=-1, keepdims=True) + eps)


def rms_rows(value, gain):
    return value * rms_scale(value) * gain


def swap(value):
    return lax.ppermute(
        value, ("core", "xl"), [(a * 2 + b, b * 2 + a) for a in range(2) for b in range(2)]
    )


def from_z(value, k):
    return lax.ppermute(value, "z", [(z, (z - k) % 4) for z in range(4)])


def swap_from_z(value, k):
    perm = [
        (a * 8 + z * 2 + b, b * 8 + ((z - k) % 4) * 2 + a)
        for a in range(2)
        for z in range(4)
        for b in range(2)
    ]
    return lax.ppermute(value, ("core", "z", "xl"), perm)


def swap_from_x(value, k):
    perm = []
    for xh in range(2):
        for a in range(2):
            for b in range(2):
                x = (xh * 2 + a - k) % 4
                perm.append((xh * 4 + a * 2 + b, (x // 2) * 4 + b * 2 + x % 2))
    return lax.ppermute(value, ("xh", "core", "xl"), perm)


def from_y(value, k):
    return lax.ppermute(value, "y", [(y, (y - k) % 4) for y in range(4)])


def other_core(value):
    return lax.ppermute(value, "core", CORE)


def from_chain(value):
    return [value] + [from_z(value, k) for k in (1, 2, 3)]


def gather_chains(pieces):
    chain = jnp.stack(pieces)
    return chain, other_core(chain)


def gather(value):
    chain = [value] + [from_z(value, k) for k in (1, 2, 3)]
    return chain + [other_core(v) for v in chain]


def ordered(value, z, core, axis):
    shape = value.shape
    block = shape[axis] // 8
    v = value.reshape(shape[:axis] + (4, 2, block) + shape[axis + 1 :])
    v = lax.dynamic_slice_in_dim(jnp.concatenate([v, v], axis), z, 4, axis)
    v = lax.dynamic_slice_in_dim(jnp.concatenate([v, v], axis + 1), core, 2, axis + 1)
    return jnp.swapaxes(v, axis, axis + 1).reshape(shape)


def group_sum(value):
    value = value + other_core(value)
    return value + sum(from_z(value, k) for k in (1, 2, 3))


def tie(*values):
    return lax.optimization_barrier(values)


def halves(value):
    lane = lax.broadcasted_iota(jnp.int32, value.shape, value.ndim - 1)
    return lane < 64


def quarter(value):
    lane = lax.broadcasted_iota(jnp.int32, value.shape, value.ndim - 1)
    return (lane & 32) == 0


def turn(value):
    return jnp.where(quarter(value), -pltpu.roll(value, 96, 1), pltpu.roll(value, 32, 1))


def turn_back(value):
    return jnp.where(quarter(value), pltpu.roll(value, 96, 1), -pltpu.roll(value, 32, 1))


def head_mean(value):
    low = halves(value)
    first = jnp.sum(jnp.where(low, value, 0.0), axis=-1, keepdims=True)
    second = jnp.sum(jnp.where(low, 0.0, value), axis=-1, keepdims=True)
    return jnp.where(low, first, second) * (1.0 / 64)


def attend_kernel(at_ref, *refs):
    x_refs, w_refs = refs[:2], refs[2:6]
    gain_ref, qk_gain_ref, cos_ref, sin_ref, bias_ref = refs[6:11]
    mixed_ref, x_ref, normed_ref, w_ref, raw_ref, q_ref, kk_ref, vv_ref, stat_ref = refs[11:]

    @pl.when(pl.program_id(0) == 0)
    def _():
        for ky in range(4):
            for kx in range(4):
                row = lax.rem(at_ref[0] + ky, 4) * 256 + lax.rem(at_ref[1] + kx, 4) * 64
                row = pl.multiple_of(row, 64)
                w_ref[pl.ds(row, 64), :] = w_refs[ky][kx * 64 : kx * 64 + 64, :]

    for i in range(8):
        block = x_refs[i // 4][i % 4, 0]
        x_ref[i * 64 : i * 64 + 64, :] = block
        block = block.astype(f32)
        normed_ref[i * 64 : i * 64 + 64, :] = (
            block * rms_scale(block) * gain_ref[0:1, :]
        ).astype(bf16)
    raw = product(normed_ref[...], w_ref[:, :256])
    raw_ref[...] = raw
    cosine, sine = cos_ref[0], sin_ref[0]
    query, kv = raw[:, :128], raw[:, 128:]
    low = halves(kv)
    query = query * lax.rsqrt(head_mean(query * query) + eps) * qk_gain_ref[0:1, :]
    q_ref[...] = (query * cosine + turn(query) * sine).astype(bf16)
    key = kv * lax.rsqrt(head_mean(kv * kv) + eps) * qk_gain_ref[1:2, :]
    key = key * cosine + turn(key) * sine
    kk_ref[...] = jnp.where(low, key, pltpu.roll(key, 64, 1)).astype(bf16)
    vv_ref[...] = jnp.where(low, pltpu.roll(kv, 64, 1), kv).astype(bf16)
    keys, values = kk_ref[...], vv_ref[...]
    for rows in (slice(0, 256), slice(256, 512)):
        queries = q_ref[rows, :]
        low = halves(queries)
        bias = bias_ref[0, rows, :].astype(f32)
        parts = []
        for head in range(2):
            one = jnp.where(low == (head == 0), queries, jnp.zeros_like(queries))
            scores = product_nt(one, keys) * 0.125 + bias
            top = jnp.max(scores, axis=-1, keepdims=True)
            expo = jnp.exp(scores - top)
            total = jnp.sum(expo, axis=-1, keepdims=True)
            weights = (expo * (1.0 / total)).astype(bf16)
            parts.append((product(weights, values), top + jnp.log(total)))
        first = halves(parts[0][0])
        mixed_ref[rows, :] = jnp.where(first, parts[0][0], parts[1][0]).astype(bf16)
        stat_ref[rows, :] = jnp.where(first, parts[0][1], parts[1][1])


def attend(at, pieces, weights, gain, qk_gain, cosine, sine, bias):
    width = pieces[0].shape[3]
    micro = pieces[0].shape[1]
    group = 512
    chain = pl.BlockSpec((4, 1, 64, width), lambda m, at: (0, m, 0, 0))
    whole = lambda a: pl.BlockSpec(a.shape, lambda m, at: (0,) * a.ndim)
    part = lambda a: pl.BlockSpec((1,) + a.shape[1:], lambda m, at: (m, 0, 0))
    rows = lambda cols: pl.BlockSpec((group, cols), lambda m, at: (m, 0))
    out = lambda cols, kind: jax.ShapeDtypeStruct((micro * group, cols), kind)
    return pl.pallas_call(
        attend_kernel,
        grid_spec=pltpu.PrefetchScalarGridSpec(
            num_scalar_prefetch=1,
            grid=(micro,),
            in_specs=[chain, chain]
            + [whole(w) for w in weights]
            + [whole(gain), whole(qk_gain), part(cosine), part(sine), part(bias)],
            out_specs=[
                rows(128),
                rows(width),
                rows(width),
                pl.BlockSpec((width, 384), lambda m, at: (0, 0)),
                rows(256),
                rows(128),
                rows(128),
                rows(128),
                rows(128),
            ],
        ),
        out_shape=[
            out(128, bf16),
            out(width, bf16),
            out(width, bf16),
            jax.ShapeDtypeStruct((width, 384), bf16),
            out(256, f32),
            out(128, bf16),
            out(128, bf16),
            out(128, bf16),
            out(128, f32),
        ],
        compiler_params=pltpu.CompilerParams(vmem_limit_bytes=VMEM),
        cost_estimate=pl.CostEstimate(flops=2 * 10**9, bytes_accessed=10**7, transcendentals=10**6),
        name="attend",
    )(at, *pieces, *weights, gain, qk_gain, cosine, sine, bias)


def feed_kernel(at_ref, *refs):
    mixed_refs, w_refs = refs[:8], refs[8:10]
    x_ref, gain_ref, wf_ref = refs[10:13]
    up_refs = refs[13:15]
    state_ref, second_ref, inner_ref, low_ref, own_ref, other_ref = refs[15:21]
    up_ref, down_own_ref, down_other_ref = refs[21:24]
    w_out, mixed, w_gu = refs[24:]
    step = pl.program_id(0)
    micro, side = step // 2, lax.rem(step, 2)

    @pl.when(step == 0)
    def _():
        for i in range(8):
            for ky in range(4):
                for kx in range(4):
                    row = lax.rem(at_ref[0] + ky, 4) * 256 + lax.rem(at_ref[1] + kx, 4) * 64
                    row = pl.multiple_of(row, 64)
                    w_out[pl.ds(row, 64), i * 128 : i * 128 + 128] = w_refs[i // 4][
                        i % 4, ky * 256 + kx * 64 : ky * 256 + kx * 64 + 64, :
                    ]
        for rows in (slice(i, i + 128) for i in range(0, w_gu.shape[0], 128)):
            w_gu[rows, :512] = wf_ref[rows, :512]
            rest = wf_ref[rows, 512:1152].astype(f32)
            w_gu[rows, 512:] = pltpu.roll(rest, 576, 1).astype(bf16)

    for i, ref in enumerate(up_refs):

        @pl.when(side == i)
        def _():
            for j in range(4):
                up_ref[j * 64 : j * 64 + 64, :] = ref[j, 0]

    for i, ref in enumerate(mixed_refs):
        flip, k = i // 4, i % 4
        base = micro * 512 + lax.rem(side + flip, 2) * 256
        for j in range(4):
            row = pl.multiple_of(base + (j - k) % 4 * 64, 64)
            mixed[j * 64 : j * 64 + 64, i * 128 : i * 128 + 128] = ref[pl.ds(row, 64), :]
    state = x_ref[...].astype(f32) + product_nt(mixed[...], w_out[...])
    state_ref[...] = state[:64]
    second = (state * rms_scale(state) * gain_ref[0:1, :]).astype(bf16)
    second_ref[...] = second
    both = product(second, w_gu[...])
    grad_inner = product(up_ref[...], wf_ref[:, 1152:1728])

    def glu(gate, up, grad):
        sig = 1.0 / (1.0 + jnp.exp(-gate))
        silu = gate * sig
        inner = (silu * up).astype(bf16)
        grad_gate = (grad * up * sig * (1.0 + gate * (1.0 - sig))).astype(bf16)
        return inner, grad_gate, (grad * silu).astype(bf16)

    inner, grad_gate, grad_up = glu(both[:, :512], both[:, 512:1024], grad_inner[:, :512])
    inner_ref[:, :512] = inner
    low_ref[:, :512] = grad_gate
    low_ref[:, 512:1024] = grad_up
    tail = both[:, 1024:]
    gate_tail = pltpu.roll(tail, 64, 1)
    inner, grad_gate, grad_up = glu(gate_tail[:, :64], tail[:, :64], grad_inner[:, 512:])
    inner_ref[:, 512:] = inner
    low_ref[:, 1024:1088] = grad_up
    low_ref[:, 1088:] = grad_gate
    grad = product_nt(low_ref[...], w_gu[...]).astype(bf16)
    down = product_nt(inner_ref[...], wf_ref[:, 1152:]).astype(bf16)

    @pl.when(side == 0)
    def _():
        own_ref[0] = grad
        down_own_ref[0] = down

    @pl.when(side == 1)
    def _():
        other_ref[0] = grad
        down_other_ref[0] = down


def feed(at, mixed, w_out, x, cotangent, gain, w_ffn):
    count, width = x.shape
    steps = count // 256
    whole = lambda a: pl.BlockSpec(a.shape, lambda b, at: (0,) * a.ndim)
    rows = lambda cols, block=256: pl.BlockSpec((block, cols), lambda b, at: (b, 0))
    half = pl.BlockSpec((1, 256, width), lambda b, at: (b // 2, 0, 0))
    out = lambda shape, kind: jax.ShapeDtypeStruct(shape, kind)

    chain = pl.BlockSpec((4, 1, 64, width), lambda b, at: (0, b // 2, 0, 0))
    return pl.pallas_call(
        feed_kernel,
        grid_spec=pltpu.PrefetchScalarGridSpec(
            num_scalar_prefetch=1,
            grid=(steps,),
            in_specs=[whole(p) for p in mixed]
            + [whole(w) for w in w_out]
            + [rows(width), whole(gain), whole(w_ffn)]
            + [chain, chain],
            out_specs=[rows(width, 64), rows(width), rows(576), rows(1152)]
            + [half, half, rows(width), half, half],
            scratch_shapes=[
                pltpu.VMEM((width, 1024), bf16),
                pltpu.VMEM((256, 1024), bf16),
                pltpu.VMEM((width, 1152), bf16),
            ],
        ),
        out_shape=[
            out((steps * 64, width), f32),
            out((count, width), bf16),
            out((count, 576), bf16),
            out((count, 1152), bf16),
            out((steps // 2, 256, width), bf16),
            out((steps // 2, 256, width), bf16),
            out((count, width), bf16),
            out((steps // 2, 256, width), bf16),
            out((steps // 2, 256, width), bf16),
        ],
        compiler_params=pltpu.CompilerParams(vmem_limit_bytes=VMEM),
        cost_estimate=pl.CostEstimate(flops=9 * 10**9, bytes_accessed=10**7, transcendentals=10**6),
        name="feed",
    )(at, *mixed, *w_out, x, gain, w_ffn, *cotangent)


def weights_kernel(second_ref, up_ref, low_ref, inner_ref, grad_ref):
    grad = product_tn(second_ref[...], low_ref[...])
    grad_ref[:, :512] = grad[:, :512].astype(bf16)
    grad_ref[:, 512:1152] = pltpu.roll(grad[:, 512:], 64, 1).astype(bf16)
    grad_ref[:, 1152:] = product_tn(up_ref[...], inner_ref[...]).astype(bf16)


def weights_back(second, upstream, low, inner):
    count, width = second.shape
    whole = lambda a: pl.BlockSpec(a.shape, lambda b: (0,) * a.ndim)
    columns = pl.BlockSpec((count, 256), lambda b: (0, b))
    return pl.pallas_call(
        weights_kernel,
        grid=(width // 256,),
        in_specs=[columns, columns, whole(low), whole(inner)],
        out_specs=pl.BlockSpec((256, 1728), lambda b: (b, 0)),
        out_shape=jax.ShapeDtypeStruct((width, 1728), bf16),
        compiler_params=pltpu.CompilerParams(vmem_limit_bytes=VMEM),
        cost_estimate=pl.CostEstimate(flops=4 * 10**9, bytes_accessed=10**7, transcendentals=0),
        name="weights_back",
    )(second, upstream, low, inner)


def back_kernel(*refs):
    state_refs = refs[:8]
    normed_ref, w_ref, raw_ref, q_ref, kk_ref, vv_ref, stat_ref, mixed_ref = refs[8:16]
    qk_gain_ref, cos_ref, sin_ref, bias_ref, gain_ref, ffn_ref = refs[16:22]
    own_ref, other_ref, grad_ref = refs[22:25]
    state, low_ref, total, norm_ref, qk_grad_ref = refs[25:]
    step = pl.program_id(0)
    for i, ref in enumerate(state_refs):
        state[i * 64 : i * 64 + 64, :] = ref[0]
    grad_mixed = product(state[...], w_ref[:, 256:]).astype(bf16)
    keys, values = kk_ref[...], vv_ref[...]
    grad_key = jnp.zeros((512, 128), f32)
    grad_value = jnp.zeros((512, 128), f32)
    grad_query = []
    for rows in (slice(0, 256), slice(256, 512)):
        queries, grads = q_ref[rows, :], grad_mixed[rows, :]
        low = halves(queries)
        bias = bias_ref[0, rows, :].astype(f32)
        parts = []
        for head in range(2):
            keep = low == (head == 0)
            one = jnp.where(keep, queries, jnp.zeros_like(queries))
            grad_one = jnp.where(keep, grads, jnp.zeros_like(grads))
            scores = product_nt(one, keys) * 0.125 + bias
            soft = jnp.exp(scores - stat_ref[rows, head * 64 : head * 64 + 1])
            grad_weights = product_nt(grad_one, values)
            center = jnp.sum(soft * grad_weights, axis=-1, keepdims=True)
            grad_scores = (soft * (grad_weights - center)).astype(bf16)
            parts.append(product(grad_scores, keys))
            grad_key = grad_key + product_tn(grad_scores, one)
            grad_value = grad_value + product_tn(soft.astype(bf16), grad_one)
        grad_query.append(jnp.where(halves(parts[0]), parts[0], parts[1]))
    cosine, sine = cos_ref[0], sin_ref[0]

    def prepare_back(grad, raw, gain):
        grad = grad * cosine + turn_back(grad * sine)
        scale = lax.rsqrt(head_mean(raw * raw) + eps)
        unit = raw * scale
        grad_gain = jnp.sum(grad * unit, axis=0, keepdims=True)
        scaled = grad * gain
        return scale * (scaled - unit * head_mean(scaled * unit)), grad_gain

    raw = raw_ref[...]
    grad_q = jnp.concatenate(grad_query, axis=0) * 0.125
    grad_q, gain_q = prepare_back(grad_q, raw[:, :128], qk_gain_ref[0:1, :])
    grad_key = (grad_key + pltpu.roll(grad_key, 64, 1)) * 0.125
    grad_value = grad_value + pltpu.roll(grad_value, 64, 1)
    low = halves(grad_value)
    raw_k = jnp.where(low, raw[:, 128:], 0.0)
    grad_k, gain_k = prepare_back(jnp.where(low, grad_key, 0.0), raw_k, qk_gain_ref[1:2, :])
    low_ref[:, :128] = grad_q.astype(bf16)
    low_ref[:, 128:] = jnp.where(low, grad_k, grad_value).astype(bf16)

    @pl.when(step == 0)
    def _():
        total[...] = jnp.zeros_like(total)
        norm_ref[...] = jnp.zeros_like(norm_ref)
        qk_grad_ref[...] = jnp.zeros_like(qk_grad_ref)

    qk_grad_ref[0:1, :] += gain_q
    qk_grad_ref[1:2, :] += gain_k
    for rows, ref in ((slice(0, 256), own_ref), (slice(256, 512), other_ref)):
        grad = product_nt(low_ref[rows, :], w_ref[:, :256])
        ref[0] = grad.astype(bf16)
        norm_ref[0:1, :] += jnp.sum(grad * normed_ref[rows, :].astype(f32), axis=0, keepdims=True)
    total[:, :256] += product_tn(normed_ref[...], low_ref[...])
    total[:, 256:] += product_tn(state[...], mixed_ref[...])

    @pl.when(step == pl.num_programs(0) - 1)
    def _():
        norm = norm_ref[0:1, :] / gain_ref[0:1, :]
        chunks = [norm[:, i : i + 128] for i in range(0, 1024, 128)]
        chunks += [ffn_ref[0:1, i : i + 128] for i in range(0, 1024, 128)]
        chunks += [qk_grad_ref[0:1, :], qk_grad_ref[1:2, :]]
        lines = [jnp.concatenate(chunks[i : i + 3], axis=1) for i in range(0, 18, 3)]
        lines = jnp.concatenate(lines + [jnp.zeros((10, 384), f32)], axis=0).astype(bf16)
        for i in range(16):
            grad_ref[i, :64, :] = total[i * 64 : i * 64 + 64, :].astype(bf16)
            grad_ref[i, 64:, :] = lines


def back(
    state, normed, w_att, raw, query, keys, values, stat, mixed, qk_gain, cosine, sine, bias, gain, ffn
):
    width = state[0].shape[2]
    micro = state[0].shape[0]
    whole = lambda a: pl.BlockSpec(a.shape, lambda m: (0,) * a.ndim)
    part = lambda a: pl.BlockSpec((1,) + a.shape[1:], lambda m: (m, 0, 0))
    rows = lambda a: pl.BlockSpec((512, a.shape[1]), lambda m: (m, 0))
    half = pl.BlockSpec((1, 256, width), lambda m: (m, 0, 0))
    out = jax.ShapeDtypeStruct
    return pl.pallas_call(
        back_kernel,
        grid=(micro,),
        in_specs=[part(p) for p in state]
        + [rows(normed), whole(w_att), rows(raw), rows(query), rows(keys), rows(values)]
        + [rows(stat), rows(mixed), whole(qk_gain), part(cosine), part(sine), part(bias)]
        + [whole(gain), whole(ffn)],
        out_specs=[half, half, pl.BlockSpec((16, 80, 384), lambda m: (0, 0, 0))],
        scratch_shapes=[
            pltpu.VMEM((512, width), bf16),
            pltpu.VMEM((512, 256), bf16),
            pltpu.VMEM((width, 384), f32),
            pltpu.VMEM((8, width), f32),
            pltpu.VMEM((8, 128), f32),
        ],
        out_shape=[
            out((micro, 256, width), bf16),
            out((micro, 256, width), bf16),
            out((16, 80, 384), bf16),
        ],
        compiler_params=pltpu.CompilerParams(vmem_limit_bytes=VMEM),
        cost_estimate=pl.CostEstimate(flops=4 * 10**9, bytes_accessed=10**7, transcendentals=10**6),
        name="back",
    )(
        *(*state, normed, w_att, raw, query, keys, values, stat, mixed),
        *(qk_gain, cosine, sine, bias, gain, ffn),
    )


def split_kernel(own_ref, got_ref, *refs):
    for k, ref in enumerate(refs):
        rows = slice(k * 64, k * 64 + 64)
        value = own_ref[:, rows].astype(f32) + got_ref[:, rows].astype(f32)
        ref[...] = value.astype(ref.dtype)


def split(own, other, first):
    micro, _, width = own.shape
    out = lambda kind: jax.ShapeDtypeStruct((micro, 64, width), kind)
    return pl.pallas_call(
        split_kernel,
        out_shape=[out(first), out(bf16), out(bf16), out(bf16)],
        compiler_params=pltpu.CompilerParams(vmem_limit_bytes=VMEM),
        name="split",
    )(own, other_core(other))


def local(
    tokens,
    segment_ids,
    cotangent,
    w_query,
    w_key,
    w_value,
    w_out,
    w_gate,
    w_up,
    w_down,
    norm_gain,
    ffn_gain,
    query_gain,
    key_gain,
):
    micro, own, width = tokens.shape
    head_size = query_gain.shape[0]
    nq = w_query.shape[1]
    nk = w_key.shape[1]
    group = segment_ids.shape[1]
    hidden = w_gate.shape[1]
    z = lax.axis_index("z")
    core = lax.axis_index("core")
    at = jnp.stack([lax.axis_index("y"), lax.axis_index("xh") * 2 + lax.axis_index("xl"), z, core])
    at = at.astype(jnp.int32)

    w_ffn = swap(jnp.concatenate([w_gate, w_up, w_down.T], axis=1))
    w_att = jnp.concatenate([w_query, w_key, w_value, w_out.T], axis=1)
    w_att = jnp.concatenate([swap_from_x(w_att, k) for k in range(4)], axis=0)
    x_chain, x_other = gather_chains(from_chain(swap(tokens)))
    segment = swap(segment_ids)
    cotangent_own = swap(cotangent)
    w_att = [w_att] + [from_y(w_att, k) for k in (1, 2, 3)]
    w_ffn, *w_att = tie(w_ffn, *w_att)
    w_ffn = lax.all_gather(w_ffn, plane, axis=0, tiled=True)
    w_out_own = jnp.concatenate([w[:, nq + 2 * nk :] for w in w_att], axis=0)
    x_other, cotangent_own, w_out_own = tie(x_other, cotangent_own, w_out_own)
    cotangent_chain = from_chain(cotangent_own)
    w_out_chain = from_chain(w_out_own)

    index = jnp.arange(group, dtype=jnp.int32)
    change = jnp.concatenate(
        [jnp.ones((micro, 1), dtype=bool), segment[:, 1:] != segment[:, :-1]], axis=1
    )
    start = lax.cummax(jnp.where(change, index, 0), axis=1)
    start = ordered(start, z, core, 1)
    index = ordered(index[None], z, core, 1)
    place = (index - start).astype(f32)
    freq = rope_base ** (-(jnp.arange(head_size // 2, dtype=f32) * 2.0 / head_size))
    angle = place[:, :, None] * jnp.tile(freq, 4)
    cosine, sine = jnp.cos(angle), jnp.sin(angle)
    allowed = (start[:, :, None] == start[:, None, :]) & (index[:, :, None] >= index[:, None, :])
    bias = jnp.where(allowed, 0.0, -1e30).astype(bf16)
    qk_gain = jnp.stack([jnp.tile(query_gain, 2), jnp.tile(key_gain, 2)])
    qk_gain = jnp.concatenate([qk_gain, jnp.zeros((6, 128), f32)])
    gain_rows = lambda gain: jnp.broadcast_to(gain, (8, width))

    mixed, x, normed, w_abs, raw, query, keys, values, stat = attend(
        at, (x_chain, x_other), w_att, gain_rows(norm_gain), qk_gain, cosine, sine, bias
    )
    mixed, *chains = tie(mixed, *cotangent_chain, *w_out_chain)
    mixed_pieces = gather(mixed)
    w_out_all = gather_chains(chains[4:])
    cotangent_all = gather_chains(chains[:4])
    state, second, inner, gu_low, grad_own, grad_other, upstream, down_own, down_other = feed(
        at, mixed_pieces, w_out_all, x, cotangent_all, gain_rows(ffn_gain), w_ffn
    )
    parts = split(grad_own, grad_other, f32)
    got = [from_z(parts[k], -k) for k in (1, 2, 3)]
    grad_ffn = weights_back(second, upstream, gu_low, inner)
    grad_second = parts[0]
    for part in got:
        grad_second = grad_second + part.astype(f32)
    grad_ffn = lax.psum_scatter(grad_ffn, plane, scatter_dimension=0, tiled=True)
    state_own = state.reshape(micro, 2, own, width)[:, 0]
    _, norm_pull = jax.vjp(rms_rows, state_own, ffn_gain)
    grad_state_norm, grad_ffn_gain = norm_pull(grad_second)
    grad_state = (cotangent_own.astype(f32) + grad_state_norm).astype(bf16)
    state_pieces = gather(grad_state)

    down_own, state_pieces[1] = tie(down_own, state_pieces[1])
    down = split(down_own, down_other, f32)
    down = [(down[0] + state_own).astype(bf16)] + list(down[1:])
    state_pieces[-1], down[1] = tie(state_pieces[-1], down[1])
    output = sum(swap_from_z(down[k], -k).astype(f32) for k in range(4)).astype(bf16)

    grad_own, grad_other, grad_att = back(
        *(state_pieces, normed, w_abs, raw, query, keys, values, stat, mixed, qk_gain),
        *(cosine, sine, bias, gain_rows(norm_gain), gain_rows(grad_ffn_gain)),
    )
    parts = split(grad_own, grad_other, bf16)
    got = [swap_from_z(parts[k], -k).astype(f32) for k in range(4)]
    grad_att, got[0] = tie(grad_att, got[0])
    grad_normed = sum(got)
    grad_att = lax.all_to_all(grad_att, plane, 0, 0)
    grad_att = jnp.sum(grad_att.astype(f32), axis=0)
    gains = group_sum(grad_att[64:70].reshape(-1))
    grad_att = swap(grad_att[:64])
    _, first_pull = jax.vjp(rms_rows, tokens.astype(f32), norm_gain)
    grad_resid_norm, _ = first_pull(grad_normed)
    input_grad = (swap(grad_state).astype(f32) + grad_resid_norm).astype(bf16)
    grad_ffn = swap(grad_ffn).astype(f32)
    both = nq + nk
    q_gains = gains[2 * width :]
    return (
        output,
        input_grad,
        grad_att[:, :nq],
        grad_att[:, nq:both],
        grad_att[:, both : both + nk],
        grad_att[:, both + nk :].T,
        grad_ffn[:, :hidden],
        grad_ffn[:, hidden : 2 * hidden],
        grad_ffn[:, 2 * hidden :].T,
        gains[:width],
        gains[width : 2 * width],
        q_gains[:head_size] + q_gains[head_size : 2 * head_size],
        q_gains[2 * head_size : 3 * head_size],
    )


def solution(mesh):
    inner = Mesh(mesh.devices.reshape(4, 2, 2, 4, 2), axes)
    dp, mp = ("y", "xh", "core"), ("z", "xl")
    rows = P(None, dp + mp, None)
    weight_in = [P(dp, mp)] * 3 + [P(mp, dp)] + [P(dp, mp)] * 2 + [P(mp, dp)]
    return jax.shard_map(
        local,
        mesh=inner,
        in_specs=tuple([rows, P(None, dp), rows] + weight_in + [P()] * 4),
        out_specs=tuple([rows, rows] + weight_in + [P()] * 4),
        check_vma=False,
    )
```

profile of v0, /device:TPU:1, one launch (start us, length us, event | category | flops | bytes accessed | tf_op | source)
XLA Modules:
  0.0 289.6 jit_solution(16106779532579084609)
XLA Ops:
  8.1 4.5 %collective-permute-start.7 = (bf16[64,384]{1,0:T(8,128)(2,1)S(1)}, bf16[64,384]{1,0:T(8,128)(2,1)S(1)}, u32[]{:S(2)}, u32[]{:S(2)}) collective-permute-start(bf16[64,384]{1,0:T(8,128)(2,1)S(1)} %pad_maximum_fusion.4), channel_id=1, source_target_pairs={{0,0},{1,8},{8,1},{9,9},{16,16},{17,24},{24,17},{25,25},{2,2},{3,1... | collective-permute-start | bytes 147464 | tf_op jit(solution)/shard_map/ppermute | solution.py:69
  17.2 3.9 %collective-permute-start.6 = (bf16[64,1728]{1,0:T(8,128)(2,1)S(1)}, bf16[64,1728]{1,0:T(8,128)(2,1)S(1)}, u32[]{:S(2)}, u32[]{:S(2)}) collective-permute-start(bf16[64,1728]{1,0:T(8,128)(2,1)S(1)} %concatenate.30), channel_id=1, source_target_pairs={{0,0},{1,8},{8,1},{9,9},{2,2},{3,10},{10,3},{11,11},{4,4},{5,12},{... | collective-permute-start | bytes 663560 | tf_op jit(solution)/shard_map/ppermute | solution.py:43
  28.2 4.5 %collective-permute-done.12.refs_4_ = bf16[256,384]{1,0:T(8,128)(2,1)S(1)} collective-permute-done((bf16[256,384]{1,0:T(8,128)(2,1)S(1)}, bf16[256,384]{1,0:T(8,128)(2,1)S(1)}, u32[]{:S(2)}, u32[]{:S(2)}) %collective-permute-start.12) | collective-permute-done | bytes 196640 | tf_op jit(solution)/shard_map/ppermute | solution.py:73
  32.8 4.2 %collective-permute-start.14 = (s32[2,512]{1,0:T(2,128)}, s32[2,512]{1,0:T(2,128)S(1)}, u32[]{:S(2)}, u32[]{:S(2)}) collective-permute-start(s32[2,512]{1,0:T(2,128)} %param.15), channel_id=1, source_target_pairs={{0,0},{1,8},{8,1},{9,9},{2,2},{3,10},{10,3},{11,11},{4,4},{5,12},{... | collective-permute-start | bytes 12296 | tf_op jit(solution)/shard_map/ppermute | solution.py:43
  38.9 3.6 %collective-permute-start = (bf16[2,64,1024]{2,1,0:T(8,128)(2,1)}, bf16[2,64,1024]{2,1,0:T(8,128)(2,1)S(1)}, u32[]{:S(2)}, u32[]{:S(2)}) collective-permute-start(bf16[2,64,1024]{2,1,0:T(8,128)(2,1)} %param.14), channel_id=1, source_target_pairs={{0,0},{1,8},{8,1},{9,9},{2,2},{3,10},{10,3},{11,11},{4,4},{5,12},{... | collective-permute-start | bytes 786440 | tf_op jit(solution)/shard_map/ppermute | solution.py:43
  50.8 3.4 %collective-permute-start.2 = (bf16[2,64,1024]{2,1,0:T(8,128)(2,1)S(1)}, bf16[2,64,1024]{2,1,0:T(8,128)(2,1)S(1)}, u32[]{:S(2)}, u32[]{:S(2)}) collective-permute-start(bf16[2,64,1024]{2,1,0:T(8,128)(2,1)S(1)} %collective-permute-done), channel_id=1, source_target_pairs={{0,4},{2,6},{4,0},{6,2},{1,5},{3,7},{5,1},{7,3},{8,12},{10,14},{12... | collective-permute-start | bytes 786440 | tf_op jit(solution)/shard_map/ppermute | solution.py:49
  56.8 4.0 %collective-permute-done.2 = bf16[2,64,1024]{2,1,0:T(8,128)(2,1)S(1)} collective-permute-done((bf16[2,64,1024]{2,1,0:T(8,128)(2,1)S(1)}, bf16[2,64,1024]{2,1,0:T(8,128)(2,1)S(1)}, u32[]{:S(2)}, u32[]{:S(2)}) %collective-permute-start.2) | collective-permute-done | bytes 262176 | tf_op jit(solution)/shard_map/ppermute | solution.py:49
  77.5 10.9 %attend.1 = (bf16[1024,128]{1,0:T(8,128)(2,1)}, bf16[1024,1024]{1,0:T(8,128)(2,1)}, bf16[1024,1024]{1,0:T(8,128)(2,1)}, bf16[1024,384]{1,0:T(8,128)(2,1)}, f32[1...) custom-call(s32[4]{0:T(128)} %pad_add_fusion.at_ref, ...), custom_call_target="tpu_custom_call" | custom-call | flops 2000000000 | bytes 10000000 | tf_op jit(solution)/shard_map/attend/pallas_call | solution.py:196
  104.7 5.9 %collective-permute-done.22.refs_2_ = bf16[1024,128]{1,0:T(8,128)(2,1)S(1)} collective-permute-done((bf16[1024,128]{1,0:T(8,128)(2,1)S(1)}, bf16[1024,128]{1,0:T(8,128)(2,1)S(1)}, u32[]{:S(2)}, u32[]{:S(2)}) %collective-permute-start.22) | collective-permute-done | bytes 262176 | tf_op jit(solution)/shard_map/ppermute | solution.py:49
  115.8 21.3 %feed.1 = (f32[256,1024]{1,0:T(8,128)}, bf16[1024,1024]{1,0:T(8,128)(2,1)}, bf16[1024,576]{1,0:T(8,128)(2,1)}, bf16[1024,1152]{1,0:T(8,128)(2,1)}, bf16[2,256,10...) custom-call(s32[4]{0:T(128)} %pad_add_fusion.at_ref, ...), custom_call_target="tpu_custom_call" | custom-call | flops 8999999488 | bytes 10000000 | tf_op jit(solution)/shard_map/feed/pallas_call | solution.py:318
  137.1 8.8 %weights_back.1 = bf16[1024,1728]{1,0:T(8,128)(2,1)} custom-call(bf16[1024,1024]{1,0:T(8,128)(2,1)} %get-tuple-element.121.second_ref, bf16[1024,1024]{1,0:T(8,128)(2,1)} %get-tuple-element.122.up_ref, bf16[1024,1152]{1,0:T(8,128)(2,1)} %get-tuple-element.123.low_ref, bf16[1024,576]{1,0:T(8,128)(2,1)} %get-tuple-element.124.inner_ref), custom_call_target="tpu_custom_call" | custom-call | flops 4000000000 | bytes 10000000 | tf_op jit(solution)/shard_map/weights_back/pallas_call | solution.py:363
  157.3 4.4 %collective-permute-done.31 = bf16[2,64,1024]{2,1,0:T(8,128)(2,1)S(1)} collective-permute-done((bf16[2,64,1024]{2,1,0:T(8,128)(2,1)}, bf16[2,64,1024]{2,1,0:T(8,128)(2,1)S(1)}, u32[]{:S(2)}, u32[]{:S(2)}) %collective-permute-start.31) | collective-permute-done | bytes 262176 | tf_op jit(solution)/shard_map/ppermute | solution.py:49
  161.7 5.4 %collective-permute-done.32 = bf16[2,64,1024]{2,1,0:T(8,128)(2,1)S(1)} collective-permute-done((bf16[2,64,1024]{2,1,0:T(8,128)(2,1)}, bf16[2,64,1024]{2,1,0:T(8,128)(2,1)S(1)}, u32[]{:S(2)}, u32[]{:S(2)}) %collective-permute-start.32) | collective-permute-done | bytes 262176 | tf_op jit(solution)/shard_map/ppermute | solution.py:49
  173.7 4.3 %collective-permute-done.37.refs_3_ = bf16[2,64,1024]{2,1,0:T(8,128)(2,1)S(1)} collective-permute-done((bf16[2,64,1024]{2,1,0:T(8,128)(2,1)S(1)}, bf16[2,64,1024]{2,1,0:T(8,128)(2,1)S(1)}, u32[]{:S(2)}, u32[]{:S(2)}) %collective-permute-start.37) | collective-permute-done | bytes 262176 | tf_op jit(solution)/shard_map/ppermute | solution.py:49
  179.8 5.4 %collective-permute-done.43.refs_2_ = bf16[2,64,1024]{2,1,0:T(8,128)(2,1)S(1)} collective-permute-done((bf16[2,64,1024]{2,1,0:T(8,128)(2,1)S(1)}, bf16[2,64,1024]{2,1,0:T(8,128)(2,1)S(1)}, u32[]{:S(2)}, u32[]{:S(2)}) %collective-permute-start.43) | collective-permute-done | bytes 262176 | tf_op jit(solution)/shard_map/ppermute | solution.py:49
  191.0 14.7 %back.1 = (bf16[2,256,1024]{2,1,0:T(8,128)(2,1)}, bf16[2,256,1024]{2,1,0:T(8,128)(2,1)}, bf16[16,80,384]{2,1,0:T(8,128)(2,1)}) custom-call(bf16[2,64,1024]{2,1,0:T(8,128)(2,1)} %copy-done.9, bf16[2,64,1024]{2,1,0:T(8,128)(2,1)} %collective-permute-done.34.refs_1_, bf16[2,64,1024]{2,1,0:T(8,128)(2,1)} %copy-done.22, bf16[2,64,1024]{2,1,0:T(8,128)(2,1)} %copy-done.21, ...), custom_call_target="tpu_custom_call" | custom-call | flops 4000000000 | bytes 10000000 | tf_op jit(solution)/shard_map/back/pallas_call | solution.py:466
  212.4 3.8 %collective-permute-start.48 = (bf16[2,64,1024]{2,1,0:T(8,128)(2,1)}, bf16[2,64,1024]{2,1,0:T(8,128)(2,1)S(1)}, u32[]{:S(2)}, u32[]{:S(2)}) collective-permute-start(bf16[2,64,1024]{2,1,0:T(8,128)(2,1)} %get-tuple-element.115), channel_id=1, source_target_pairs={{0,0},{1,8},{2,2},{3,10},{4,4},{5,12},{6,6},{7,14},{8,1},{9,9},{10... | collective-permute-start | bytes 786440 | tf_op jit(solution)/shard_map/ppermute | solution.py:59
  216.2 5.5 %collective-permute-done.48 = bf16[2,64,1024]{2,1,0:T(8,128)(2,1)S(1)} collective-permute-done((bf16[2,64,1024]{2,1,0:T(8,128)(2,1)}, bf16[2,64,1024]{2,1,0:T(8,128)(2,1)S(1)}, u32[]{:S(2)}, u32[]{:S(2)}) %collective-permute-start.48) | collective-permute-done | bytes 262176 | tf_op jit(solution)/shard_map/ppermute | solution.py:59
  221.8 5.3 %all-to-all-start = ((bf16[16,80,384]{2,1,0:T(8,128)(2,1)}), bf16[16,80,384]{2,1,0:T(8,128)(2,1)S(1)}, u32[]{:S(2)}, u32[]{:S(2)}) async-start(bf16[16,80,384]{2,1,0:T(8,128)(2,1)} %get-tuple-element.120), calls=%async_computation | async-start | bytes 1966080 | tf_op jit(solution)/shard_map/all_to_all | solution.py:608
  227.2 4.2 %collective-permute-start.36 = (bf16[2,64,1024]{2,1,0:T(8,128)(2,1)S(1)}, bf16[2,64,1024]{2,1,0:T(8,128)(2,1)S(1)}, u32[]{:S(2)}, u32[]{:S(2)}) collective-permute-start(bf16[2,64,1024]{2,1,0:T(8,128)(2,1)S(1)} %add_convert_fusion.1), channel_id=1, source_target_pairs={{0,0},{1,8},{2,2},{3,10},{4,4},{5,12},{6,6},{7,14},{8,1},{9,9},{10... | collective-permute-start | bytes 786440 | tf_op jit(solution)/shard_map/ppermute | solution.py:59
  237.8 5.5 %collective-permute-done.36 = bf16[2,64,1024]{2,1,0:T(8,128)(2,1)S(1)} collective-permute-done((bf16[2,64,1024]{2,1,0:T(8,128)(2,1)S(1)}, bf16[2,64,1024]{2,1,0:T(8,128)(2,1)S(1)}, u32[]{:S(2)}, u32[]{:S(2)}) %collective-permute-start.36) | collective-permute-done | bytes 262176 | tf_op jit(solution)/shard_map/ppermute | solution.py:59
  256.2 3.7 %collective-permute-done.50 = bf16[2,64,1024]{2,1,0:T(8,128)(2,1)S(1)} collective-permute-done((bf16[2,64,1024]{2,1,0:T(8,128)(2,1)}, bf16[2,64,1024]{2,1,0:T(8,128)(2,1)S(1)}, u32[]{:S(2)}, u32[]{:S(2)}) %collective-permute-start.50) | collective-permute-done | bytes 262176 | tf_op jit(solution)/shard_map/ppermute | solution.py:59
  267.8 3.6 %collective-permute-start.52 = (f32[64,384]{1,0:T(8,128)S(1)}, f32[64,384]{1,0:T(8,128)S(1)}, u32[]{:S(2)}, u32[]{:S(2)}) collective-permute-start(f32[64,384]{1,0:T(8,128)S(1)} %slice.100), channel_id=1, source_target_pairs={{0,0},{1,8},{8,1},{9,9},{2,2},{3,10},{10,3},{11,11},{4,4},{5,12},{... | collective-permute-start | bytes 294920 | tf_op jit(solution)/shard_map/ppermute | solution.py:43
  274.3 3.6 %collective-permute-start.53 = (bf16[64,1728]{1,0:T(8,128)(2,1)}, bf16[64,1728]{1,0:T(8,128)(2,1)S(1)}, u32[]{:S(2)}, u32[]{:S(2)}) collective-permute-start(bf16[64,1728]{1,0:T(8,128)(2,1)} %reduce-scatter.2.cloned.1.call-done), channel_id=1, source_target_pairs={{0,0},{1,8},{8,1},{9,9},{2,2},{3,10},{10,3},{11,11},{4,4},{5,12},{... | collective-permute-start | bytes 663560 | tf_op jit(solution)/shard_map/ppermute | solution.py:43
  (238 shorter events, 130.1 us)
Async XLA Ops:
  7.2 107.5 %all-gather.2.cloned.1.call-start = ((), (), s32[]{:S(2)}) async-start(), calls=%async_computation.2 | async-start | bytes 3899392 | tf_op jit(solution)/shard_map/all_gather | solution.py:548
  8.1 13.0 %collective-permute-start.7 = (bf16[64,384]{1,0:T(8,128)(2,1)S(1)}, bf16[64,384]{1,0:T(8,128)(2,1)S(1)}, u32[]{:S(2)}, u32[]{:S(2)}) collective-permute-start(bf16[64,384]{1,0:T(8,128)(2,1)S(1)} %pad_maximum_fusion.4), channel_id=1, source_target_pairs={{0,0},{1,8},{8,1},{9,9},{16,16},{17,24},{24,17},{25,25},{2,2},{3,1... | collective-permute-start | bytes 147464 | tf_op jit(solution)/shard_map/ppermute | solution.py:69
  32.7 241.6 %reduce-scatter.2.cloned.1.call-start = ((), (), s32[]{:S(2)}) async-start(), calls=%async_computation.3 | async-start | bytes 3899392 | tf_op jit(solution)/shard_map/reduce_scatter | solution.py:587
  32.8 29.1 %collective-permute-start.14 = (s32[2,512]{1,0:T(2,128)}, s32[2,512]{1,0:T(2,128)S(1)}, u32[]{:S(2)}, u32[]{:S(2)}) collective-permute-start(s32[2,512]{1,0:T(2,128)} %param.15), channel_id=1, source_target_pairs={{0,0},{1,8},{8,1},{9,9},{2,2},{3,10},{10,3},{11,11},{4,4},{5,12},{... | collective-permute-start | bytes 12296 | tf_op jit(solution)/shard_map/ppermute | solution.py:43
  37.0 27.4 %collective-permute-start.5 = (bf16[2,64,1024]{2,1,0:T(8,128)(2,1)}, bf16[2,64,1024]{2,1,0:T(8,128)(2,1)S(1)}, u32[]{:S(2)}, u32[]{:S(2)}) collective-permute-start(bf16[2,64,1024]{2,1,0:T(8,128)(2,1)} %param.16), channel_id=1, source_target_pairs={{0,0},{1,8},{8,1},{9,9},{2,2},{3,10},{10,3},{11,11},{4,4},{5,12},{... | collective-permute-start | bytes 786440 | tf_op jit(solution)/shard_map/ppermute | solution.py:43
  66.8 21.7 %collective-permute-start.19 = (bf16[1024,128]{1,0:T(8,128)(2,1)S(1)}, bf16[1024,128]{1,0:T(8,128)(2,1)S(1)}, u32[]{:S(2)}, u32[]{:S(2)}) collective-permute-start(bf16[1024,128]{1,0:T(8,128)(2,1)S(1)} %pad_maximum_fusion.3), channel_id=1, source_target_pairs={{0,4},{2,6},{4,0},{6,2},{1,5},{3,7},{5,1},{7,3},{8,12},{10,14},{12... | collective-permute-start | bytes 786440 | tf_op jit(solution)/shard_map/ppermute | solution.py:49
  68.9 19.6 %collective-permute-start.18 = (bf16[1024,128]{1,0:T(8,128)(2,1)S(1)}, bf16[1024,128]{1,0:T(8,128)(2,1)S(1)}, u32[]{:S(2)}, u32[]{:S(2)}) collective-permute-start(bf16[1024,128]{1,0:T(8,128)(2,1)S(1)} %pad_maximum_fusion.3), channel_id=1, source_target_pairs={{0,6},{2,0},{4,2},{6,4},{1,7},{3,1},{5,3},{7,5},{8,14},{10,8},{12,... | collective-permute-start | bytes 786440 | tf_op jit(solution)/shard_map/ppermute | solution.py:49
  69.9 18.6 %collective-permute-start.17 = (bf16[2,64,1024]{2,1,0:T(8,128)(2,1)S(1)}, bf16[2,64,1024]{2,1,0:T(8,128)(2,1)S(1)}, u32[]{:S(2)}, u32[]{:S(2)}) collective-permute-start(bf16[2,64,1024]{2,1,0:T(8,128)(2,1)S(1)} %collective-permute-done.5), channel_id=1, source_target_pairs={{0,2},{2,4},{4,6},{6,0},{1,3},{3,5},{5,7},{7,1},{8,10},{10,12},{12... | collective-permute-start | bytes 786440 | tf_op jit(solution)/shard_map/ppermute | solution.py:49
  70.3 20.0 %collective-permute-start.16 = (bf16[2,64,1024]{2,1,0:T(8,128)(2,1)S(1)}, bf16[2,64,1024]{2,1,0:T(8,128)(2,1)S(1)}, u32[]{:S(2)}, u32[]{:S(2)}) collective-permute-start(bf16[2,64,1024]{2,1,0:T(8,128)(2,1)S(1)} %collective-permute-done.5), channel_id=1, source_target_pairs={{0,4},{2,6},{4,0},{6,2},{1,5},{3,7},{5,1},{7,3},{8,12},{10,14},{12... | collective-permute-start | bytes 786440 | tf_op jit(solution)/shard_map/ppermute | solution.py:49
  73.3 18.6 %collective-permute-start.15 = (bf16[2,64,1024]{2,1,0:T(8,128)(2,1)S(1)}, bf16[2,64,1024]{2,1,0:T(8,128)(2,1)S(1)}, u32[]{:S(2)}, u32[]{:S(2)}) collective-permute-start(bf16[2,64,1024]{2,1,0:T(8,128)(2,1)S(1)} %collective-permute-done.5), channel_id=1, source_target_pairs={{0,6},{2,0},{4,2},{6,4},{1,7},{3,1},{5,3},{7,5},{8,14},{10,8},{12,... | collective-permute-start | bytes 786440 | tf_op jit(solution)/shard_map/ppermute | solution.py:49
  92.0 21.0 %collective-permute-start.29 = (bf16[4,2,64,1024]{3,2,1,0:T(8,128)(2,1)S(1)}, bf16[4,2,64,1024]{3,2,1,0:T(8,128)(2,1)S(1)}, u32[]{:S(2)}, u32[]{:S(2)}) collective-permute-start(bf16[4,2,64,1024]{3,2,1,0:T(8,128)(2,1)S(1)} %pad_maximum_fusion.2.refs_13_), channel_id=1, source_target_pairs={{0,8},{8,0},{1,9},{9,1},{2,10},{10,2},{3,11},{11,3},{4,12},{12,4},... | collective-permute-start | bytes 3145736 | tf_op jit(solution)/shard_map/ppermute | solution.py:77
  93.9 20.8 %collective-permute-start.28 = (bf16[4,1024,128]{2,1,0:T(8,128)(2,1)S(1)}, bf16[4,1024,128]{2,1,0:T(8,128)(2,1)S(1)}, u32[]{:S(2)}, u32[]{:S(2)}) collective-permute-start(bf16[4,1024,128]{2,1,0:T(8,128)(2,1)S(1)} %pad_maximum_fusion.1.refs_8_), channel_id=1, source_target_pairs={{0,8},{8,0},{1,9},{9,1},{2,10},{10,2},{3,11},{11,3},{4,12},{12,4},... | collective-permute-start | bytes 3145736 | tf_op jit(solution)/shard_map/ppermute | solution.py:77
  95.8 14.8 %collective-permute-start.22 = (bf16[1024,128]{1,0:T(8,128)(2,1)S(1)}, bf16[1024,128]{1,0:T(8,128)(2,1)S(1)}, u32[]{:S(2)}, u32[]{:S(2)}) collective-permute-start(bf16[1024,128]{1,0:T(8,128)(2,1)S(1)} %copy-done.20), channel_id=1, source_target_pairs={{0,4},{2,6},{4,0},{6,2},{1,5},{3,7},{5,1},{7,3},{8,12},{10,14},{12... | collective-permute-start | bytes 786440 | tf_op jit(solution)/shard_map/ppermute | solution.py:49
  153.2 14.0 %collective-permute-start.32 = (bf16[2,64,1024]{2,1,0:T(8,128)(2,1)}, bf16[2,64,1024]{2,1,0:T(8,128)(2,1)S(1)}, u32[]{:S(2)}, u32[]{:S(2)}) collective-permute-start(bf16[2,64,1024]{2,1,0:T(8,128)(2,1)} %get-tuple-element.93), channel_id=1, source_target_pairs={{0,4},{2,6},{4,0},{6,2},{1,5},{3,7},{5,1},{7,3},{8,12},{10,14},{12... | collective-permute-start | bytes 786440 | tf_op jit(solution)/shard_map/ppermute | solution.py:49
  156.1 30.6 %collective-permute-start.35 = (bf16[2,256,1024]{2,1,0:T(8,128)(2,1)S(1)}, bf16[2,256,1024]{2,1,0:T(8,128)(2,1)S(1)}, u32[]{:S(2)}, u32[]{:S(2)}) collective-permute-start(bf16[2,256,1024]{2,1,0:T(8,128)(2,1)S(1)} %copy-done.17), channel_id=1, source_target_pairs={{0,8},{8,0},{1,9},{9,1},{2,10},{10,2},{3,11},{11,3},{4,12},{12,4},... | collective-permute-start | bytes 3145736 | tf_op jit(solution)/shard_map/ppermute | solution.py:77
  170.8 14.4 %collective-permute-start.43 = (bf16[2,64,1024]{2,1,0:T(8,128)(2,1)S(1)}, bf16[2,64,1024]{2,1,0:T(8,128)(2,1)S(1)}, u32[]{:S(2)}, u32[]{:S(2)}) collective-permute-start(bf16[2,64,1024]{2,1,0:T(8,128)(2,1)S(1)} %fusion.1.refs_0_), channel_id=1, source_target_pairs={{0,4},{2,6},{4,0},{6,2},{1,5},{3,7},{5,1},{7,3},{8,12},{10,14},{12... | collective-permute-start | bytes 786440 | tf_op jit(solution)/shard_map/ppermute | solution.py:49
  221.8 38.9 %all-to-all-start = ((bf16[16,80,384]{2,1,0:T(8,128)(2,1)}), bf16[16,80,384]{2,1,0:T(8,128)(2,1)S(1)}, u32[]{:S(2)}, u32[]{:S(2)}) async-start(bf16[16,80,384]{2,1,0:T(8,128)(2,1)} %get-tuple-element.120), calls=%async_computation | async-start | bytes 1966080 | tf_op jit(solution)/shard_map/all_to_all | solution.py:608
  227.2 16.1 %collective-permute-start.36 = (bf16[2,64,1024]{2,1,0:T(8,128)(2,1)S(1)}, bf16[2,64,1024]{2,1,0:T(8,128)(2,1)S(1)}, u32[]{:S(2)}, u32[]{:S(2)}) collective-permute-start(bf16[2,64,1024]{2,1,0:T(8,128)(2,1)S(1)} %add_convert_fusion.1), channel_id=1, source_target_pairs={{0,0},{1,8},{2,2},{3,10},{4,4},{5,12},{6,6},{7,14},{8,1},{9,9},{10... | collective-permute-start | bytes 786440 | tf_op jit(solution)/shard_map/ppermute | solution.py:59
  231.4 16.4 %collective-permute-start.40 = (bf16[2,64,1024]{2,1,0:T(8,128)(2,1)}, bf16[2,64,1024]{2,1,0:T(8,128)(2,1)S(1)}, u32[]{:S(2)}, u32[]{:S(2)}) collective-permute-start(bf16[2,64,1024]{2,1,0:T(8,128)(2,1)} %get-tuple-element.101), channel_id=1, source_target_pairs={{0,4},{1,12},{2,6},{3,14},{4,0},{5,8},{6,2},{7,10},{8,5},{9,13},{1... | collective-permute-start | bytes 786440 | tf_op jit(solution)/shard_map/ppermute | solution.py:59
  233.0 16.6 %collective-permute-start.41 = (bf16[2,64,1024]{2,1,0:T(8,128)(2,1)}, bf16[2,64,1024]{2,1,0:T(8,128)(2,1)S(1)}, u32[]{:S(2)}, u32[]{:S(2)}) collective-permute-start(bf16[2,64,1024]{2,1,0:T(8,128)(2,1)} %get-tuple-element.102), channel_id=1, source_target_pairs={{0,6},{1,14},{2,0},{3,8},{4,2},{5,10},{6,4},{7,12},{8,7},{9,15},{1... | collective-permute-start | bytes 786440 | tf_op jit(solution)/shard_map/ppermute | solution.py:59
  235.8 17.6 %collective-permute-start.39 = (bf16[2,64,1024]{2,1,0:T(8,128)(2,1)}, bf16[2,64,1024]{2,1,0:T(8,128)(2,1)S(1)}, u32[]{:S(2)}, u32[]{:S(2)}) collective-permute-start(bf16[2,64,1024]{2,1,0:T(8,128)(2,1)} %get-tuple-element.100), channel_id=1, source_target_pairs={{0,2},{1,10},{2,4},{3,12},{4,6},{5,14},{6,0},{7,8},{8,3},{9,11},{1... | collective-permute-start | bytes 786440 | tf_op jit(solution)/shard_map/ppermute | solution.py:59
  235.8 20.4 %collective-permute-start.49 = (bf16[2,64,1024]{2,1,0:T(8,128)(2,1)}, bf16[2,64,1024]{2,1,0:T(8,128)(2,1)S(1)}, u32[]{:S(2)}, u32[]{:S(2)}) collective-permute-start(bf16[2,64,1024]{2,1,0:T(8,128)(2,1)} %get-tuple-element.117), channel_id=1, source_target_pairs={{0,2},{1,10},{2,4},{3,12},{4,6},{5,14},{6,0},{7,8},{8,3},{9,11},{1... | collective-permute-start | bytes 786440 | tf_op jit(solution)/shard_map/ppermute | solution.py:59
  243.3 16.5 %collective-permute-start.50 = (bf16[2,64,1024]{2,1,0:T(8,128)(2,1)}, bf16[2,64,1024]{2,1,0:T(8,128)(2,1)S(1)}, u32[]{:S(2)}, u32[]{:S(2)}) collective-permute-start(bf16[2,64,1024]{2,1,0:T(8,128)(2,1)} %get-tuple-element.118), channel_id=1, source_target_pairs={{0,4},{1,12},{2,6},{3,14},{4,0},{5,8},{6,2},{7,10},{8,5},{9,13},{1... | collective-permute-start | bytes 786440 | tf_op jit(solution)/shard_map/ppermute | solution.py:59
  249.6 17.2 %collective-permute-start.42 = (bf16[2,64,1024]{2,1,0:T(8,128)(2,1)}, bf16[2,64,1024]{2,1,0:T(8,128)(2,1)S(1)}, u32[]{:S(2)}, u32[]{:S(2)}) collective-permute-start(bf16[2,64,1024]{2,1,0:T(8,128)(2,1)} %copy-done.9), channel_id=1, source_target_pairs={{0,0},{1,8},{8,1},{9,9},{2,2},{3,10},{10,3},{11,11},{4,4},{5,12},{... | collective-permute-start | bytes 786440 | tf_op jit(solution)/shard_map/ppermute | solution.py:43
  (67 other events, 700.0 us)
Sparse Core Ops, SparseCore 0:
  32.9 51.1 all-gather.1
  146.1 74.4 reduce-scatter.1
where the time goes:
time: 290 us
  starting transfers between devices  103 us (36%)
  waiting for transfers between devices  81.2 us (28%)
  Pallas kernels  63.9 us (22%)
  between operations  14.7 us (5%)
  local copies, waits for them, and re-layouts  13.8 us (5%)
  other arithmetic  13.2 us (5%)
    ppermute x21, waiting for transfers between devices, from_z(): return lax.ppermute(value, 'z', [(z, (z - k) % 4) for z in range(4)])  40.1 us
    ppermute x21, starting transfers between devices, from_z(): return lax.ppermute(value, 'z', [(z, (z - k) % 4) for z in range(4)])  31.6 us
    ppermute x7, starting transfers between devices, swap(): lax.ppermute(value, ('core', 'xl'), [(a * 2 + b, b * 2 + a) for a in rang...  23.9 us
    pallas_call x1, Pallas kernels, feed(): pl.pallas_call(feed_kernel, grid_spec=pltpu.PrefetchScalarGridSpec(num_sc...  21.3 us
    ppermute x8, waiting for transfers between devices, swap_from_z(): return lax.ppermute(value, ('core', 'z', 'xl'), perm)  19.4 us
    ppermute x8, starting transfers between devices, swap_from_z(): return lax.ppermute(value, ('core', 'z', 'xl'), perm)  19.2 us
    pallas_call x1, Pallas kernels, back(): pl.pallas_call(back_kernel, grid=(micro,), in_specs=[part(p) for p in sta...  14.7 us
    pallas_call x1, Pallas kernels, attend(): pl.pallas_call(attend_kernel, grid_spec=pltpu.PrefetchScalarGridSpec(num_...  10.9 us
  transfers between devices with their start and end apart: 61, of which 29 were waited for; matrix products, arithmetic and copies ran while one was open for 7% of the time, Pallas kernels for 12%

commit v1 on v0

--- a/solution.py
+++ b/solution.py
@@ -49,16 +49,6 @@
     return lax.ppermute(value, "z", [(z, (z - k) % 4) for z in range(4)])
 
 
-def swap_from_z(value, k):
-    perm = [
-        (a * 8 + z * 2 + b, b * 8 + ((z - k) % 4) * 2 + a)
-        for a in range(2)
-        for z in range(4)
-        for b in range(2)
-    ]
-    return lax.ppermute(value, ("core", "z", "xl"), perm)
-
-
 def swap_from_x(value, k):
     perm = []
     for xh in range(2):
@@ -87,7 +77,7 @@
 
 
 def gather(value):
-    chain = [value] + [from_z(value, k) for k in (1, 2, 3)]
+    chain = tie(*from_chain(value))
     return chain + [other_core(v) for v in chain]
 
 
@@ -106,7 +96,7 @@
 
 
 def tie(*values):
-    return lax.optimization_barrier(values)
+    return list(lax.optimization_barrier(values))
 
 
 def halves(value):
@@ -225,7 +215,7 @@
             out(128, f32),
         ],
         compiler_params=pltpu.CompilerParams(vmem_limit_bytes=VMEM),
-        cost_estimate=pl.CostEstimate(flops=2 * 10**9, bytes_accessed=10**7, transcendentals=10**6),
+        cost_estimate=pl.CostEstimate(flops=12 * 10**9, bytes_accessed=10**7, transcendentals=10**6),
         name="attend",
     )(at, *pieces, *weights, gain, qk_gain, cosine, sine, bias)
 
@@ -484,7 +474,7 @@
             out((16, 80, 384), bf16),
         ],
         compiler_params=pltpu.CompilerParams(vmem_limit_bytes=VMEM),
-        cost_estimate=pl.CostEstimate(flops=4 * 10**9, bytes_accessed=10**7, transcendentals=10**6),
+        cost_estimate=pl.CostEstimate(flops=15 * 10**9, bytes_accessed=10**7, transcendentals=10**6),
         name="back",
     )(
         *(*state, normed, w_att, raw, query, keys, values, stat, mixed),
@@ -492,22 +482,27 @@
     )
 
 
-def split_kernel(own_ref, got_ref, *refs):
-    for k, ref in enumerate(refs):
-        rows = slice(k * 64, k * 64 + 64)
-        value = own_ref[:, rows].astype(f32) + got_ref[:, rows].astype(f32)
-        ref[...] = value.astype(ref.dtype)
-
-
-def split(own, other, first):
+def split_kernel(*refs):
+    count = len(refs) // 2 - 2
+    for i in range(count):
+        own_ref, got_ref = refs[2 * i], refs[2 * i + 1]
+        micro = own_ref.shape[0]
+        for k, ref in enumerate(refs[-4:]):
+            rows = slice(k * 64, k * 64 + 64)
+            value = own_ref[:, rows].astype(f32) + got_ref[:, rows].astype(f32)
+            ref[i * micro : (i + 1) * micro] = value.astype(ref.dtype)
+
+
+def split(own, other, *more):
     micro, _, width = own.shape
-    out = lambda kind: jax.ShapeDtypeStruct((micro, 64, width), kind)
+    values = (own, other_core(other)) + more
+    out = lambda kind: jax.ShapeDtypeStruct((len(values) // 2 * micro, 64, width), kind)
     return pl.pallas_call(
         split_kernel,
-        out_shape=[out(first), out(bf16), out(bf16), out(bf16)],
+        out_shape=[out(f32), out(bf16), out(bf16), out(bf16)],
         compiler_params=pltpu.CompilerParams(vmem_limit_bytes=VMEM),
         name="split",
-    )(own, other_core(other))
+    )(*values)
 
 
 def local(
@@ -537,19 +532,15 @@
     at = jnp.stack([lax.axis_index("y"), lax.axis_index("xh") * 2 + lax.axis_index("xl"), z, core])
     at = at.astype(jnp.int32)
 
-    w_ffn = swap(jnp.concatenate([w_gate, w_up, w_down.T], axis=1))
+    segment = swap(segment_ids)
+    tokens_own = swap(jnp.concatenate([tokens, cotangent]))
     w_att = jnp.concatenate([w_query, w_key, w_value, w_out.T], axis=1)
     w_att = jnp.concatenate([swap_from_x(w_att, k) for k in range(4)], axis=0)
-    x_chain, x_other = gather_chains(from_chain(swap(tokens)))
-    segment = swap(segment_ids)
-    cotangent_own = swap(cotangent)
+    w_ffn = jnp.concatenate([w_gate, w_up, w_down.T], axis=1)
+    w_att, tokens_own, segment, w_ffn = tie(w_att, tokens_own, segment, w_ffn)
+    token_pieces = from_chain(tokens_own)
     w_att = [w_att] + [from_y(w_att, k) for k in (1, 2, 3)]
-    w_ffn, *w_att = tie(w_ffn, *w_att)
-    w_ffn = lax.all_gather(w_ffn, plane, axis=0, tiled=True)
-    w_out_own = jnp.concatenate([w[:, nq + 2 * nk :] for w in w_att], axis=0)
-    x_other, cotangent_own, w_out_own = tie(x_other, cotangent_own, w_out_own)
-    cotangent_chain = from_chain(cotangent_own)
-    w_out_chain = from_chain(w_out_own)
+    w_ffn = swap(w_ffn)
 
     index = jnp.arange(group, dtype=jnp.int32)
     change = jnp.concatenate(
@@ -565,59 +556,58 @@
     allowed = (start[:, :, None] == start[:, None, :]) & (index[:, :, None] >= index[:, None, :])
     bias = jnp.where(allowed, 0.0, -1e30).astype(bf16)
     qk_gain = jnp.stack([jnp.tile(query_gain, 2), jnp.tile(key_gain, 2)])
-    qk_gain = jnp.concatenate([qk_gain, jnp.zeros((6, 128), f32)])
-    gain_rows = lambda gain: jnp.broadcast_to(gain, (8, width))
+
+    w_ffn, *w_att = tie(w_ffn, *w_att)
+    w_ffn = lax.all_gather(w_ffn, plane, axis=0, tiled=True)
+    w_out_chain = from_chain(jnp.concatenate([w[:, nq + 2 * nk :] for w in w_att], axis=0))
+    token_pieces = tie(*token_pieces)
+    x_chain, x_other = gather_chains([piece[:micro] for piece in token_pieces])
+    cotangent_all = gather_chains([piece[micro:] for piece in token_pieces])
 
     mixed, x, normed, w_abs, raw, query, keys, values, stat = attend(
-        at, (x_chain, x_other), w_att, gain_rows(norm_gain), qk_gain, cosine, sine, bias
-    )
-    mixed, *chains = tie(mixed, *cotangent_chain, *w_out_chain)
+        at, (x_chain, x_other), w_att, norm_gain.reshape(1, width), qk_gain, cosine, sine, bias
+    )
+    mixed, *w_out_chain = tie(mixed, *w_out_chain)
+    w_out_all = gather_chains(w_out_chain)
     mixed_pieces = gather(mixed)
-    w_out_all = gather_chains(chains[4:])
-    cotangent_all = gather_chains(chains[:4])
     state, second, inner, gu_low, grad_own, grad_other, upstream, down_own, down_other = feed(
-        at, mixed_pieces, w_out_all, x, cotangent_all, gain_rows(ffn_gain), w_ffn
-    )
-    parts = split(grad_own, grad_other, f32)
+        at, mixed_pieces, w_out_all, x, cotangent_all, ffn_gain.reshape(1, width), w_ffn
+    )
+    down_got = other_core(down_other)
+    parts = split(grad_own, grad_other)
     got = [from_z(parts[k], -k) for k in (1, 2, 3)]
     grad_ffn = weights_back(second, upstream, gu_low, inner)
-    grad_second = parts[0]
-    for part in got:
-        grad_second = grad_second + part.astype(f32)
-    grad_ffn = lax.psum_scatter(grad_ffn, plane, scatter_dimension=0, tiled=True)
+    got = tie(*got)
+    grad_second = parts[0] + sum(piece.astype(f32) for piece in got)
     state_own = state.reshape(micro, 2, own, width)[:, 0]
     _, norm_pull = jax.vjp(rms_rows, state_own, ffn_gain)
     grad_state_norm, grad_ffn_gain = norm_pull(grad_second)
-    grad_state = (cotangent_own.astype(f32) + grad_state_norm).astype(bf16)
-    state_pieces = gather(grad_state)
-
-    down_own, state_pieces[1] = tie(down_own, state_pieces[1])
-    down = split(down_own, down_other, f32)
-    down = [(down[0] + state_own).astype(bf16)] + list(down[1:])
-    state_pieces[-1], down[1] = tie(state_pieces[-1], down[1])
-    output = sum(swap_from_z(down[k], -k).astype(f32) for k in range(4)).astype(bf16)
+    grad_state = (tokens_own[micro:].astype(f32) + grad_state_norm).astype(bf16)
+    grad_ffn, *state_pieces = tie(grad_ffn, *from_chain(grad_state))
+    state_pieces += [other_core(piece) for piece in state_pieces]
+    grad_ffn = lax.psum_scatter(grad_ffn, plane, scatter_dimension=0, tiled=True)
 
     grad_own, grad_other, grad_att = back(
         *(state_pieces, normed, w_abs, raw, query, keys, values, stat, mixed, qk_gain),
-        *(cosine, sine, bias, gain_rows(norm_gain), gain_rows(grad_ffn_gain)),
-    )
-    parts = split(grad_own, grad_other, bf16)
-    got = [swap_from_z(parts[k], -k).astype(f32) for k in range(4)]
-    grad_att, got[0] = tie(grad_att, got[0])
-    grad_normed = sum(got)
+        *(cosine, sine, bias, norm_gain.reshape(1, width), grad_ffn_gain.reshape(1, width)),
+    )
     grad_att = lax.all_to_all(grad_att, plane, 0, 0)
+    parts = split(grad_own, grad_other, down_own, down_got)
+    grad_att, *got = tie(grad_att, *[from_z(parts[k], -k) for k in (1, 2, 3)])
+    total = parts[0] + sum(piece.astype(f32) for piece in got)
+    _, first_pull = jax.vjp(rms_rows, tokens_own[:micro].astype(f32), norm_gain)
+    grad_resid_norm, _ = first_pull(total[:micro])
+    input_grad = grad_state.astype(f32) + grad_resid_norm
+    results = swap(jnp.concatenate([state_own + total[micro:], input_grad]).astype(bf16))
     grad_att = jnp.sum(grad_att.astype(f32), axis=0)
     gains = group_sum(grad_att[64:70].reshape(-1))
     grad_att = swap(grad_att[:64])
-    _, first_pull = jax.vjp(rms_rows, tokens.astype(f32), norm_gain)
-    grad_resid_norm, _ = first_pull(grad_normed)
-    input_grad = (swap(grad_state).astype(f32) + grad_resid_norm).astype(bf16)
     grad_ffn = swap(grad_ffn).astype(f32)
     both = nq + nk
     q_gains = gains[2 * width :]
     return (
-        output,
-        input_grad,
+        results[:micro],
+        results[micro:],
         grad_att[:, :nq],
         grad_att[:, nq:both],
         grad_att[:, both : both + nk],

time: 290 us -> 278 us (0.959)
  starting transfers between devices: 103 us -> 72.6 us
  waiting for transfers between devices: 81.2 us -> 99.4 us
    ppermute x8 -> x0, waiting for transfers between devices: 19.4 us -> none  [swap_from_z(): return lax.ppermute(value, ('core', 'z', 'xl'), perm)]
    ppermute x8 -> x0, starting transfers between devices: 19.2 us -> none  [swap_from_z(): return lax.ppermute(value, ('core', 'z', 'xl'), perm)]
    ppermute x21, waiting for transfers between devices: 40.1 us -> 56.7 us  [from_z(): return lax.ppermute(value, 'z', [(z, (z - k) % 4) for z in range(4)])]
    reduce_scatter x1, waiting for transfers between devices: 0.01 us -> 12.6 us  [local(): lax.psum_scatter(grad_ffn, plane, scatter_dimension=0, tiled=True)]
    all_to_all x1, waiting for transfers between devices: 0.01 us -> 12.2 us  [local(): grad_att = lax.all_to_all(grad_att, plane, 0, 0)]
    ppermute x7 -> x6, starting transfers between devices: 23.9 us -> 18.7 us  [swap(): lax.ppermute(value, ('core', 'xl'), [(a * 2 + b, b * 2 + a) for a in rang...]
    ppermute x21, starting transfers between devices: 31.6 us -> 28.2 us  [from_z(): return lax.ppermute(value, 'z', [(z, (z - k) % 4) for z in range(4)])]
    pallas_call x3 -> x2, Pallas kernels: 8.04 us -> 6.53 us  [split(): pl.pallas_call(split_kernel, out_shape=[out(f32), out(bf16), out(bf16), o...]
  transfers between devices with their start and end apart: 61 -> 52, of which waited for: 29 -> 23; matrix products, arithmetic and copies ran while one was open for 7% -> 7% of each run, Pallas kernels for 12% -> 14%
where the time goes in v1:
time: 278 us
  waiting for transfers between devices  99.4 us (36%)
  starting transfers between devices  72.6 us (26%)
  Pallas kernels  62.3 us (22%)
  other arithmetic  15.8 us (6%)
  between operations  14.7 us (5%)
  local copies, waits for them, and re-layouts  12.6 us (5%)
    ppermute x21, waiting for transfers between devices, from_z(): return lax.ppermute(value, 'z', [(z, (z - k) % 4) for z in range(4)])  56.7 us
    ppermute x21, starting transfers between devices, from_z(): return lax.ppermute(value, 'z', [(z, (z - k) % 4) for z in range(4)])  28.2 us
    pallas_call x1, Pallas kernels, feed(): pl.pallas_call(feed_kernel, grid_spec=pltpu.PrefetchScalarGridSpec(num_sc...  21.3 us
    ppermute x6, starting transfers between devices, swap(): lax.ppermute(value, ('core', 'xl'), [(a * 2 + b, b * 2 + a) for a in rang...  18.7 us
    pallas_call x1, Pallas kernels, back(): pl.pallas_call(back_kernel, grid=(micro,), in_specs=[part(p) for p in sta...  14.7 us
    reduce_scatter x1, waiting for transfers between devices, local(): lax.psum_scatter(grad_ffn, plane, scatter_dimension=0, tiled=True)  12.6 us
    all_to_all x1, waiting for transfers between devices, local(): grad_att = lax.all_to_all(grad_att, plane, 0, 0)  12.2 us
    pallas_call x1, Pallas kernels, attend(): pl.pallas_call(attend_kernel, grid_spec=pltpu.PrefetchScalarGridSpec(num_...  11 us
  transfers between devices with their start and end apart: 52, of which 23 were waited for; matrix products, arithmetic and copies ran while one was open for 7% of the time, Pallas kernels for 14%

profile of v1, /device:TPU:1, one launch (start us, length us, event | category | flops | bytes accessed | tf_op | source)
XLA Modules:
  0.0 277.5 jit_solution(10553148445922283143)
XLA Ops:
  8.3 4.5 %collective-permute-start.4 = (bf16[4,64,1024]{2,1,0:T(8,128)(2,1)S(1)}, bf16[4,64,1024]{2,1,0:T(8,128)(2,1)S(1)}, u32[]{:S(2)}, u32[]{:S(2)}) collective-permute-start(bf16[4,64,1024]{2,1,0:T(8,128)(2,1)S(1)} %pad_maximum_fusion.3), channel_id=1, source_target_pairs={{0,0},{1,8},{8,1},{9,9},{2,2},{3,10},{10,3},{11,11},{4,4},{5,12},{... | collective-permute-start | bytes 1572872 | tf_op jit(solution)/shard_map/ppermute | solution.py:43
  17.2 3.9 %collective-permute-start = (bf16[64,384]{1,0:T(8,128)(2,1)S(1)}, bf16[64,384]{1,0:T(8,128)(2,1)S(1)}, u32[]{:S(2)}, u32[]{:S(2)}) collective-permute-start(bf16[64,384]{1,0:T(8,128)(2,1)S(1)} %pad_maximum_fusion.7), channel_id=1, source_target_pairs={{0,0},{1,8},{8,1},{9,9},{16,16},{17,24},{24,17},{25,25},{2,2},{3,1... | collective-permute-start | bytes 147464 | tf_op jit(solution)/shard_map/ppermute | solution.py:59
  24.2 3.1 %collective-permute-done.5 = s32[2,512]{1,0:T(2,128)S(1)} collective-permute-done((s32[2,512]{1,0:T(2,128)}, s32[2,512]{1,0:T(2,128)S(1)}, u32[]{:S(2)}, u32[]{:S(2)}) %collective-permute-start.5) | collective-permute-done | bytes 4128 | tf_op jit(solution)/shard_map/ppermute | solution.py:43
  34.3 3.1 %collective-permute-done.13.refs_5_ = bf16[256,384]{1,0:T(8,128)(2,1)S(1)} collective-permute-done((bf16[256,384]{1,0:T(8,128)(2,1)S(1)}, bf16[256,384]{1,0:T(8,128)(2,1)S(1)}, u32[]{:S(2)}, u32[]{:S(2)}) %collective-permute-start.13) | collective-permute-done | bytes 196640 | tf_op jit(solution)/shard_map/ppermute | solution.py:63
  44.4 3.3 %collective-permute-start.7 = (bf16[4,64,1024]{2,1,0:T(8,128)(2,1)S(1)}, bf16[4,64,1024]{2,1,0:T(8,128)(2,1)S(1)}, u32[]{:S(2)}, u32[]{:S(2)}) collective-permute-start(bf16[4,64,1024]{2,1,0:T(8,128)(2,1)S(1)} %collective-permute-done.4), channel_id=1, source_target_pairs={{0,4},{2,6},{4,0},{6,2},{1,5},{3,7},{5,1},{7,3},{8,12},{10,14},{12... | collective-permute-start | bytes 1572872 | tf_op jit(solution)/shard_map/ppermute | solution.py:49
  49.8 7.5 %collective-permute-done.8 = bf16[4,64,1024]{2,1,0:T(8,128)(2,1)S(1)} collective-permute-done((bf16[4,64,1024]{2,1,0:T(8,128)(2,1)S(1)}, bf16[4,64,1024]{2,1,0:T(8,128)(2,1)S(1)}, u32[]{:S(2)}, u32[]{:S(2)}) %collective-permute-start.8) | collective-permute-done | bytes 524320 | tf_op jit(solution)/shard_map/ppermute | solution.py:49
  57.3 12.7 %collective-permute-done.7 = bf16[4,64,1024]{2,1,0:T(8,128)(2,1)S(1)} collective-permute-done((bf16[4,64,1024]{2,1,0:T(8,128)(2,1)S(1)}, bf16[4,64,1024]{2,1,0:T(8,128)(2,1)S(1)}, u32[]{:S(2)}, u32[]{:S(2)}) %collective-permute-start.7) | collective-permute-done | bytes 524320 | tf_op jit(solution)/shard_map/ppermute | solution.py:49
  70.6 3.1 %multiply_sine_fusion = (f32[2,512,128]{2,1,0:T(8,128)}, f32[2,512,128]{2,1,0:T(8,128)}) fusion(f32[128]{0:T(128)S(1)} %mul.108, f32[2,512]{1,0:T(2,128)S(1)} %subtract_convert_fusion), kind=kLoop, calls=%fused_computation.11 | loop fusion | flops 131072 | bytes 1053184 | tf_op jit(solution)/shard_map/sin | solution.py:555
  83.7 11.0 %attend.1 = (bf16[1024,128]{1,0:T(8,128)(2,1)}, bf16[1024,1024]{1,0:T(8,128)(2,1)}, bf16[1024,1024]{1,0:T(8,128)(2,1)}, bf16[1024,384]{1,0:T(8,128)(2,1)}, f32[1...) custom-call(s32[4]{0:T(128)} %pad_add_fusion.at_ref, ...), custom_call_target="tpu_custom_call" | custom-call | flops 12000000000 | bytes 10000000 | tf_op jit(solution)/shard_map/attend/pallas_call | solution.py:186
  99.7 5.1 %collective-permute-done.19.refs_3_ = bf16[1024,128]{1,0:T(8,128)(2,1)S(1)} collective-permute-done((bf16[1024,128]{1,0:T(8,128)(2,1)S(1)}, bf16[1024,128]{1,0:T(8,128)(2,1)S(1)}, u32[]{:S(2)}, u32[]{:S(2)}) %collective-permute-start.19) | collective-permute-done | bytes 262176 | tf_op jit(solution)/shard_map/ppermute | solution.py:49
  104.8 6.1 %collective-permute-done.18.refs_2_ = bf16[1024,128]{1,0:T(8,128)(2,1)S(1)} collective-permute-done((bf16[1024,128]{1,0:T(8,128)(2,1)S(1)}, bf16[1024,128]{1,0:T(8,128)(2,1)S(1)}, u32[]{:S(2)}, u32[]{:S(2)}) %collective-permute-start.18) | collective-permute-done | bytes 262176 | tf_op jit(solution)/shard_map/ppermute | solution.py:49
  116.0 21.3 %feed.1 = (f32[256,1024]{1,0:T(8,128)}, bf16[1024,1024]{1,0:T(8,128)(2,1)}, bf16[1024,576]{1,0:T(8,128)(2,1)}, bf16[1024,1152]{1,0:T(8,128)(2,1)}, bf16[2,256,10...) custom-call(s32[4]{0:T(128)} %pad_add_fusion.at_ref, ...), custom_call_target="tpu_custom_call" | custom-call | flops 8999999488 | bytes 10000000 | tf_op jit(solution)/shard_map/feed/pallas_call | solution.py:308
  147.6 5.3 %collective-permute-done.27 = bf16[2,64,1024]{2,1,0:T(8,128)(2,1)S(1)} collective-permute-done((bf16[2,64,1024]{2,1,0:T(8,128)(2,1)}, bf16[2,64,1024]{2,1,0:T(8,128)(2,1)S(1)}, u32[]{:S(2)}, u32[]{:S(2)}) %collective-permute-start.27) | collective-permute-done | bytes 262176 | tf_op jit(solution)/shard_map/ppermute | solution.py:49
  152.9 6.5 %collective-permute-done.28 = bf16[2,64,1024]{2,1,0:T(8,128)(2,1)S(1)} collective-permute-done((bf16[2,64,1024]{2,1,0:T(8,128)(2,1)}, bf16[2,64,1024]{2,1,0:T(8,128)(2,1)S(1)}, u32[]{:S(2)}, u32[]{:S(2)}) %collective-permute-start.28) | collective-permute-done | bytes 262176 | tf_op jit(solution)/shard_map/ppermute | solution.py:49
  165.5 8.8 %weights_back.1 = bf16[1024,1728]{1,0:T(8,128)(2,1)} custom-call(bf16[1024,1024]{1,0:T(8,128)(2,1)} %get-tuple-element.101.second_ref, bf16[1024,1024]{1,0:T(8,128)(2,1)} %get-tuple-element.102.up_ref, bf16[1024,1152]{1,0:T(8,128)(2,1)} %get-tuple-element.103.low_ref, bf16[1024,576]{1,0:T(8,128)(2,1)} %get-tuple-element.104.inner_ref), custom_call_target="tpu_custom_call" | custom-call | flops 4000000000 | bytes 10000000 | tf_op jit(solution)/shard_map/weights_back/pallas_call | solution.py:353
  181.9 14.7 %back.1 = (bf16[2,256,1024]{2,1,0:T(8,128)(2,1)}, bf16[2,256,1024]{2,1,0:T(8,128)(2,1)}, bf16[16,80,384]{2,1,0:T(8,128)(2,1)}) custom-call(bf16[2,64,1024]{2,1,0:T(8,128)(2,1)} %copy-done.5, bf16[2,64,1024]{2,1,0:T(8,128)(2,1)} %copy-done.18, bf16[2,64,1024]{2,1,0:T(8,128)(2,1)} %copy-done.17, bf16[2,64,1024]{2,1,0:T(8,128)(2,1)} %copy-done.16, ...), custom_call_target="tpu_custom_call" | custom-call | flops 15000000512 | bytes 10000000 | tf_op jit(solution)/shard_map/back/pallas_call | solution.py:456
  197.0 4.9 %all-to-all-start = ((bf16[16,80,384]{2,1,0:T(8,128)(2,1)}), bf16[16,80,384]{2,1,0:T(8,128)(2,1)S(1)}, u32[]{:S(2)}, u32[]{:S(2)}) async-start(bf16[16,80,384]{2,1,0:T(8,128)(2,1)} %get-tuple-element.130), calls=%async_computation | async-start | bytes 1966080 | tf_op jit(solution)/shard_map/all_to_all | solution.py:594
  201.9 3.9 %split.3 = (f32[4,64,1024]{2,1,0:T(8,128)}, bf16[4,64,1024]{2,1,0:T(8,128)(2,1)}, bf16[4,64,1024]{2,1,0:T(8,128)(2,1)}, bf16[4,64,1024]{2,1,0:T(8,128)(2,1)}) custom-call(bf16[2,256,1024]{2,1,0:T(8,128)(2,1)} %get-tuple-element.125.refs_0_, bf16[2,256,1024]{2,1,0:T(8,128)(2,1)} %collective-permute-done.37.refs_1_, ...), custom_call_target="tpu_custom_call" | custom-call | tf_op jit(solution)/shard_map/split/pallas_call | solution.py:500
  209.1 12.2 %all-to-all-done = bf16[16,80,384]{2,1,0:T(8,128)(2,1)S(1)} async-done(((bf16[16,80,384]{2,1,0:T(8,128)(2,1)}), bf16[16,80,384]{2,1,0:T(8,128)(2,1)S(1)}, u32[]{:S(2)}, u32[]{:S(2)}) %all-to-all-start) | async-done | bytes 983072 | tf_op jit(solution)/shard_map/all_to_all | solution.py:594
  221.2 10.8 %collective-permute-done.40 = bf16[4,64,1024]{2,1,0:T(8,128)(2,1)} collective-permute-done((bf16[4,64,1024]{2,1,0:T(8,128)(2,1)}, bf16[4,64,1024]{2,1,0:T(8,128)(2,1)}, u32[]{:S(2)}, u32[]{:S(2)}) %collective-permute-start.40) | collective-permute-done | bytes 524320 | tf_op jit(solution)/shard_map/ppermute | solution.py:49
  233.8 3.1 %collective-permute-start.43 = (f32[64,384]{1,0:T(8,128)S(1)}, f32[64,384]{1,0:T(8,128)S(1)}, u32[]{:S(2)}, u32[]{:S(2)}) collective-permute-start(f32[64,384]{1,0:T(8,128)S(1)} %slice.158), channel_id=1, source_target_pairs={{0,0},{1,8},{8,1},{9,9},{2,2},{3,10},{10,3},{11,11},{4,4},{5,12},{... | collective-permute-start | bytes 294920 | tf_op jit(solution)/shard_map/ppermute | solution.py:43
  248.5 12.6 %reduce-scatter.2.cloned.1.call-done = bf16[64,1728]{1,0:T(8,128)(2,1)} async-done(((bf16[1024,1728]{1,0:T(8,128)(2,1)}), bf16[64,1728]{1,0:T(8,128)(2,1)}) %reduce-scatter.2.cloned.1.call-update) | async-done | bytes 221200 | tf_op jit(solution)/shard_map/reduce_scatter | solution.py:588
  261.1 4.2 %collective-permute-start.44 = (bf16[64,1728]{1,0:T(8,128)(2,1)}, bf16[64,1728]{1,0:T(8,128)(2,1)S(1)}, u32[]{:S(2)}, u32[]{:S(2)}) collective-permute-start(bf16[64,1728]{1,0:T(8,128)(2,1)} %reduce-scatter.2.cloned.1.call-done), channel_id=1, source_target_pairs={{0,0},{1,8},{8,1},{9,9},{2,2},{3,10},{10,3},{11,11},{4,4},{5,12},{... | collective-permute-start | bytes 663560 | tf_op jit(solution)/shard_map/ppermute | solution.py:43
  266.2 3.1 %collective-permute-done.44 = bf16[64,1728]{1,0:T(8,128)(2,1)S(1)} collective-permute-done((bf16[64,1728]{1,0:T(8,128)(2,1)}, bf16[64,1728]{1,0:T(8,128)(2,1)S(1)}, u32[]{:S(2)}, u32[]{:S(2)}) %collective-permute-start.44) | collective-permute-done | bytes 221216 | tf_op jit(solution)/shard_map/ppermute | solution.py:43
  (219 shorter events, 88.1 us)
Async XLA Ops:
  7.2 107.8 %all-gather.2.cloned.1.call-start = ((), (), s32[]{:S(2)}) async-start(), calls=%async_computation.2 | async-start | bytes 3899392 | tf_op jit(solution)/shard_map/all_gather | solution.py:561
  8.3 19.0 %collective-permute-start.4 = (bf16[4,64,1024]{2,1,0:T(8,128)(2,1)S(1)}, bf16[4,64,1024]{2,1,0:T(8,128)(2,1)S(1)}, u32[]{:S(2)}, u32[]{:S(2)}) collective-permute-start(bf16[4,64,1024]{2,1,0:T(8,128)(2,1)S(1)} %pad_maximum_fusion.3), channel_id=1, source_target_pairs={{0,0},{1,8},{8,1},{9,9},{2,2},{3,10},{10,3},{11,11},{4,4},{5,12},{... | collective-permute-start | bytes 1572872 | tf_op jit(solution)/shard_map/ppermute | solution.py:43
  27.3 12.7 %collective-permute-start.10 = (bf16[64,1728]{1,0:T(8,128)(2,1)S(1)}, bf16[64,1728]{1,0:T(8,128)(2,1)S(1)}, u32[]{:S(2)}, u32[]{:S(2)}) collective-permute-start(bf16[64,1728]{1,0:T(8,128)(2,1)S(1)} %concatenate.37), channel_id=1, source_target_pairs={{0,0},{1,8},{8,1},{9,9},{2,2},{3,10},{10,3},{11,11},{4,4},{5,12},{... | collective-permute-start | bytes 663560 | tf_op jit(solution)/shard_map/ppermute | solution.py:43
  40.8 220.3 %reduce-scatter.2.cloned.1.call-start = ((), (), s32[]{:S(2)}) async-start(), calls=%async_computation.3 | async-start | bytes 3899392 | tf_op jit(solution)/shard_map/reduce_scatter | solution.py:588
  42.7 14.6 %collective-permute-start.8 = (bf16[4,64,1024]{2,1,0:T(8,128)(2,1)S(1)}, bf16[4,64,1024]{2,1,0:T(8,128)(2,1)S(1)}, u32[]{:S(2)}, u32[]{:S(2)}) collective-permute-start(bf16[4,64,1024]{2,1,0:T(8,128)(2,1)S(1)} %collective-permute-done.4), channel_id=1, source_target_pairs={{0,2},{2,4},{4,6},{6,0},{1,3},{3,5},{5,7},{7,1},{8,10},{10,12},{12... | collective-permute-start | bytes 1572872 | tf_op jit(solution)/shard_map/ppermute | solution.py:49
  44.4 25.6 %collective-permute-start.7 = (bf16[4,64,1024]{2,1,0:T(8,128)(2,1)S(1)}, bf16[4,64,1024]{2,1,0:T(8,128)(2,1)S(1)}, u32[]{:S(2)}, u32[]{:S(2)}) collective-permute-start(bf16[4,64,1024]{2,1,0:T(8,128)(2,1)S(1)} %collective-permute-done.4), channel_id=1, source_target_pairs={{0,4},{2,6},{4,0},{6,2},{1,5},{3,7},{5,1},{7,3},{8,12},{10,14},{12... | collective-permute-start | bytes 1572872 | tf_op jit(solution)/shard_map/ppermute | solution.py:49
  47.7 22.3 %collective-permute-start.6 = (bf16[4,64,1024]{2,1,0:T(8,128)(2,1)S(1)}, bf16[4,64,1024]{2,1,0:T(8,128)(2,1)S(1)}, u32[]{:S(2)}, u32[]{:S(2)}) collective-permute-start(bf16[4,64,1024]{2,1,0:T(8,128)(2,1)S(1)} %collective-permute-done.4), channel_id=1, source_target_pairs={{0,6},{2,0},{4,2},{6,4},{1,7},{3,1},{5,3},{7,5},{8,14},{10,8},{12,... | collective-permute-start | bytes 1572872 | tf_op jit(solution)/shard_map/ppermute | solution.py:49
  70.4 13.3 %collective-permute-start.9 = (bf16[4,2,64,1024]{3,2,1,0:T(8,128)(2,1)S(1)}, bf16[4,2,64,1024]{3,2,1,0:T(8,128)(2,1)}, u32[]{:S(2)}, u32[]{:S(2)}) collective-permute-start(bf16[4,2,64,1024]{3,2,1,0:T(8,128)(2,1)S(1)} %pad_maximum_fusion.refs_0_), channel_id=1, source_target_pairs={{0,8},{8,0},{1,9},{9,1},{2,10},{10,2},{3,11},{11,3},{4,12},{12,4},... | collective-permute-start | bytes 3145736 | tf_op jit(solution)/shard_map/ppermute | solution.py:67
  77.7 17.0 %collective-permute-start.16 = (bf16[1024,128]{1,0:T(8,128)(2,1)S(1)}, bf16[1024,128]{1,0:T(8,128)(2,1)}, u32[]{:S(2)}, u32[]{:S(2)}) collective-permute-start(bf16[1024,128]{1,0:T(8,128)(2,1)S(1)} %pad_maximum_fusion.5), channel_id=1, source_target_pairs={{0,2},{2,4},{4,6},{6,0},{1,3},{3,5},{5,7},{7,1},{8,10},{10,12},{12... | collective-permute-start | bytes 786440 | tf_op jit(solution)/shard_map/ppermute | solution.py:49
  79.3 15.4 %collective-permute-start.15 = (bf16[1024,128]{1,0:T(8,128)(2,1)S(1)}, bf16[1024,128]{1,0:T(8,128)(2,1)}, u32[]{:S(2)}, u32[]{:S(2)}) collective-permute-start(bf16[1024,128]{1,0:T(8,128)(2,1)S(1)} %pad_maximum_fusion.5), channel_id=1, source_target_pairs={{0,4},{2,6},{4,0},{6,2},{1,5},{3,7},{5,1},{7,3},{8,12},{10,14},{12... | collective-permute-start | bytes 786440 | tf_op jit(solution)/shard_map/ppermute | solution.py:49
  81.5 13.2 %collective-permute-start.14 = (bf16[1024,128]{1,0:T(8,128)(2,1)S(1)}, bf16[1024,128]{1,0:T(8,128)(2,1)}, u32[]{:S(2)}, u32[]{:S(2)}) collective-permute-start(bf16[1024,128]{1,0:T(8,128)(2,1)S(1)} %pad_maximum_fusion.5), channel_id=1, source_target_pairs={{0,6},{2,0},{4,2},{6,4},{1,7},{3,1},{5,3},{7,5},{8,14},{10,8},{12,... | collective-permute-start | bytes 786440 | tf_op jit(solution)/shard_map/ppermute | solution.py:49
  82.2 30.6 %collective-permute-start.25 = (bf16[4,2,64,1024]{3,2,1,0:T(8,128)(2,1)S(1)}, bf16[4,2,64,1024]{3,2,1,0:T(8,128)(2,1)}, u32[]{:S(2)}, u32[]{:S(2)}) collective-permute-start(bf16[4,2,64,1024]{3,2,1,0:T(8,128)(2,1)S(1)} %pad_maximum_fusion.2.refs_13_), channel_id=1, source_target_pairs={{0,8},{8,0},{1,9},{9,1},{2,10},{10,2},{3,11},{11,3},{4,12},{12,4},... | collective-permute-start | bytes 3145736 | tf_op jit(solution)/shard_map/ppermute | solution.py:67
  96.0 19.0 %collective-permute-start.24 = (bf16[4,1024,128]{2,1,0:T(8,128)(2,1)S(1)}, bf16[4,1024,128]{2,1,0:T(8,128)(2,1)S(1)}, u32[]{:S(2)}, u32[]{:S(2)}) collective-permute-start(bf16[4,1024,128]{2,1,0:T(8,128)(2,1)S(1)} %pad_maximum_fusion.1.refs_8_), channel_id=1, source_target_pairs={{0,8},{8,0},{1,9},{9,1},{2,10},{10,2},{3,11},{11,3},{4,12},{12,4},... | collective-permute-start | bytes 3145736 | tf_op jit(solution)/shard_map/ppermute | solution.py:67
  96.8 14.1 %collective-permute-start.18 = (bf16[1024,128]{1,0:T(8,128)(2,1)S(1)}, bf16[1024,128]{1,0:T(8,128)(2,1)S(1)}, u32[]{:S(2)}, u32[]{:S(2)}) collective-permute-start(bf16[1024,128]{1,0:T(8,128)(2,1)S(1)} %copy-done.15), channel_id=1, source_target_pairs={{0,4},{2,6},{4,0},{6,2},{1,5},{3,7},{5,1},{7,3},{8,12},{10,14},{12... | collective-permute-start | bytes 786440 | tf_op jit(solution)/shard_map/ppermute | solution.py:49
  144.7 14.6 %collective-permute-start.28 = (bf16[2,64,1024]{2,1,0:T(8,128)(2,1)}, bf16[2,64,1024]{2,1,0:T(8,128)(2,1)S(1)}, u32[]{:S(2)}, u32[]{:S(2)}) collective-permute-start(bf16[2,64,1024]{2,1,0:T(8,128)(2,1)} %get-tuple-element.109), channel_id=1, source_target_pairs={{0,4},{2,6},{4,0},{6,2},{1,5},{3,7},{5,1},{7,3},{8,12},{10,14},{12... | collective-permute-start | bytes 786440 | tf_op jit(solution)/shard_map/ppermute | solution.py:49
  161.4 12.9 %collective-permute-start.32 = (bf16[2,64,1024]{2,1,0:T(8,128)(2,1)S(1)}, bf16[2,64,1024]{2,1,0:T(8,128)(2,1)S(1)}, u32[]{:S(2)}, u32[]{:S(2)}) collective-permute-start(bf16[2,64,1024]{2,1,0:T(8,128)(2,1)S(1)} %fusion.1.refs_0_), channel_id=1, source_target_pairs={{0,2},{2,4},{4,6},{6,0},{1,3},{3,5},{5,7},{7,1},{8,10},{10,12},{12... | collective-permute-start | bytes 786440 | tf_op jit(solution)/shard_map/ppermute | solution.py:49
  162.8 14.2 %collective-permute-start.31 = (bf16[2,64,1024]{2,1,0:T(8,128)(2,1)S(1)}, bf16[2,64,1024]{2,1,0:T(8,128)(2,1)S(1)}, u32[]{:S(2)}, u32[]{:S(2)}) collective-permute-start(bf16[2,64,1024]{2,1,0:T(8,128)(2,1)S(1)} %fusion.1.refs_0_), channel_id=1, source_target_pairs={{0,4},{2,6},{4,0},{6,2},{1,5},{3,7},{5,1},{7,3},{8,12},{10,14},{12... | collective-permute-start | bytes 786440 | tf_op jit(solution)/shard_map/ppermute | solution.py:49
  179.1 22.8 %collective-permute-start.38 = (bf16[2,256,1024]{2,1,0:T(8,128)(2,1)}, bf16[2,256,1024]{2,1,0:T(8,128)(2,1)}, u32[]{:S(2)}, u32[]{:S(2)}) collective-permute-start(bf16[2,256,1024]{2,1,0:T(8,128)(2,1)} %get-tuple-element.128), channel_id=1, source_target_pairs={{0,8},{8,0},{1,9},{9,1},{2,10},{10,2},{3,11},{11,3},{4,12},{12,4},... | collective-permute-start | bytes 3145736 | tf_op jit(solution)/shard_map/ppermute | solution.py:67
  197.0 24.2 %all-to-all-start = ((bf16[16,80,384]{2,1,0:T(8,128)(2,1)}), bf16[16,80,384]{2,1,0:T(8,128)(2,1)S(1)}, u32[]{:S(2)}, u32[]{:S(2)}) async-start(bf16[16,80,384]{2,1,0:T(8,128)(2,1)} %get-tuple-element.130), calls=%async_computation | async-start | bytes 1966080 | tf_op jit(solution)/shard_map/all_to_all | solution.py:594
  205.8 15.4 %collective-permute-start.39 = (bf16[4,64,1024]{2,1,0:T(8,128)(2,1)}, bf16[4,64,1024]{2,1,0:T(8,128)(2,1)S(1)}, u32[]{:S(2)}, u32[]{:S(2)}) collective-permute-start(bf16[4,64,1024]{2,1,0:T(8,128)(2,1)} %get-tuple-element.131), channel_id=1, source_target_pairs={{0,2},{2,4},{4,6},{6,0},{1,3},{3,5},{5,7},{7,1},{8,10},{10,12},{12... | collective-permute-start | bytes 1572872 | tf_op jit(solution)/shard_map/ppermute | solution.py:49
  206.3 25.7 %collective-permute-start.40 = (bf16[4,64,1024]{2,1,0:T(8,128)(2,1)}, bf16[4,64,1024]{2,1,0:T(8,128)(2,1)}, u32[]{:S(2)}, u32[]{:S(2)}) collective-permute-start(bf16[4,64,1024]{2,1,0:T(8,128)(2,1)} %get-tuple-element.132), channel_id=1, source_target_pairs={{0,4},{2,6},{4,0},{6,2},{1,5},{3,7},{5,1},{7,3},{8,12},{10,14},{12... | collective-permute-start | bytes 1572872 | tf_op jit(solution)/shard_map/ppermute | solution.py:49
  208.9 23.2 %collective-permute-start.41 = (bf16[4,64,1024]{2,1,0:T(8,128)(2,1)}, bf16[4,64,1024]{2,1,0:T(8,128)(2,1)}, u32[]{:S(2)}, u32[]{:S(2)}) collective-permute-start(bf16[4,64,1024]{2,1,0:T(8,128)(2,1)} %get-tuple-element.133), channel_id=1, source_target_pairs={{0,6},{2,0},{4,2},{6,4},{1,7},{3,1},{5,3},{7,5},{8,14},{10,8},{12,... | collective-permute-start | bytes 1572872 | tf_op jit(solution)/shard_map/ppermute | solution.py:49
  233.8 13.3 %collective-permute-start.43 = (f32[64,384]{1,0:T(8,128)S(1)}, f32[64,384]{1,0:T(8,128)S(1)}, u32[]{:S(2)}, u32[]{:S(2)}) collective-permute-start(f32[64,384]{1,0:T(8,128)S(1)} %slice.158), channel_id=1, source_target_pairs={{0,0},{1,8},{8,1},{9,9},{2,2},{3,10},{10,3},{11,11},{4,4},{5,12},{... | collective-permute-start | bytes 294920 | tf_op jit(solution)/shard_map/ppermute | solution.py:43
  243.0 22.4 %collective-permute-start.42 = (bf16[4,64,1024]{2,1,0:T(8,128)(2,1)S(1)}, bf16[4,64,1024]{2,1,0:T(8,128)(2,1)S(1)}, u32[]{:S(2)}, u32[]{:S(2)}) collective-permute-start(bf16[4,64,1024]{2,1,0:T(8,128)(2,1)S(1)} %pad_maximum_fusion.4), channel_id=1, source_target_pairs={{0,0},{1,8},{8,1},{9,9},{2,2},{3,10},{10,3},{11,11},{4,4},{5,12},{... | collective-permute-start | bytes 1572872 | tf_op jit(solution)/shard_map/ppermute | solution.py:43
  (60 other events, 471.9 us)
Sparse Core Ops, SparseCore 0:
  41.0 49.6 all-gather.1
  177.2 83.8 reduce-scatter.1

commit v2 on v1

--- a/solution.py
+++ b/solution.py
@@ -57,6 +57,10 @@
                 x = (xh * 2 + a - k) % 4
                 perm.append((xh * 4 + a * 2 + b, (x // 2) * 4 + b * 2 + x % 2))
     return lax.ppermute(value, ("xh", "core", "xl"), perm)
+
+
+def to_x(value, k):
+    return lax.ppermute(value, ("xh", "xl"), [(x, (x + k) % 4) for x in range(4)])
 
 
 def from_y(value, k):
@@ -220,13 +224,9 @@
     )(at, *pieces, *weights, gain, qk_gain, cosine, sine, bias)
 
 
-def feed_kernel(at_ref, *refs):
+def state_kernel(at_ref, *refs):
     mixed_refs, w_refs = refs[:8], refs[8:10]
-    x_ref, gain_ref, wf_ref = refs[10:13]
-    up_refs = refs[13:15]
-    state_ref, second_ref, inner_ref, low_ref, own_ref, other_ref = refs[15:21]
-    up_ref, down_own_ref, down_other_ref = refs[21:24]
-    w_out, mixed, w_gu = refs[24:]
+    x_ref, gain_ref, state_ref, second_ref, w_out, mixed = refs[10:]
     step = pl.program_id(0)
     micro, side = step // 2, lax.rem(step, 2)
 
@@ -240,17 +240,6 @@
                     w_out[pl.ds(row, 64), i * 128 : i * 128 + 128] = w_refs[i // 4][
                         i % 4, ky * 256 + kx * 64 : ky * 256 + kx * 64 + 64, :
                     ]
-        for rows in (slice(i, i + 128) for i in range(0, w_gu.shape[0], 128)):
-            w_gu[rows, :512] = wf_ref[rows, :512]
-            rest = wf_ref[rows, 512:1152].astype(f32)
-            w_gu[rows, 512:] = pltpu.roll(rest, 576, 1).astype(bf16)
-
-    for i, ref in enumerate(up_refs):
-
-        @pl.when(side == i)
-        def _():
-            for j in range(4):
-                up_ref[j * 64 : j * 64 + 64, :] = ref[j, 0]
 
     for i, ref in enumerate(mixed_refs):
         flip, k = i // 4, i % 4
@@ -260,9 +249,57 @@
             mixed[j * 64 : j * 64 + 64, i * 128 : i * 128 + 128] = ref[pl.ds(row, 64), :]
     state = x_ref[...].astype(f32) + product_nt(mixed[...], w_out[...])
     state_ref[...] = state[:64]
-    second = (state * rms_scale(state) * gain_ref[0:1, :]).astype(bf16)
-    second_ref[...] = second
-    both = product(second, w_gu[...])
+    second_ref[...] = (state * rms_scale(state) * gain_ref[0:1, :]).astype(bf16)
+
+
+def second_norm(at, mixed, w_out, x, gain):
+    count, width = x.shape
+    steps = count // 256
+    whole = lambda a: pl.BlockSpec(a.shape, lambda b, at: (0,) * a.ndim)
+    rows = lambda block: pl.BlockSpec((block, width), lambda b, at: (b, 0))
+    return pl.pallas_call(
+        state_kernel,
+        grid_spec=pltpu.PrefetchScalarGridSpec(
+            num_scalar_prefetch=1,
+            grid=(steps,),
+            in_specs=[whole(p) for p in mixed]
+            + [whole(w) for w in w_out]
+            + [rows(256), whole(gain)],
+            out_specs=[rows(64), rows(256)],
+            scratch_shapes=[pltpu.VMEM((width, 1024), bf16), pltpu.VMEM((256, 1024), bf16)],
+        ),
+        out_shape=[
+            jax.ShapeDtypeStruct((steps * 64, width), f32),
+            jax.ShapeDtypeStruct((count, width), bf16),
+        ],
+        compiler_params=pltpu.CompilerParams(vmem_limit_bytes=VMEM),
+        cost_estimate=pl.CostEstimate(flops=3 * 10**9, bytes_accessed=10**7, transcendentals=0),
+        name="second_norm",
+    )(at, *mixed, *w_out, x, gain)
+
+
+def feed_kernel(second_ref, wf_ref, *refs):
+    up_refs = refs[:2]
+    inner_ref, low_ref, own_ref, other_ref = refs[2:6]
+    up_ref, down_own_ref, down_other_ref, w_gu = refs[6:]
+    step = pl.program_id(0)
+    side = lax.rem(step, 2)
+
+    @pl.when(step == 0)
+    def _():
+        for rows in (slice(i, i + 128) for i in range(0, w_gu.shape[0], 128)):
+            w_gu[rows, :512] = wf_ref[rows, :512]
+            rest = wf_ref[rows, 512:1152].astype(f32)
+            w_gu[rows, 512:] = pltpu.roll(rest, 576, 1).astype(bf16)
+
+    for i, ref in enumerate(up_refs):
+
+        @pl.when(side == i)
+        def _():
+            for j in range(4):
+                up_ref[j * 64 : j * 64 + 64, :] = ref[j, 0]
+
+    both = product(second_ref[...], w_gu[...])
     grad_inner = product(up_ref[...], wf_ref[:, 1152:1728])
 
     def glu(gate, up, grad):
@@ -296,70 +333,76 @@
         down_other_ref[0] = down
 
 
-def feed(at, mixed, w_out, x, cotangent, gain, w_ffn):
-    count, width = x.shape
+def feed(second, w_ffn, cotangent):
+    count, width = second.shape
     steps = count // 256
-    whole = lambda a: pl.BlockSpec(a.shape, lambda b, at: (0,) * a.ndim)
-    rows = lambda cols, block=256: pl.BlockSpec((block, cols), lambda b, at: (b, 0))
-    half = pl.BlockSpec((1, 256, width), lambda b, at: (b // 2, 0, 0))
-    out = lambda shape, kind: jax.ShapeDtypeStruct(shape, kind)
-
-    chain = pl.BlockSpec((4, 1, 64, width), lambda b, at: (0, b // 2, 0, 0))
+    whole = lambda a: pl.BlockSpec(a.shape, lambda b: (0,) * a.ndim)
+    rows = lambda cols: pl.BlockSpec((256, cols), lambda b: (b, 0))
+    half = pl.BlockSpec((1, 256, width), lambda b: (b // 2, 0, 0))
+    chain = pl.BlockSpec((4, 1, 64, width), lambda b: (0, b // 2, 0, 0))
+    out = lambda *shape: jax.ShapeDtypeStruct(shape, bf16)
+    halves_out = out(steps // 2, 256, width)
     return pl.pallas_call(
         feed_kernel,
-        grid_spec=pltpu.PrefetchScalarGridSpec(
-            num_scalar_prefetch=1,
-            grid=(steps,),
-            in_specs=[whole(p) for p in mixed]
-            + [whole(w) for w in w_out]
-            + [rows(width), whole(gain), whole(w_ffn)]
-            + [chain, chain],
-            out_specs=[rows(width, 64), rows(width), rows(576), rows(1152)]
-            + [half, half, rows(width), half, half],
-            scratch_shapes=[
-                pltpu.VMEM((width, 1024), bf16),
-                pltpu.VMEM((256, 1024), bf16),
-                pltpu.VMEM((width, 1152), bf16),
-            ],
-        ),
+        grid=(steps,),
+        in_specs=[rows(width), whole(w_ffn), chain, chain],
+        out_specs=[rows(576), rows(1152), half, half, rows(width), half, half],
+        scratch_shapes=[pltpu.VMEM((width, 1152), bf16)],
         out_shape=[
-            out((steps * 64, width), f32),
-            out((count, width), bf16),
-            out((count, 576), bf16),
-            out((count, 1152), bf16),
-            out((steps // 2, 256, width), bf16),
-            out((steps // 2, 256, width), bf16),
-            out((count, width), bf16),
-            out((steps // 2, 256, width), bf16),
-            out((steps // 2, 256, width), bf16),
+            *(out(count, 576), out(count, 1152), halves_out, halves_out),
+            *(out(count, width), halves_out, halves_out),
         ],
         compiler_params=pltpu.CompilerParams(vmem_limit_bytes=VMEM),
         cost_estimate=pl.CostEstimate(flops=9 * 10**9, bytes_accessed=10**7, transcendentals=10**6),
         name="feed",
-    )(at, *mixed, *w_out, x, gain, w_ffn, *cotangent)
-
-
-def weights_kernel(second_ref, up_ref, low_ref, inner_ref, grad_ref):
+    )(second, w_ffn, *cotangent)
+
+
+def weights_kernel(at_ref, second_ref, up_ref, low_ref, inner_ref, *refs):
+    out_refs, total = refs[:4], refs[4]
     grad = product_tn(second_ref[...], low_ref[...])
-    grad_ref[:, :512] = grad[:, :512].astype(bf16)
-    grad_ref[:, 512:1152] = pltpu.roll(grad[:, 512:], 64, 1).astype(bf16)
-    grad_ref[:, 1152:] = product_tn(up_ref[...], inner_ref[...]).astype(bf16)
-
-
-def weights_back(second, upstream, low, inner):
+    total[:, :512] = grad[:, :512].astype(bf16)
+    total[:, 512:1152] = pltpu.roll(grad[:, 512:], 64, 1).astype(bf16)
+    total[:, 1152:] = product_tn(up_ref[...], inner_ref[...]).astype(bf16)
+    for k, ref in enumerate(out_refs):
+        row = pl.multiple_of(lax.rem(at_ref[1] + k, 4) * 64, 64)
+        ref[0] = total[pl.ds(row, 64), :]
+
+
+def weights_back(at, second, upstream, low, inner):
     count, width = second.shape
-    whole = lambda a: pl.BlockSpec(a.shape, lambda b: (0,) * a.ndim)
-    columns = pl.BlockSpec((count, 256), lambda b: (0, b))
+    whole = lambda a: pl.BlockSpec(a.shape, lambda b, at: (0,) * a.ndim)
+    columns = pl.BlockSpec((count, 256), lambda b, at: (0, lax.rem(at[0] + b, 4)))
     return pl.pallas_call(
         weights_kernel,
-        grid=(width // 256,),
-        in_specs=[columns, columns, whole(low), whole(inner)],
-        out_specs=pl.BlockSpec((256, 1728), lambda b: (b, 0)),
-        out_shape=jax.ShapeDtypeStruct((width, 1728), bf16),
+        grid_spec=pltpu.PrefetchScalarGridSpec(
+            num_scalar_prefetch=1,
+            grid=(4,),
+            in_specs=[columns, columns, whole(low), whole(inner)],
+            out_specs=[pl.BlockSpec((1, 64, 1728), lambda b, at: (b, 0, 0))] * 4,
+            scratch_shapes=[pltpu.VMEM((256, 1728), bf16)],
+        ),
+        out_shape=[jax.ShapeDtypeStruct((4, 64, 1728), bf16)] * 4,
         compiler_params=pltpu.CompilerParams(vmem_limit_bytes=VMEM),
         cost_estimate=pl.CostEstimate(flops=4 * 10**9, bytes_accessed=10**7, transcendentals=0),
         name="weights_back",
-    )(second, upstream, low, inner)
+    )(at, second, upstream, low, inner)
+
+
+def rows_kernel(*refs):
+    for k, out_ref in enumerate(refs[4:]):
+        value = sum(ref[k].astype(f32) for ref in refs[:4])
+        out_ref[...] = value.astype(out_ref.dtype)
+
+
+def sum_rows(values):
+    shape = values[0].shape[1:]
+    return pl.pallas_call(
+        rows_kernel,
+        out_shape=[jax.ShapeDtypeStruct(shape, f32)] + [jax.ShapeDtypeStruct(shape, bf16)] * 3,
+        compiler_params=pltpu.CompilerParams(vmem_limit_bytes=VMEM),
+        name="sum_rows",
+    )(*values)
 
 
 def back_kernel(*refs):
@@ -482,27 +525,22 @@
     )
 
 
-def split_kernel(*refs):
-    count = len(refs) // 2 - 2
-    for i in range(count):
-        own_ref, got_ref = refs[2 * i], refs[2 * i + 1]
-        micro = own_ref.shape[0]
-        for k, ref in enumerate(refs[-4:]):
-            rows = slice(k * 64, k * 64 + 64)
-            value = own_ref[:, rows].astype(f32) + got_ref[:, rows].astype(f32)
-            ref[i * micro : (i + 1) * micro] = value.astype(ref.dtype)
-
-
-def split(own, other, *more):
+def split_kernel(own_ref, got_ref, *refs):
+    for k, ref in enumerate(refs):
+        rows = slice(k * 64, k * 64 + 64)
+        value = own_ref[:, rows].astype(f32) + got_ref[:, rows].astype(f32)
+        ref[...] = value.astype(ref.dtype)
+
+
+def split(own, got):
     micro, _, width = own.shape
-    values = (own, other_core(other)) + more
-    out = lambda kind: jax.ShapeDtypeStruct((len(values) // 2 * micro, 64, width), kind)
+    out = lambda kind: jax.ShapeDtypeStruct((micro, 64, width), kind)
     return pl.pallas_call(
         split_kernel,
         out_shape=[out(f32), out(bf16), out(bf16), out(bf16)],
         compiler_params=pltpu.CompilerParams(vmem_limit_bytes=VMEM),
         name="split",
-    )(*values)
+    )(own, got)
 
 
 def local(
@@ -533,14 +571,14 @@
     at = at.astype(jnp.int32)
 
     segment = swap(segment_ids)
-    tokens_own = swap(jnp.concatenate([tokens, cotangent]))
+    x_own = swap(tokens)
     w_att = jnp.concatenate([w_query, w_key, w_value, w_out.T], axis=1)
     w_att = jnp.concatenate([swap_from_x(w_att, k) for k in range(4)], axis=0)
-    w_ffn = jnp.concatenate([w_gate, w_up, w_down.T], axis=1)
-    w_att, tokens_own, segment, w_ffn = tie(w_att, tokens_own, segment, w_ffn)
-    token_pieces = from_chain(tokens_own)
+    w_att, x_own, segment = tie(w_att, x_own, segment)
+    x_pieces = from_chain(x_own)
     w_att = [w_att] + [from_y(w_att, k) for k in (1, 2, 3)]
-    w_ffn = swap(w_ffn)
+    w_ffn = swap(jnp.concatenate([w_gate, w_up, w_down.T], axis=1))
+    cotangent_own = swap(cotangent)
 
     index = jnp.arange(group, dtype=jnp.int32)
     change = jnp.concatenate(
@@ -557,57 +595,67 @@
     bias = jnp.where(allowed, 0.0, -1e30).astype(bf16)
     qk_gain = jnp.stack([jnp.tile(query_gain, 2), jnp.tile(key_gain, 2)])
 
-    w_ffn, *w_att = tie(w_ffn, *w_att)
+    w_ffn, *pieces = tie(w_ffn, *w_att, *x_pieces)
+    w_att, x_pieces = pieces[:4], pieces[4:]
     w_ffn = lax.all_gather(w_ffn, plane, axis=0, tiled=True)
     w_out_chain = from_chain(jnp.concatenate([w[:, nq + 2 * nk :] for w in w_att], axis=0))
-    token_pieces = tie(*token_pieces)
-    x_chain, x_other = gather_chains([piece[:micro] for piece in token_pieces])
-    cotangent_all = gather_chains([piece[micro:] for piece in token_pieces])
+    x_chain, x_other = gather_chains(x_pieces)
 
     mixed, x, normed, w_abs, raw, query, keys, values, stat = attend(
         at, (x_chain, x_other), w_att, norm_gain.reshape(1, width), qk_gain, cosine, sine, bias
     )
-    mixed, *w_out_chain = tie(mixed, *w_out_chain)
-    w_out_all = gather_chains(w_out_chain)
-    mixed_pieces = gather(mixed)
-    state, second, inner, gu_low, grad_own, grad_other, upstream, down_own, down_other = feed(
-        at, mixed_pieces, w_out_all, x, cotangent_all, ffn_gain.reshape(1, width), w_ffn
-    )
-    down_got = other_core(down_other)
-    parts = split(grad_own, grad_other)
+    mixed, *chains = tie(mixed, *w_out_chain, *from_chain(cotangent_own))
+    w_out_all = gather_chains(chains[:4])
+    cotangent_all = gather_chains(chains[4:])
+    state, second = second_norm(at, gather(mixed), w_out_all, x, ffn_gain.reshape(1, width))
+    inner, gu_low, grad_own, grad_other, upstream, down_own, down_other = feed(
+        second, w_ffn, cotangent_all
+    )
+    parts = split(grad_own, other_core(grad_other))
     got = [from_z(parts[k], -k) for k in (1, 2, 3)]
-    grad_ffn = weights_back(second, upstream, gu_low, inner)
-    got = tie(*got)
+    grad_ffn = weights_back(at, second, upstream, gu_low, inner)
+    *grad_ffn, got_1, got_2, got_3 = tie(*grad_ffn, *got)
+    got = [got_1, got_2, got_3]
+    grad_ffn_got = [to_x(grad_ffn[k], k) for k in (1, 2, 3)]
     grad_second = parts[0] + sum(piece.astype(f32) for piece in got)
     state_own = state.reshape(micro, 2, own, width)[:, 0]
     _, norm_pull = jax.vjp(rms_rows, state_own, ffn_gain)
     grad_state_norm, grad_ffn_gain = norm_pull(grad_second)
-    grad_state = (tokens_own[micro:].astype(f32) + grad_state_norm).astype(bf16)
-    grad_ffn, *state_pieces = tie(grad_ffn, *from_chain(grad_state))
+    grad_state = (cotangent_own.astype(f32) + grad_state_norm).astype(bf16)
+    down = split(down_own, other_core(down_other))
+    state_pieces = from_chain(grad_state)
+    *state_pieces, down_first, down_low = tie(*state_pieces, *down[:2])
+    down = [down_first, down_low] + list(down[2:])
+    down_got = [from_z(down[k], -k) for k in (1, 2, 3)]
     state_pieces += [other_core(piece) for piece in state_pieces]
-    grad_ffn = lax.psum_scatter(grad_ffn, plane, scatter_dimension=0, tiled=True)
 
     grad_own, grad_other, grad_att = back(
         *(state_pieces, normed, w_abs, raw, query, keys, values, stat, mixed, qk_gain),
         *(cosine, sine, bias, norm_gain.reshape(1, width), grad_ffn_gain.reshape(1, width)),
     )
     grad_att = lax.all_to_all(grad_att, plane, 0, 0)
-    parts = split(grad_own, grad_other, down_own, down_got)
-    grad_att, *got = tie(grad_att, *[from_z(parts[k], -k) for k in (1, 2, 3)])
-    total = parts[0] + sum(piece.astype(f32) for piece in got)
-    _, first_pull = jax.vjp(rms_rows, tokens_own[:micro].astype(f32), norm_gain)
-    grad_resid_norm, _ = first_pull(total[:micro])
-    input_grad = grad_state.astype(f32) + grad_resid_norm
-    results = swap(jnp.concatenate([state_own + total[micro:], input_grad]).astype(bf16))
+    grad_got, *down_got = tie(other_core(grad_other), *down_got)
+    output = state_own + down[0] + sum(piece.astype(f32) for piece in down_got)
+    output = swap(output.astype(bf16))
+    parts = split(grad_own, grad_got)
+    got = [from_z(parts[k], -k) for k in (1, 2, 3)]
+    grad_att, got[0], got[1], got[2], *grad_ffn_got = tie(grad_att, *got, *grad_ffn_got)
+    grad_ffn = sum_rows([grad_ffn[0]] + grad_ffn_got)
+    grad_ffn_got = [from_y(grad_ffn[k], -k) for k in (1, 2, 3)]
+    grad_ffn = grad_ffn[0] + sum(piece.astype(f32) for piece in grad_ffn_got)
+    grad_normed = parts[0] + sum(piece.astype(f32) for piece in got)
+    _, first_pull = jax.vjp(rms_rows, x_own.astype(f32), norm_gain)
+    grad_resid_norm, _ = first_pull(grad_normed)
+    input_grad = swap((grad_state.astype(f32) + grad_resid_norm).astype(bf16))
     grad_att = jnp.sum(grad_att.astype(f32), axis=0)
     gains = group_sum(grad_att[64:70].reshape(-1))
     grad_att = swap(grad_att[:64])
-    grad_ffn = swap(grad_ffn).astype(f32)
+    grad_ffn = swap(grad_ffn.astype(bf16)).astype(f32)
     both = nq + nk
     q_gains = gains[2 * width :]
     return (
-        results[:micro],
-        results[micro:],
+        output,
+        input_grad,
         grad_att[:, :nq],
         grad_att[:, nq:both],
         grad_att[:, both : both + nk],

time: 278 us -> 303 us (1.090); the launches traced: 278 us -> 299 us
  starting transfers between devices: 72.6 us -> 98.5 us
  waiting for transfers between devices: 99.4 us -> 86.5 us
  Pallas kernels: 62.3 us -> 70.5 us
    ppermute x0 -> x3, waiting for transfers between devices: none -> 21.5 us  [to_x(): lax.ppermute(value, ('xh', 'xl'), [(x, (x + k) % 4) for x in range(4)])]
    ppermute x21 -> x27, waiting for transfers between devices: 56.7 us -> 41.7 us  [from_z(): return lax.ppermute(value, 'z', [(z, (z - k) % 4) for z in range(4)])]
    reduce_scatter x1 -> x0, waiting for transfers between devices: 12.6 us -> none  [local(): lax.psum_scatter(grad_ffn, plane, scatter_dimension=0, tiled=True)]
    all_to_all x1, waiting for transfers between devices: 12.2 us -> 0.01 us  [local(): grad_att = lax.all_to_all(grad_att, plane, 0, 0)]
    ppermute x15, starting transfers between devices: 8.41 us -> 16.7 us  [other_core(): return lax.ppermute(value, 'core', CORE)]
    pallas_call x2 -> x4, Pallas kernels: 30.1 us -> 36.9 us  [the longest x1 15.4 us: feed(): pl.pallas_call(feed_kernel, grid=(steps,), in_specs=[rows(width), whole(w...]
    ppermute x0 -> x3, starting transfers between devices: none -> 5.19 us  [to_x(): lax.ppermute(value, ('xh', 'xl'), [(x, (x + k) % 4) for x in range(4)])]
    ppermute x6 -> x8, starting transfers between devices: 18.7 us -> 23.2 us  [swap(): lax.ppermute(value, ('core', 'xl'), [(a * 2 + b, b * 2 + a) for a in rang...]
  transfers between devices with their start and end apart: 52 -> 65, of which waited for: 23 -> 26; matrix products, arithmetic and copies ran while one was open for 7% -> 7% of each run, Pallas kernels for 14% -> 14%
where the time goes in v2:
time: 303 us; the launch traced here: 299 us
  starting transfers between devices  98.5 us (33%)
  waiting for transfers between devices  86.5 us (29%)
  Pallas kernels  70.5 us (23%)
  other arithmetic  15.7 us (5%)
  between operations  14.9 us (5%)
  local copies, waits for them, and re-layouts  12.5 us (4%)
    ppermute x27, waiting for transfers between devices, from_z(): return lax.ppermute(value, 'z', [(z, (z - k) % 4) for z in range(4)])  41.7 us
    ppermute x27, starting transfers between devices, from_z(): return lax.ppermute(value, 'z', [(z, (z - k) % 4) for z in range(4)])  32.4 us
    ppermute x8, starting transfers between devices, swap(): lax.ppermute(value, ('core', 'xl'), [(a * 2 + b, b * 2 + a) for a in rang...  23.2 us
    ppermute x3, waiting for transfers between devices, to_x(): lax.ppermute(value, ('xh', 'xl'), [(x, (x + k) % 4) for x in range(4)])  21.5 us
    ppermute x15, starting transfers between devices, other_core(): return lax.ppermute(value, 'core', CORE)  16.7 us
    pallas_call x1, Pallas kernels, feed(): pl.pallas_call(feed_kernel, grid=(steps,), in_specs=[rows(width), whole(w...  15.4 us
    pallas_call x1, Pallas kernels, back(): pl.pallas_call(back_kernel, grid=(micro,), in_specs=[part(p) for p in sta...  14.7 us
    pallas_call x1, Pallas kernels, attend(): pl.pallas_call(attend_kernel, grid_spec=pltpu.PrefetchScalarGridSpec(num_...  10.9 us
  transfers between devices with their start and end apart: 65, of which 26 were waited for; matrix products, arithmetic and copies ran while one was open for 7% of the time, Pallas kernels for 14%

profile of v2, /device:TPU:1, one launch (start us, length us, event | category | flops | bytes accessed | tf_op | source)
XLA Modules:
  0.0 298.6 jit_solution(16437998037934250005)
XLA Ops:
  7.2 4.5 %collective-permute-start.5 = (bf16[2,64,1024]{2,1,0:T(8,128)(2,1)}, bf16[2,64,1024]{2,1,0:T(8,128)(2,1)S(1)}, u32[]{:S(2)}, u32[]{:S(2)}) collective-permute-start(bf16[2,64,1024]{2,1,0:T(8,128)(2,1)} %param.14), channel_id=1, source_target_pairs={{0,0},{1,8},{8,1},{9,9},{2,2},{3,10},{10,3},{11,11},{4,4},{5,12},{... | collective-permute-start | bytes 786440 | tf_op jit(solution)/shard_map/ppermute | solution.py:43
  17.7 3.4 %collective-permute-start.4 = (bf16[64,384]{1,0:T(8,128)(2,1)S(1)}, bf16[64,384]{1,0:T(8,128)(2,1)S(1)}, u32[]{:S(2)}, u32[]{:S(2)}) collective-permute-start(bf16[64,384]{1,0:T(8,128)(2,1)S(1)} %pad_maximum_fusion.5), channel_id=1, source_target_pairs={{0,1},{1,9},{8,16},{9,24},{16,17},{17,25},{24,0},{25,8},{2,3},{3,1... | collective-permute-start | bytes 147464 | tf_op jit(solution)/shard_map/ppermute | solution.py:59
  24.2 3.6 %collective-permute-start = (bf16[64,1728]{1,0:T(8,128)(2,1)S(1)}, bf16[64,1728]{1,0:T(8,128)(2,1)S(1)}, u32[]{:S(2)}, u32[]{:S(2)}) collective-permute-start(bf16[64,1728]{1,0:T(8,128)(2,1)S(1)} %concatenate.27), channel_id=1, source_target_pairs={{0,0},{1,8},{8,1},{9,9},{2,2},{3,10},{10,3},{11,11},{4,4},{5,12},{... | collective-permute-start | bytes 663560 | tf_op jit(solution)/shard_map/ppermute | solution.py:43
  30.7 3.8 %collective-permute-start.10 = (bf16[2,64,1024]{2,1,0:T(8,128)(2,1)S(1)}, bf16[2,64,1024]{2,1,0:T(8,128)(2,1)S(1)}, u32[]{:S(2)}, u32[]{:S(2)}) collective-permute-start(bf16[2,64,1024]{2,1,0:T(8,128)(2,1)S(1)} %collective-permute-done.5), channel_id=1, source_target_pairs={{0,6},{2,0},{4,2},{6,4},{1,7},{3,1},{5,3},{7,5},{8,14},{10,8},{12,... | collective-permute-start | bytes 786440 | tf_op jit(solution)/shard_map/ppermute | solution.py:49
  36.2 7.2 %collective-permute-done.8.refs_4_ = bf16[256,384]{1,0:T(8,128)(2,1)S(1)} collective-permute-done((bf16[256,384]{1,0:T(8,128)(2,1)S(1)}, bf16[256,384]{1,0:T(8,128)(2,1)S(1)}, u32[]{:S(2)}, u32[]{:S(2)}) %collective-permute-start.8) | collective-permute-done | bytes 196640 | tf_op jit(solution)/shard_map/ppermute | solution.py:67
  64.9 4.3 %collective-permute-start.15 = (bf16[1024,128]{1,0:T(8,128)(2,1)S(1)}, bf16[1024,128]{1,0:T(8,128)(2,1)S(1)}, u32[]{:S(2)}, u32[]{:S(2)}) collective-permute-start(bf16[1024,128]{1,0:T(8,128)(2,1)S(1)} %pad_maximum_fusion.3), channel_id=1, source_target_pairs={{0,4},{2,6},{4,0},{6,2},{1,5},{3,7},{5,1},{7,3},{8,12},{10,14},{12... | collective-permute-start | bytes 786440 | tf_op jit(solution)/shard_map/ppermute | solution.py:49
  69.7 10.9 %attend.1 = (bf16[1024,128]{1,0:T(8,128)(2,1)}, bf16[1024,1024]{1,0:T(8,128)(2,1)}, bf16[1024,1024]{1,0:T(8,128)(2,1)}, bf16[1024,384]{1,0:T(8,128)(2,1)}, f32[1...) custom-call(s32[4]{0:T(128)} %pad_add_fusion.at_ref, ...), custom_call_target="tpu_custom_call" | custom-call | flops 12000000000 | bytes 10000000 | tf_op jit(solution)/shard_map/attend/pallas_call | solution.py:190
  89.2 3.6 %collective-permute-done.21.refs_1_ = bf16[1024,128]{1,0:T(8,128)(2,1)S(1)} collective-permute-done((bf16[1024,128]{1,0:T(8,128)(2,1)S(1)}, bf16[1024,128]{1,0:T(8,128)(2,1)S(1)}, u32[]{:S(2)}, u32[]{:S(2)}) %collective-permute-start.21) | collective-permute-done | bytes 262176 | tf_op jit(solution)/shard_map/ppermute | solution.py:49
  94.8 6.2 %collective-permute-done.23.refs_3_ = bf16[1024,128]{1,0:T(8,128)(2,1)S(1)} collective-permute-done((bf16[1024,128]{1,0:T(8,128)(2,1)S(1)}, bf16[1024,128]{1,0:T(8,128)(2,1)S(1)}, u32[]{:S(2)}, u32[]{:S(2)}) %collective-permute-start.23) | collective-permute-done | bytes 262176 | tf_op jit(solution)/shard_map/ppermute | solution.py:49
  105.4 8.5 %second_norm.1 = (f32[256,1024]{1,0:T(8,128)}, bf16[1024,1024]{1,0:T(8,128)(2,1)}) custom-call(s32[4]{0:T(128)} %pad_add_fusion.at_ref, bf16[1024,128]{1,0:T(8,128)(2,1)} %get-tuple-element.116.refs_0_.refs_15_, bf16[1024,128]{1,0:T(8,128)(2,1)} %copy-done.29, bf16[1024,128]{1,0:T(8,128)(2,1)} %copy-done.30, bf16[1024,128]{1,0:T(8,128)(2,1)} %copy-done.31, ...), custom_call_target="tpu_custom_call" | custom-call | flops 3000000000 | bytes 10000000 | tf_op jit(solution)/shard_map/second_norm/pallas_call | solution.py:260
  113.9 15.4 %feed.1 = (bf16[1024,576]{1,0:T(8,128)(2,1)}, bf16[1024,1152]{1,0:T(8,128)(2,1)}, bf16[2,256,1024]{2,1,0:T(8,128)(2,1)}, bf16[2,256,1024]{2,1,0:T(8,128)(2,1)}, ...) custom-call(bf16[1024,1024]{1,0:T(8,128)(2,1)} %get-tuple-element.126.second_ref, ...), custom_call_target="tpu_custom_call" | custom-call | flops 8999999488 | bytes 10000000 | tf_op jit(solution)/shard_map/feed/pallas_call | solution.py:345
  138.5 9.9 %weights_back.1 = (bf16[4,64,1728]{2,1,0:T(8,128)(2,1)}, bf16[4,64,1728]{2,1,0:T(8,128)(2,1)}, bf16[4,64,1728]{2,1,0:T(8,128)(2,1)}, bf16[4,64,1728]{2,1,0:T(8,128)(2,1)}) custom-call(s32[4]{0:T(128)} %pad_add_fusion.at_ref, bf16[1024,1024]{1,0:T(8,128)(2,1)} %get-tuple-element.126.second_ref, bf16[1024,1024]{1,0:T(8,128)(2,1)} %get-tuple-element.135.up_ref, ...), custom_call_target="tpu_custom_call" | custom-call | flops 4000000000 | bytes 10000000 | tf_op jit(solution)/shard_map/weights_back/pallas_call | solution.py:376
  150.9 3.4 %collective-permute-start.34 = (bf16[2,64,1024]{2,1,0:T(8,128)(2,1)S(1)}, bf16[2,64,1024]{2,1,0:T(8,128)(2,1)S(1)}, u32[]{:S(2)}, u32[]{:S(2)}) collective-permute-start(bf16[2,64,1024]{2,1,0:T(8,128)(2,1)S(1)} %fusion.1.refs_0_), channel_id=1, source_target_pairs={{0,6},{2,0},{4,2},{6,4},{1,7},{3,1},{5,3},{7,5},{8,14},{10,8},{12,... | collective-permute-start | bytes 786440 | tf_op jit(solution)/shard_map/ppermute | solution.py:49
  158.6 6.3 %collective-permute-done.34.refs_1_ = bf16[2,64,1024]{2,1,0:T(8,128)(2,1)S(1)} collective-permute-done((bf16[2,64,1024]{2,1,0:T(8,128)(2,1)S(1)}, bf16[2,64,1024]{2,1,0:T(8,128)(2,1)S(1)}, u32[]{:S(2)}, u32[]{:S(2)}) %collective-permute-start.34) | collective-permute-done | bytes 262176 | tf_op jit(solution)/shard_map/ppermute | solution.py:49
  164.9 4.6 %collective-permute-done.36.refs_3_ = bf16[2,64,1024]{2,1,0:T(8,128)(2,1)S(1)} collective-permute-done((bf16[2,64,1024]{2,1,0:T(8,128)(2,1)S(1)}, bf16[2,64,1024]{2,1,0:T(8,128)(2,1)S(1)}, u32[]{:S(2)}, u32[]{:S(2)}) %collective-permute-start.36) | collective-permute-done | bytes 262176 | tf_op jit(solution)/shard_map/ppermute | solution.py:49
  170.1 9.7 %collective-permute-start.39 = (bf16[2,64,1024]{2,1,0:T(8,128)(2,1)S(1)}, bf16[2,64,1024]{2,1,0:T(8,128)(2,1)S(1)}, u32[]{:S(2)}, u32[]{:S(2)}) collective-permute-start(bf16[2,64,1024]{2,1,0:T(8,128)(2,1)S(1)} %collective-permute-done.34.refs_1_), channel_id=1, source_target_pairs={{0,8},{8,0},{1,9},{9,1},{2,10},{10,2},{3,11},{11,3},{4,12},{12,4},... | collective-permute-start | bytes 786440 | tf_op jit(solution)/shard_map/ppermute | solution.py:71
  182.8 14.7 %back.1 = (bf16[2,256,1024]{2,1,0:T(8,128)(2,1)}, bf16[2,256,1024]{2,1,0:T(8,128)(2,1)}, bf16[16,80,384]{2,1,0:T(8,128)(2,1)}) custom-call(bf16[2,64,1024]{2,1,0:T(8,128)(2,1)} %copy-done.7, bf16[2,64,1024]{2,1,0:T(8,128)(2,1)} %copy-done.26, bf16[2,64,1024]{2,1,0:T(8,128)(2,1)} %copy-done.27, bf16[2,64,1024]{2,1,0:T(8,128)(2,1)} %copy-done.28, ...), custom_call_target="tpu_custom_call" | custom-call | flops 15000000512 | bytes 10000000 | tf_op jit(solution)/shard_map/back/pallas_call | solution.py:499
  199.4 3.7 %all-to-all-start = ((bf16[16,80,384]{2,1,0:T(8,128)(2,1)}), bf16[16,80,384]{2,1,0:T(8,128)(2,1)S(1)}, u32[]{:S(2)}, u32[]{:S(2)}) async-start(bf16[16,80,384]{2,1,0:T(8,128)(2,1)} %get-tuple-element.174), calls=%async_computation | async-start | bytes 1966080 | tf_op jit(solution)/shard_map/all_to_all | solution.py:636
  208.5 6.3 %collective-permute-done.45 = bf16[2,64,1024]{2,1,0:T(8,128)(2,1)S(1)} collective-permute-done((bf16[2,64,1024]{2,1,0:T(8,128)(2,1)}, bf16[2,64,1024]{2,1,0:T(8,128)(2,1)S(1)}, u32[]{:S(2)}, u32[]{:S(2)}) %collective-permute-start.45) | collective-permute-done | bytes 262176 | tf_op jit(solution)/shard_map/ppermute | solution.py:49
  214.7 7.0 %collective-permute-done.43 = bf16[2,64,1024]{2,1,0:T(8,128)(2,1)S(1)} collective-permute-done((bf16[2,64,1024]{2,1,0:T(8,128)(2,1)}, bf16[2,64,1024]{2,1,0:T(8,128)(2,1)S(1)}, u32[]{:S(2)}, u32[]{:S(2)}) %collective-permute-start.43) | collective-permute-done | bytes 262176 | tf_op jit(solution)/shard_map/ppermute | solution.py:49
  230.8 21.0 %collective-permute-done.51.refs_2_ = bf16[4,64,1728]{2,1,0:T(8,128)(2,1)} collective-permute-done((bf16[4,64,1728]{2,1,0:T(8,128)(2,1)}, bf16[4,64,1728]{2,1,0:T(8,128)(2,1)}, u32[]{:S(2)}, u32[]{:S(2)}) %collective-permute-start.51) | collective-permute-done | bytes 884768 | tf_op jit(solution)/shard_map/ppermute | solution.py:63
  257.8 3.2 %sum_rows.1 = (f32[64,1728]{1,0:T(8,128)}, bf16[64,1728]{1,0:T(8,128)(2,1)}, bf16[64,1728]{1,0:T(8,128)(2,1)}, bf16[64,1728]{1,0:T(8,128)(2,1)}) custom-call(bf16[4,64,1728]{2,1,0:T(8,128)(2,1)} %get-tuple-element.185.refs_0_, bf16[4,64,1728]{2,1,0:T(8,128)(2,1)} %collective-permute-done.50.refs_1_, bf16[4,64,1728]{2,1,0:T(8,128)(2,1)} %collective-permute-done.51.refs_2_, ...), custom_call_target="tpu_custom_call" | custom-call | tf_op jit(solution)/shard_map/sum_rows/pallas_call | solution.py:400
  270.7 4.6 %collective-permute-start.53 = (bf16[2,64,1024]{2,1,0:T(8,128)(2,1)S(1)}, bf16[2,64,1024]{2,1,0:T(8,128)(2,1)S(1)}, u32[]{:S(2)}, u32[]{:S(2)}) collective-permute-start(bf16[2,64,1024]{2,1,0:T(8,128)(2,1)S(1)} %fusion.5), channel_id=1, source_target_pairs={{0,0},{1,8},{8,1},{9,9},{2,2},{3,10},{10,3},{11,11},{4,4},{5,12},{... | collective-permute-start | bytes 786440 | tf_op jit(solution)/shard_map/ppermute | solution.py:43
  285.5 3.8 %collective-permute-done.58 = bf16[64,1728]{1,0:T(8,128)(2,1)S(1)} collective-permute-done((bf16[64,1728]{1,0:T(8,128)(2,1)S(1)}, bf16[64,1728]{1,0:T(8,128)(2,1)S(1)}, u32[]{:S(2)}, u32[]{:S(2)}) %collective-permute-start.58) | collective-permute-done | bytes 221216 | tf_op jit(solution)/shard_map/ppermute | solution.py:43
  (264 shorter events, 114.2 us)
Async XLA Ops:
  7.2 106.7 %all-gather.2.cloned.1.call-start = ((), (), s32[]{:S(2)}) async-start(), calls=%async_computation.1 | async-start | bytes 3899392 | tf_op jit(solution)/shard_map/all_gather | solution.py:600
  7.2 20.7 %collective-permute-start.5 = (bf16[2,64,1024]{2,1,0:T(8,128)(2,1)}, bf16[2,64,1024]{2,1,0:T(8,128)(2,1)S(1)}, u32[]{:S(2)}, u32[]{:S(2)}) collective-permute-start(bf16[2,64,1024]{2,1,0:T(8,128)(2,1)} %param.14), channel_id=1, source_target_pairs={{0,0},{1,8},{8,1},{9,9},{2,2},{3,10},{10,3},{11,11},{4,4},{5,12},{... | collective-permute-start | bytes 786440 | tf_op jit(solution)/shard_map/ppermute | solution.py:43
  30.7 15.2 %collective-permute-start.10 = (bf16[2,64,1024]{2,1,0:T(8,128)(2,1)S(1)}, bf16[2,64,1024]{2,1,0:T(8,128)(2,1)S(1)}, u32[]{:S(2)}, u32[]{:S(2)}) collective-permute-start(bf16[2,64,1024]{2,1,0:T(8,128)(2,1)S(1)} %collective-permute-done.5), channel_id=1, source_target_pairs={{0,6},{2,0},{4,2},{6,4},{1,7},{3,1},{5,3},{7,5},{8,14},{10,8},{12,... | collective-permute-start | bytes 786440 | tf_op jit(solution)/shard_map/ppermute | solution.py:49
  53.4 15.8 %collective-permute-start.13 = (bf16[4,2,64,1024]{3,2,1,0:T(8,128)(2,1)S(1)}, bf16[4,2,64,1024]{3,2,1,0:T(8,128)(2,1)}, u32[]{:S(2)}, u32[]{:S(2)}) collective-permute-start(bf16[4,2,64,1024]{3,2,1,0:T(8,128)(2,1)S(1)} %pad_maximum_fusion.refs_0_), channel_id=1, source_target_pairs={{0,8},{8,0},{1,9},{9,1},{2,10},{10,2},{3,11},{11,3},{4,12},{12,4},... | collective-permute-start | bytes 3145736 | tf_op jit(solution)/shard_map/ppermute | solution.py:71
  55.7 24.9 %collective-permute-start.19 = (bf16[2,64,1024]{2,1,0:T(8,128)(2,1)S(1)}, bf16[2,64,1024]{2,1,0:T(8,128)(2,1)S(1)}, u32[]{:S(2)}, u32[]{:S(2)}) collective-permute-start(bf16[2,64,1024]{2,1,0:T(8,128)(2,1)S(1)} %collective-permute-done.17), channel_id=1, source_target_pairs={{0,4},{2,6},{4,0},{6,2},{1,5},{3,7},{5,1},{7,3},{8,12},{10,14},{12... | collective-permute-start | bytes 786440 | tf_op jit(solution)/shard_map/ppermute | solution.py:49
  57.5 23.1 %collective-permute-start.20 = (bf16[2,64,1024]{2,1,0:T(8,128)(2,1)S(1)}, bf16[2,64,1024]{2,1,0:T(8,128)(2,1)S(1)}, u32[]{:S(2)}, u32[]{:S(2)}) collective-permute-start(bf16[2,64,1024]{2,1,0:T(8,128)(2,1)S(1)} %collective-permute-done.17), channel_id=1, source_target_pairs={{0,2},{2,4},{4,6},{6,0},{1,3},{3,5},{5,7},{7,1},{8,10},{10,12},{12... | collective-permute-start | bytes 786440 | tf_op jit(solution)/shard_map/ppermute | solution.py:49
  62.1 18.5 %collective-permute-start.14 = (bf16[1024,128]{1,0:T(8,128)(2,1)S(1)}, bf16[1024,128]{1,0:T(8,128)(2,1)S(1)}, u32[]{:S(2)}, u32[]{:S(2)}) collective-permute-start(bf16[1024,128]{1,0:T(8,128)(2,1)S(1)} %pad_maximum_fusion.3), channel_id=1, source_target_pairs={{0,6},{2,0},{4,2},{6,4},{1,7},{3,1},{5,3},{7,5},{8,14},{10,8},{12,... | collective-permute-start | bytes 786440 | tf_op jit(solution)/shard_map/ppermute | solution.py:49
  64.9 15.8 %collective-permute-start.15 = (bf16[1024,128]{1,0:T(8,128)(2,1)S(1)}, bf16[1024,128]{1,0:T(8,128)(2,1)S(1)}, u32[]{:S(2)}, u32[]{:S(2)}) collective-permute-start(bf16[1024,128]{1,0:T(8,128)(2,1)S(1)} %pad_maximum_fusion.3), channel_id=1, source_target_pairs={{0,4},{2,6},{4,0},{6,2},{1,5},{3,7},{5,1},{7,3},{8,12},{10,14},{12... | collective-permute-start | bytes 786440 | tf_op jit(solution)/shard_map/ppermute | solution.py:49
  84.3 20.0 %collective-permute-start.28 = (bf16[4,1024,128]{2,1,0:T(8,128)(2,1)S(1)}, bf16[4,1024,128]{2,1,0:T(8,128)(2,1)S(1)}, u32[]{:S(2)}, u32[]{:S(2)}) collective-permute-start(bf16[4,1024,128]{2,1,0:T(8,128)(2,1)S(1)} %pad_maximum_fusion.1.refs_8_), channel_id=1, source_target_pairs={{0,8},{8,0},{1,9},{9,1},{2,10},{10,2},{3,11},{11,3},{4,12},{12,4},... | collective-permute-start | bytes 3145736 | tf_op jit(solution)/shard_map/ppermute | solution.py:71
  88.2 25.7 %collective-permute-start.29 = (bf16[4,2,64,1024]{3,2,1,0:T(8,128)(2,1)S(1)}, bf16[4,2,64,1024]{3,2,1,0:T(8,128)(2,1)}, u32[]{:S(2)}, u32[]{:S(2)}) collective-permute-start(bf16[4,2,64,1024]{3,2,1,0:T(8,128)(2,1)S(1)} %pad_maximum_fusion.2.refs_0_), channel_id=1, source_target_pairs={{0,8},{8,0},{1,9},{9,1},{2,10},{10,2},{3,11},{11,3},{4,12},{12,4},... | collective-permute-start | bytes 3145736 | tf_op jit(solution)/shard_map/ppermute | solution.py:71
  129.8 25.2 %collective-permute-start.37 = (bf16[2,256,1024]{2,1,0:T(8,128)(2,1)}, bf16[2,256,1024]{2,1,0:T(8,128)(2,1)S(1)}, u32[]{:S(2)}, u32[]{:S(2)}) collective-permute-start(bf16[2,256,1024]{2,1,0:T(8,128)(2,1)} %get-tuple-element.149), channel_id=1, source_target_pairs={{0,8},{8,0},{1,9},{9,1},{2,10},{10,2},{3,11},{11,3},{4,12},{12,4},... | collective-permute-start | bytes 3145736 | tf_op jit(solution)/shard_map/ppermute | solution.py:71
  154.5 15.0 %collective-permute-start.36 = (bf16[2,64,1024]{2,1,0:T(8,128)(2,1)S(1)}, bf16[2,64,1024]{2,1,0:T(8,128)(2,1)S(1)}, u32[]{:S(2)}, u32[]{:S(2)}) collective-permute-start(bf16[2,64,1024]{2,1,0:T(8,128)(2,1)S(1)} %fusion.1.refs_0_), channel_id=1, source_target_pairs={{0,2},{2,4},{4,6},{6,0},{1,3},{3,5},{5,7},{7,1},{8,10},{10,12},{12... | collective-permute-start | bytes 786440 | tf_op jit(solution)/shard_map/ppermute | solution.py:49
  197.5 24.3 %collective-permute-start.42 = (bf16[2,256,1024]{2,1,0:T(8,128)(2,1)}, bf16[2,256,1024]{2,1,0:T(8,128)(2,1)S(1)}, u32[]{:S(2)}, u32[]{:S(2)}) collective-permute-start(bf16[2,256,1024]{2,1,0:T(8,128)(2,1)} %get-tuple-element.164), channel_id=1, source_target_pairs={{0,8},{8,0},{1,9},{9,1},{2,10},{10,2},{3,11},{11,3},{4,12},{12,4},... | collective-permute-start | bytes 3145736 | tf_op jit(solution)/shard_map/ppermute | solution.py:71
  197.7 29.9 %collective-permute-start.50 = (bf16[4,64,1728]{2,1,0:T(8,128)(2,1)}, bf16[4,64,1728]{2,1,0:T(8,128)(2,1)}, u32[]{:S(2)}, u32[]{:S(2)}) collective-permute-start(bf16[4,64,1728]{2,1,0:T(8,128)(2,1)} %get-tuple-element.178), channel_id=1, source_target_pairs={{0,1},{1,16},{16,17},{17,0},{2,3},{3,18},{18,19},{19,2},{4,5},{5,2... | collective-permute-start | bytes 2654216 | tf_op jit(solution)/shard_map/ppermute | solution.py:63
  199.4 54.8 %all-to-all-start = ((bf16[16,80,384]{2,1,0:T(8,128)(2,1)}), bf16[16,80,384]{2,1,0:T(8,128)(2,1)S(1)}, u32[]{:S(2)}, u32[]{:S(2)}) async-start(bf16[16,80,384]{2,1,0:T(8,128)(2,1)} %get-tuple-element.174), calls=%async_computation | async-start | bytes 1966080 | tf_op jit(solution)/shard_map/all_to_all | solution.py:636
  203.0 48.7 %collective-permute-start.51 = (bf16[4,64,1728]{2,1,0:T(8,128)(2,1)}, bf16[4,64,1728]{2,1,0:T(8,128)(2,1)}, u32[]{:S(2)}, u32[]{:S(2)}) collective-permute-start(bf16[4,64,1728]{2,1,0:T(8,128)(2,1)} %get-tuple-element.179), channel_id=1, source_target_pairs={{0,16},{1,17},{16,0},{17,1},{2,18},{3,19},{18,2},{19,3},{4,20},{5,... | collective-permute-start | bytes 2654216 | tf_op jit(solution)/shard_map/ppermute | solution.py:63
  206.0 48.2 %collective-permute-start.52 = (bf16[4,64,1728]{2,1,0:T(8,128)(2,1)}, bf16[4,64,1728]{2,1,0:T(8,128)(2,1)}, u32[]{:S(2)}, u32[]{:S(2)}) collective-permute-start(bf16[4,64,1728]{2,1,0:T(8,128)(2,1)} %get-tuple-element.180), channel_id=1, source_target_pairs={{0,17},{1,0},{16,1},{17,16},{2,19},{3,2},{18,3},{19,18},{4,21},{5,... | collective-permute-start | bytes 2654216 | tf_op jit(solution)/shard_map/ppermute | solution.py:63
  226.1 28.1 %collective-permute-start.47 = (bf16[2,64,1024]{2,1,0:T(8,128)(2,1)}, bf16[2,64,1024]{2,1,0:T(8,128)(2,1)S(1)}, u32[]{:S(2)}, u32[]{:S(2)}) collective-permute-start(bf16[2,64,1024]{2,1,0:T(8,128)(2,1)} %get-tuple-element.175), channel_id=1, source_target_pairs={{0,2},{2,4},{4,6},{6,0},{1,3},{3,5},{5,7},{7,1},{8,10},{10,12},{12... | collective-permute-start | bytes 786440 | tf_op jit(solution)/shard_map/ppermute | solution.py:49
  226.1 28.1 %collective-permute-start.48 = (bf16[2,64,1024]{2,1,0:T(8,128)(2,1)}, bf16[2,64,1024]{2,1,0:T(8,128)(2,1)S(1)}, u32[]{:S(2)}, u32[]{:S(2)}) collective-permute-start(bf16[2,64,1024]{2,1,0:T(8,128)(2,1)} %get-tuple-element.176), channel_id=1, source_target_pairs={{0,4},{2,6},{4,0},{6,2},{1,5},{3,7},{5,1},{7,3},{8,12},{10,14},{12... | collective-permute-start | bytes 786440 | tf_op jit(solution)/shard_map/ppermute | solution.py:49
  227.6 26.6 %collective-permute-start.49 = (bf16[2,64,1024]{2,1,0:T(8,128)(2,1)}, bf16[2,64,1024]{2,1,0:T(8,128)(2,1)}, u32[]{:S(2)}, u32[]{:S(2)}) collective-permute-start(bf16[2,64,1024]{2,1,0:T(8,128)(2,1)} %get-tuple-element.177), channel_id=1, source_target_pairs={{0,6},{2,0},{4,2},{6,4},{1,7},{3,1},{5,3},{7,5},{8,14},{10,8},{12,... | collective-permute-start | bytes 786440 | tf_op jit(solution)/shard_map/ppermute | solution.py:49
  251.7 15.3 %collective-permute-start.46 = (bf16[2,64,1024]{2,1,0:T(8,128)(2,1)}, bf16[2,64,1024]{2,1,0:T(8,128)(2,1)S(1)}, u32[]{:S(2)}, u32[]{:S(2)}) collective-permute-start(bf16[2,64,1024]{2,1,0:T(8,128)(2,1)} %add_convert_fusion), channel_id=1, source_target_pairs={{0,0},{1,8},{8,1},{9,9},{2,2},{3,10},{10,3},{11,11},{4,4},{5,12},{... | collective-permute-start | bytes 786440 | tf_op jit(solution)/shard_map/ppermute | solution.py:43
  261.0 20.9 %collective-permute-start.55 = (bf16[64,1728]{1,0:T(8,128)(2,1)}, bf16[64,1728]{1,0:T(8,128)(2,1)S(1)}, u32[]{:S(2)}, u32[]{:S(2)}) collective-permute-start(bf16[64,1728]{1,0:T(8,128)(2,1)} %get-tuple-element.190), channel_id=1, source_target_pairs={{0,32},{32,64},{64,96},{96,0},{1,33},{33,65},{65,97},{97,1},{2,34}... | collective-permute-start | bytes 663560 | tf_op jit(solution)/shard_map/ppermute | solution.py:67
  267.0 14.8 %collective-permute-start.56 = (bf16[64,1728]{1,0:T(8,128)(2,1)S(1)}, bf16[64,1728]{1,0:T(8,128)(2,1)S(1)}, u32[]{:S(2)}, u32[]{:S(2)}) collective-permute-start(bf16[64,1728]{1,0:T(8,128)(2,1)S(1)} %copy-done.41), channel_id=1, source_target_pairs={{0,64},{32,96},{64,0},{96,32},{1,65},{33,97},{65,1},{97,33},{2,66}... | collective-permute-start | bytes 663560 | tf_op jit(solution)/shard_map/ppermute | solution.py:67
  270.7 14.8 %collective-permute-start.53 = (bf16[2,64,1024]{2,1,0:T(8,128)(2,1)S(1)}, bf16[2,64,1024]{2,1,0:T(8,128)(2,1)S(1)}, u32[]{:S(2)}, u32[]{:S(2)}) collective-permute-start(bf16[2,64,1024]{2,1,0:T(8,128)(2,1)S(1)} %fusion.5), channel_id=1, source_target_pairs={{0,0},{1,8},{8,1},{9,9},{2,2},{3,10},{10,3},{11,11},{4,4},{5,12},{... | collective-permute-start | bytes 786440 | tf_op jit(solution)/shard_map/ppermute | solution.py:43
  (83 other events, 861.7 us)
Sparse Core Ops, SparseCore 0:
  47.0 45.2 all-gather.1

commit v3 on v2

--- a/solution.py
+++ b/solution.py
@@ -57,10 +57,6 @@
                 x = (xh * 2 + a - k) % 4
                 perm.append((xh * 4 + a * 2 + b, (x // 2) * 4 + b * 2 + x % 2))
     return lax.ppermute(value, ("xh", "core", "xl"), perm)
-
-
-def to_x(value, k):
-    return lax.ppermute(value, ("xh", "xl"), [(x, (x + k) % 4) for x in range(4)])
 
 
 def from_y(value, k):
@@ -358,51 +354,27 @@
     )(second, w_ffn, *cotangent)
 
 
-def weights_kernel(at_ref, second_ref, up_ref, low_ref, inner_ref, *refs):
-    out_refs, total = refs[:4], refs[4]
+def weights_kernel(second_ref, up_ref, low_ref, inner_ref, grad_ref):
     grad = product_tn(second_ref[...], low_ref[...])
-    total[:, :512] = grad[:, :512].astype(bf16)
-    total[:, 512:1152] = pltpu.roll(grad[:, 512:], 64, 1).astype(bf16)
-    total[:, 1152:] = product_tn(up_ref[...], inner_ref[...]).astype(bf16)
-    for k, ref in enumerate(out_refs):
-        row = pl.multiple_of(lax.rem(at_ref[1] + k, 4) * 64, 64)
-        ref[0] = total[pl.ds(row, 64), :]
-
-
-def weights_back(at, second, upstream, low, inner):
+    grad_ref[:, :512] = grad[:, :512].astype(bf16)
+    grad_ref[:, 512:1152] = pltpu.roll(grad[:, 512:], 64, 1).astype(bf16)
+    grad_ref[:, 1152:] = product_tn(up_ref[...], inner_ref[...]).astype(bf16)
+
+
+def weights_back(second, upstream, low, inner):
     count, width = second.shape
-    whole = lambda a: pl.BlockSpec(a.shape, lambda b, at: (0,) * a.ndim)
-    columns = pl.BlockSpec((count, 256), lambda b, at: (0, lax.rem(at[0] + b, 4)))
+    whole = lambda a: pl.BlockSpec(a.shape, lambda b: (0,) * a.ndim)
+    columns = pl.BlockSpec((count, 256), lambda b: (0, b))
     return pl.pallas_call(
         weights_kernel,
-        grid_spec=pltpu.PrefetchScalarGridSpec(
-            num_scalar_prefetch=1,
-            grid=(4,),
-            in_specs=[columns, columns, whole(low), whole(inner)],
-            out_specs=[pl.BlockSpec((1, 64, 1728), lambda b, at: (b, 0, 0))] * 4,
-            scratch_shapes=[pltpu.VMEM((256, 1728), bf16)],
-        ),
-        out_shape=[jax.ShapeDtypeStruct((4, 64, 1728), bf16)] * 4,
+        grid=(width // 256,),
+        in_specs=[columns, columns, whole(low), whole(inner)],
+        out_specs=pl.BlockSpec((256, 1728), lambda b: (b, 0)),
+        out_shape=jax.ShapeDtypeStruct((width, 1728), bf16),
         compiler_params=pltpu.CompilerParams(vmem_limit_bytes=VMEM),
         cost_estimate=pl.CostEstimate(flops=4 * 10**9, bytes_accessed=10**7, transcendentals=0),
         name="weights_back",
-    )(at, second, upstream, low, inner)
-
-
-def rows_kernel(*refs):
-    for k, out_ref in enumerate(refs[4:]):
-        value = sum(ref[k].astype(f32) for ref in refs[:4])
-        out_ref[...] = value.astype(out_ref.dtype)
-
-
-def sum_rows(values):
-    shape = values[0].shape[1:]
-    return pl.pallas_call(
-        rows_kernel,
-        out_shape=[jax.ShapeDtypeStruct(shape, f32)] + [jax.ShapeDtypeStruct(shape, bf16)] * 3,
-        compiler_params=pltpu.CompilerParams(vmem_limit_bytes=VMEM),
-        name="sum_rows",
-    )(*values)
+    )(second, upstream, low, inner)
 
 
 def back_kernel(*refs):
@@ -525,22 +497,27 @@
     )
 
 
-def split_kernel(own_ref, got_ref, *refs):
-    for k, ref in enumerate(refs):
-        rows = slice(k * 64, k * 64 + 64)
-        value = own_ref[:, rows].astype(f32) + got_ref[:, rows].astype(f32)
-        ref[...] = value.astype(ref.dtype)
-
-
-def split(own, got):
+def split_kernel(*refs):
+    count = len(refs) // 2 - 2
+    for i in range(count):
+        own_ref, got_ref = refs[2 * i], refs[2 * i + 1]
+        micro = own_ref.shape[0]
+        for k, ref in enumerate(refs[-4:]):
+            rows = slice(k * 64, k * 64 + 64)
+            value = own_ref[:, rows].astype(f32) + got_ref[:, rows].astype(f32)
+            ref[i * micro : (i + 1) * micro] = value.astype(ref.dtype)
+
+
+def split(own, other, *more):
     micro, _, width = own.shape
-    out = lambda kind: jax.ShapeDtypeStruct((micro, 64, width), kind)
+    values = (own, other_core(other)) + more
+    out = lambda kind: jax.ShapeDtypeStruct((len(values) // 2 * micro, 64, width), kind)
     return pl.pallas_call(
         split_kernel,
         out_shape=[out(f32), out(bf16), out(bf16), out(bf16)],
         compiler_params=pltpu.CompilerParams(vmem_limit_bytes=VMEM),
         name="split",
-    )(own, got)
+    )(*values)
 
 
 def local(
@@ -595,8 +572,9 @@
     bias = jnp.where(allowed, 0.0, -1e30).astype(bf16)
     qk_gain = jnp.stack([jnp.tile(query_gain, 2), jnp.tile(key_gain, 2)])
 
-    w_ffn, *pieces = tie(w_ffn, *w_att, *x_pieces)
-    w_att, x_pieces = pieces[:4], pieces[4:]
+    w_ffn, *pieces = tie(w_ffn, *w_att, *x_pieces, cosine, sine, bias, qk_gain, at)
+    w_att, x_pieces = pieces[:4], pieces[4:8]
+    cosine, sine, bias, qk_gain, at = pieces[8:]
     w_ffn = lax.all_gather(w_ffn, plane, axis=0, tiled=True)
     w_out_chain = from_chain(jnp.concatenate([w[:, nq + 2 * nk :] for w in w_att], axis=0))
     x_chain, x_other = gather_chains(x_pieces)
@@ -611,42 +589,33 @@
     inner, gu_low, grad_own, grad_other, upstream, down_own, down_other = feed(
         second, w_ffn, cotangent_all
     )
-    parts = split(grad_own, other_core(grad_other))
+    down_got = other_core(down_other)
+    parts = split(grad_own, grad_other)
     got = [from_z(parts[k], -k) for k in (1, 2, 3)]
-    grad_ffn = weights_back(at, second, upstream, gu_low, inner)
-    *grad_ffn, got_1, got_2, got_3 = tie(*grad_ffn, *got)
-    got = [got_1, got_2, got_3]
-    grad_ffn_got = [to_x(grad_ffn[k], k) for k in (1, 2, 3)]
+    grad_ffn = weights_back(second, upstream, gu_low, inner)
+    grad_ffn, *got = tie(grad_ffn, *got)
+    grad_ffn = lax.all_to_all(grad_ffn.reshape(16, width // 16, -1), plane, 0, 0)
     grad_second = parts[0] + sum(piece.astype(f32) for piece in got)
     state_own = state.reshape(micro, 2, own, width)[:, 0]
     _, norm_pull = jax.vjp(rms_rows, state_own, ffn_gain)
     grad_state_norm, grad_ffn_gain = norm_pull(grad_second)
     grad_state = (cotangent_own.astype(f32) + grad_state_norm).astype(bf16)
-    down = split(down_own, other_core(down_other))
-    state_pieces = from_chain(grad_state)
-    *state_pieces, down_first, down_low = tie(*state_pieces, *down[:2])
-    down = [down_first, down_low] + list(down[2:])
-    down_got = [from_z(down[k], -k) for k in (1, 2, 3)]
-    state_pieces += [other_core(piece) for piece in state_pieces]
+    state_pieces = gather(grad_state)
 
     grad_own, grad_other, grad_att = back(
         *(state_pieces, normed, w_abs, raw, query, keys, values, stat, mixed, qk_gain),
         *(cosine, sine, bias, norm_gain.reshape(1, width), grad_ffn_gain.reshape(1, width)),
     )
     grad_att = lax.all_to_all(grad_att, plane, 0, 0)
-    grad_got, *down_got = tie(other_core(grad_other), *down_got)
-    output = state_own + down[0] + sum(piece.astype(f32) for piece in down_got)
-    output = swap(output.astype(bf16))
-    parts = split(grad_own, grad_got)
+    parts = split(grad_own, grad_other, down_own, down_got)
     got = [from_z(parts[k], -k) for k in (1, 2, 3)]
-    grad_att, got[0], got[1], got[2], *grad_ffn_got = tie(grad_att, *got, *grad_ffn_got)
-    grad_ffn = sum_rows([grad_ffn[0]] + grad_ffn_got)
-    grad_ffn_got = [from_y(grad_ffn[k], -k) for k in (1, 2, 3)]
-    grad_ffn = grad_ffn[0] + sum(piece.astype(f32) for piece in grad_ffn_got)
-    grad_normed = parts[0] + sum(piece.astype(f32) for piece in got)
+    grad_att, grad_ffn, *got = tie(grad_att, grad_ffn, *got)
+    total = parts[0] + sum(piece.astype(f32) for piece in got)
     _, first_pull = jax.vjp(rms_rows, x_own.astype(f32), norm_gain)
-    grad_resid_norm, _ = first_pull(grad_normed)
-    input_grad = swap((grad_state.astype(f32) + grad_resid_norm).astype(bf16))
+    grad_resid_norm, _ = first_pull(total[:micro])
+    input_grad = grad_state.astype(f32) + grad_resid_norm
+    results = swap(jnp.concatenate([state_own + total[micro:], input_grad]).astype(bf16))
+    grad_ffn = jnp.sum(grad_ffn.astype(f32), axis=0)
     grad_att = jnp.sum(grad_att.astype(f32), axis=0)
     gains = group_sum(grad_att[64:70].reshape(-1))
     grad_att = swap(grad_att[:64])
@@ -654,8 +623,8 @@
     both = nq + nk
     q_gains = gains[2 * width :]
     return (
-        output,
-        input_grad,
+        results[:micro],
+        results[micro:],
         grad_att[:, :nq],
         grad_att[:, nq:both],
         grad_att[:, both : both + nk],

time: 303 us -> 304 us (level); the launches traced: 299 us -> 303 us
  blocking collectives: 0 us -> 19.8 us
  starting transfers between devices: 98.5 us -> 79.8 us
  waiting for transfers between devices: 86.5 us -> 95.9 us
  Pallas kernels: 70.5 us -> 65.1 us
    ppermute x3 -> x0, waiting for transfers between devices: 21.5 us -> none  [to_x(): lax.ppermute(value, ('xh', 'xl'), [(x, (x + k) % 4) for x in range(4)])]
    all_to_all x0 -> x1, blocking collectives: none -> 19.8 us  [local(): grad_att = lax.all_to_all(grad_att, plane, 0, 0)]
    all_to_all x1, waiting for transfers between devices: 0.01 us -> 16.2 us  [local(): lax.all_to_all(grad_ffn.reshape(16, width // 16, -1), plane, 0, 0)]
    ppermute x27 -> x24, waiting for transfers between devices: 41.7 us -> 54 us  [from_z(): return lax.ppermute(value, 'z', [(z, (z - k) % 4) for z in range(4)])]
    ppermute x15, starting transfers between devices: 16.7 us -> 8.7 us  [other_core(): return lax.ppermute(value, 'core', CORE)]
    ppermute x6 -> x3, starting transfers between devices: 8.76 us -> 3.17 us  [from_y(): return lax.ppermute(value, 'y', [(y, (y - k) % 4) for y in range(4)])]
    ppermute x3 -> x0, starting transfers between devices: 5.19 us -> none  [to_x(): lax.ppermute(value, ('xh', 'xl'), [(x, (x + k) % 4) for x in range(4)])]
    ppermute x15, waiting for transfers between devices: 5.78 us -> 9.99 us  [other_core(): return lax.ppermute(value, 'core', CORE)]
  transfers between devices with their start and end apart: 65 -> 55, of which waited for: 26 -> 26; matrix products, arithmetic and copies ran while one was open for 7% -> 7% of each run, Pallas kernels for 14% -> 11%
where the time goes in v3:
time: 304 us; the launch traced here: 303 us
  waiting for transfers between devices  95.9 us (32%)
  starting transfers between devices  79.8 us (26%)
  Pallas kernels  65.1 us (21%)
  blocking collectives  19.8 us (7%)
  other arithmetic  15.8 us (5%)
  between operations  14.7 us (5%)
  local copies, waits for them, and re-layouts  12 us (4%)
    ppermute x24, waiting for transfers between devices, from_z(): return lax.ppermute(value, 'z', [(z, (z - k) % 4) for z in range(4)])  54 us
    ppermute x24, starting transfers between devices, from_z(): return lax.ppermute(value, 'z', [(z, (z - k) % 4) for z in range(4)])  34.1 us
    all_to_all x1, blocking collectives, local(): grad_att = lax.all_to_all(grad_att, plane, 0, 0)  19.8 us
    ppermute x7, starting transfers between devices, swap(): lax.ppermute(value, ('core', 'xl'), [(a * 2 + b, b * 2 + a) for a in rang...  19.6 us
    all_to_all x1, waiting for transfers between devices, local(): lax.all_to_all(grad_ffn.reshape(16, width // 16, -1), plane, 0, 0)  16.2 us
    pallas_call x1, Pallas kernels, feed(): pl.pallas_call(feed_kernel, grid=(steps,), in_specs=[rows(width), whole(w...  15.4 us
    pallas_call x1, Pallas kernels, back(): pl.pallas_call(back_kernel, grid=(micro,), in_specs=[part(p) for p in sta...  14.7 us
    pallas_call x1, Pallas kernels, attend(): pl.pallas_call(attend_kernel, grid_spec=pltpu.PrefetchScalarGridSpec(num_...  11 us
  transfers between devices with their start and end apart: 55, of which 26 were waited for; matrix products, arithmetic and copies ran while one was open for 7% of the time, Pallas kernels for 11%

profile of v3, /device:TPU:1, one launch (start us, length us, event | category | flops | bytes accessed | tf_op | source)
XLA Modules:
  0.0 303.1 jit_solution(15919349676926890308)
XLA Ops:
  8.1 4.5 %collective-permute-start.1 = (bf16[64,384]{1,0:T(8,128)(2,1)S(1)}, bf16[64,384]{1,0:T(8,128)(2,1)S(1)}, u32[]{:S(2)}, u32[]{:S(2)}) collective-permute-start(bf16[64,384]{1,0:T(8,128)(2,1)S(1)} %pad_maximum_fusion.6), channel_id=1, source_target_pairs={{0,0},{1,8},{8,1},{9,9},{16,16},{17,24},{24,17},{25,25},{2,2},{3,1... | collective-permute-start | bytes 147464 | tf_op jit(solution)/shard_map/ppermute | solution.py:59
  23.9 3.6 %collective-permute-start.6 = (s32[2,512]{1,0:T(2,128)}, s32[2,512]{1,0:T(2,128)S(1)}, u32[]{:S(2)}, u32[]{:S(2)}) collective-permute-start(s32[2,512]{1,0:T(2,128)} %param.15), channel_id=1, source_target_pairs={{0,0},{1,8},{8,1},{9,9},{2,2},{3,10},{10,3},{11,11},{4,4},{5,12},{... | collective-permute-start | bytes 12296 | tf_op jit(solution)/shard_map/ppermute | solution.py:43
  30.6 3.8 %collective-permute-start.10 = (bf16[2,64,1024]{2,1,0:T(8,128)(2,1)S(1)}, bf16[2,64,1024]{2,1,0:T(8,128)(2,1)S(1)}, u32[]{:S(2)}, u32[]{:S(2)}) collective-permute-start(bf16[2,64,1024]{2,1,0:T(8,128)(2,1)S(1)} %collective-permute-done.5), channel_id=1, source_target_pairs={{0,6},{2,0},{4,2},{6,4},{1,7},{3,1},{5,3},{7,5},{8,14},{10,8},{12,... | collective-permute-start | bytes 786440 | tf_op jit(solution)/shard_map/ppermute | solution.py:49
  40.2 3.5 %collective-permute-done.7.refs_3_ = bf16[256,384]{1,0:T(8,128)(2,1)S(1)} collective-permute-done((bf16[256,384]{1,0:T(8,128)(2,1)S(1)}, bf16[256,384]{1,0:T(8,128)(2,1)S(1)}, u32[]{:S(2)}, u32[]{:S(2)}) %collective-permute-start.7) | collective-permute-done | bytes 196640 | tf_op jit(solution)/shard_map/ppermute | solution.py:63
  50.3 4.0 %collective-permute-start.17 = (bf16[2,64,1024]{2,1,0:T(8,128)(2,1)}, bf16[2,64,1024]{2,1,0:T(8,128)(2,1)S(1)}, u32[]{:S(2)}, u32[]{:S(2)}) collective-permute-start(bf16[2,64,1024]{2,1,0:T(8,128)(2,1)} %param.16), channel_id=1, source_target_pairs={{0,0},{1,8},{8,1},{9,9},{2,2},{3,10},{10,3},{11,11},{4,4},{5,12},{... | collective-permute-start | bytes 786440 | tf_op jit(solution)/shard_map/ppermute | solution.py:43
  54.2 4.3 %collective-permute-done.17 = bf16[2,64,1024]{2,1,0:T(8,128)(2,1)S(1)} collective-permute-done((bf16[2,64,1024]{2,1,0:T(8,128)(2,1)}, bf16[2,64,1024]{2,1,0:T(8,128)(2,1)S(1)}, u32[]{:S(2)}, u32[]{:S(2)}) %collective-permute-start.17) | collective-permute-done | bytes 262176 | tf_op jit(solution)/shard_map/ppermute | solution.py:43
  67.4 6.6 %collective-permute-start.15 = (bf16[1024,128]{1,0:T(8,128)(2,1)S(1)}, bf16[1024,128]{1,0:T(8,128)(2,1)S(1)}, u32[]{:S(2)}, u32[]{:S(2)}) collective-permute-start(bf16[1024,128]{1,0:T(8,128)(2,1)S(1)} %pad_maximum_fusion.4), channel_id=1, source_target_pairs={{0,4},{2,6},{4,0},{6,2},{1,5},{3,7},{5,1},{7,3},{8,12},{10,14},{12... | collective-permute-start | bytes 786440 | tf_op jit(solution)/shard_map/ppermute | solution.py:49
  76.8 11.0 %attend.1 = (bf16[1024,128]{1,0:T(8,128)(2,1)}, bf16[1024,1024]{1,0:T(8,128)(2,1)}, bf16[1024,1024]{1,0:T(8,128)(2,1)}, bf16[1024,384]{1,0:T(8,128)(2,1)}, f32[1...) custom-call(s32[4]{0:T(128)} %pad_add_fusion.at_ref, ...), custom_call_target="tpu_custom_call" | custom-call | flops 12000000000 | bytes 10000000 | tf_op jit(solution)/shard_map/attend/pallas_call | solution.py:186
  92.6 4.3 %collective-permute-done.21.refs_1_ = bf16[1024,128]{1,0:T(8,128)(2,1)S(1)} collective-permute-done((bf16[1024,128]{1,0:T(8,128)(2,1)S(1)}, bf16[1024,128]{1,0:T(8,128)(2,1)S(1)}, u32[]{:S(2)}, u32[]{:S(2)}) %collective-permute-start.21) | collective-permute-done | bytes 262176 | tf_op jit(solution)/shard_map/ppermute | solution.py:49
  98.9 6.1 %collective-permute-done.23.refs_3_ = bf16[1024,128]{1,0:T(8,128)(2,1)S(1)} collective-permute-done((bf16[1024,128]{1,0:T(8,128)(2,1)S(1)}, bf16[1024,128]{1,0:T(8,128)(2,1)S(1)}, u32[]{:S(2)}, u32[]{:S(2)}) %collective-permute-start.23) | collective-permute-done | bytes 262176 | tf_op jit(solution)/shard_map/ppermute | solution.py:49
  109.2 8.5 %second_norm.1 = (f32[256,1024]{1,0:T(8,128)}, bf16[1024,1024]{1,0:T(8,128)(2,1)}) custom-call(s32[4]{0:T(128)} %pad_add_fusion.at_ref, bf16[1024,128]{1,0:T(8,128)(2,1)} %get-tuple-element.103.refs_0_.refs_15_, bf16[1024,128]{1,0:T(8,128)(2,1)} %copy-done.23, bf16[1024,128]{1,0:T(8,128)(2,1)} %copy-done.25, bf16[1024,128]{1,0:T(8,128)(2,1)} %copy-done.27, ...), custom_call_target="tpu_custom_call" | custom-call | flops 3000000000 | bytes 10000000 | tf_op jit(solution)/shard_map/second_norm/pallas_call | solution.py:256
  117.8 15.4 %feed.1 = (bf16[1024,576]{1,0:T(8,128)(2,1)}, bf16[1024,1152]{1,0:T(8,128)(2,1)}, bf16[2,256,1024]{2,1,0:T(8,128)(2,1)}, bf16[2,256,1024]{2,1,0:T(8,128)(2,1)}, ...) custom-call(bf16[1024,1024]{1,0:T(8,128)(2,1)} %get-tuple-element.113.second_ref, ...), custom_call_target="tpu_custom_call" | custom-call | flops 8999999488 | bytes 10000000 | tf_op jit(solution)/shard_map/feed/pallas_call | solution.py:341
  143.1 8.9 %weights_back.1 = bf16[1024,1728]{1,0:T(8,128)(2,1)} custom-call(bf16[1024,1024]{1,0:T(8,128)(2,1)} %get-tuple-element.113.second_ref, bf16[1024,1024]{1,0:T(8,128)(2,1)} %get-tuple-element.122.up_ref, bf16[1024,1152]{1,0:T(8,128)(2,1)} %get-tuple-element.123.low_ref, bf16[1024,576]{1,0:T(8,128)(2,1)} %get-tuple-element.124.inner_ref), custom_call_target="tpu_custom_call" | custom-call | flops 4000000000 | bytes 10000000 | tf_op jit(solution)/shard_map/weights_back/pallas_call | solution.py:368
  159.8 10.0 %collective-permute-done.34.refs_1_ = bf16[2,64,1024]{2,1,0:T(8,128)(2,1)S(1)} collective-permute-done((bf16[2,64,1024]{2,1,0:T(8,128)(2,1)S(1)}, bf16[2,64,1024]{2,1,0:T(8,128)(2,1)S(1)}, u32[]{:S(2)}, u32[]{:S(2)}) %collective-permute-start.34) | collective-permute-done | bytes 262176 | tf_op jit(solution)/shard_map/ppermute | solution.py:49
  169.8 4.0 %collective-permute-done.36.refs_3_ = bf16[2,64,1024]{2,1,0:T(8,128)(2,1)S(1)} collective-permute-done((bf16[2,64,1024]{2,1,0:T(8,128)(2,1)S(1)}, bf16[2,64,1024]{2,1,0:T(8,128)(2,1)S(1)}, u32[]{:S(2)}, u32[]{:S(2)}) %collective-permute-start.36) | collective-permute-done | bytes 262176 | tf_op jit(solution)/shard_map/ppermute | solution.py:49
  177.7 14.7 %back.1 = (bf16[2,256,1024]{2,1,0:T(8,128)(2,1)}, bf16[2,256,1024]{2,1,0:T(8,128)(2,1)}, bf16[16,80,384]{2,1,0:T(8,128)(2,1)}) custom-call(bf16[2,64,1024]{2,1,0:T(8,128)(2,1)} %copy-done.6, bf16[2,64,1024]{2,1,0:T(8,128)(2,1)} %copy-done.22, bf16[2,64,1024]{2,1,0:T(8,128)(2,1)} %copy-done.24, bf16[2,64,1024]{2,1,0:T(8,128)(2,1)} %copy-done.26, ...), custom_call_target="tpu_custom_call" | custom-call | flops 15000000512 | bytes 10000000 | tf_op jit(solution)/shard_map/back/pallas_call | solution.py:471
  192.4 19.8 %all_to_all.10 = bf16[16,80,384]{2,1,0:T(8,128)(2,1)S(1)} all-to-all(bf16[16,80,384]{2,1,0:T(8,128)(2,1)} %get-tuple-element.147), channel_id=1, replica_groups=mesh['y'=4,'xh'=2,'core'=2,'z'=4,'xl'=2] {'y','xh','xl'}, dimensions={0} | all-to-all | bytes 1966080 | tf_op jit(solution)/shard_map/all_to_all | solution.py:609
  212.2 4.5 %all-to-all-start.1 = ((bf16[16,64,1728]{2,1,0:T(8,128)(2,1)}), bf16[16,64,1728]{2,1,0:T(8,128)(2,1)}, u32[]{:S(2)}, u32[]{:S(2)}) async-start(bf16[16,64,1728]{2,1,0:T(8,128)(2,1)} %bitcast.50), calls=%async_computation.1 | async-start | bytes 7340032 | tf_op jit(solution)/shard_map/all_to_all | solution.py:597
  222.7 3.8 %split.3 = (f32[4,64,1024]{2,1,0:T(8,128)}, bf16[4,64,1024]{2,1,0:T(8,128)(2,1)}, bf16[4,64,1024]{2,1,0:T(8,128)(2,1)}, bf16[4,64,1024]{2,1,0:T(8,128)(2,1)}) custom-call(bf16[2,256,1024]{2,1,0:T(8,128)(2,1)} %get-tuple-element.142.refs_0_, bf16[2,256,1024]{2,1,0:T(8,128)(2,1)} %collective-permute-done.41.refs_1_, ...), custom_call_target="tpu_custom_call" | custom-call | tf_op jit(solution)/shard_map/split/pallas_call | solution.py:515
  229.3 12.8 %collective-permute-done.43 = bf16[4,64,1024]{2,1,0:T(8,128)(2,1)} collective-permute-done((bf16[4,64,1024]{2,1,0:T(8,128)(2,1)}, bf16[4,64,1024]{2,1,0:T(8,128)(2,1)}, u32[]{:S(2)}, u32[]{:S(2)}) %collective-permute-start.43) | collective-permute-done | bytes 524320 | tf_op jit(solution)/shard_map/ppermute | solution.py:49
  242.0 9.6 %collective-permute-done.44 = bf16[4,64,1024]{2,1,0:T(8,128)(2,1)} collective-permute-done((bf16[4,64,1024]{2,1,0:T(8,128)(2,1)}, bf16[4,64,1024]{2,1,0:T(8,128)(2,1)}, u32[]{:S(2)}, u32[]{:S(2)}) %collective-permute-start.44) | collective-permute-done | bytes 524320 | tf_op jit(solution)/shard_map/ppermute | solution.py:49
  252.8 16.2 %all-to-all-done.1 = bf16[16,64,1728]{2,1,0:T(8,128)(2,1)} async-done(((bf16[16,64,1728]{2,1,0:T(8,128)(2,1)}), bf16[16,64,1728]{2,1,0:T(8,128)(2,1)}, u32[]{:S(2)}, u32[]{:S(2)}) %all-to-all-start.1) | async-done | bytes 3538976 | tf_op jit(solution)/shard_map/all_to_all | solution.py:597
  281.1 4.2 %collective-permute-start.46 = (bf16[4,64,1024]{2,1,0:T(8,128)(2,1)S(1)}, bf16[4,64,1024]{2,1,0:T(8,128)(2,1)S(1)}, u32[]{:S(2)}, u32[]{:S(2)}) collective-permute-start(bf16[4,64,1024]{2,1,0:T(8,128)(2,1)S(1)} %pad_maximum_fusion.3), channel_id=1, source_target_pairs={{0,0},{1,8},{8,1},{9,9},{2,2},{3,10},{10,3},{11,11},{4,4},{5,12},{... | collective-permute-start | bytes 1572872 | tf_op jit(solution)/shard_map/ppermute | solution.py:43
  288.5 4.7 %collective-permute-done.47 = f32[64,384]{1,0:T(8,128)S(1)} collective-permute-done((f32[64,384]{1,0:T(8,128)S(1)}, f32[64,384]{1,0:T(8,128)S(1)}, u32[]{:S(2)}, u32[]{:S(2)}) %collective-permute-start.47) | collective-permute-done | bytes 98336 | tf_op jit(solution)/shard_map/ppermute | solution.py:43
  (231 shorter events, 99.4 us)
Async XLA Ops:
  7.2 110.6 %all-gather.2.cloned.1.call-start = ((), (), s32[]{:S(2)}) async-start(), calls=%async_computation.2 | async-start | bytes 3899392 | tf_op jit(solution)/shard_map/all_gather | solution.py:578
  8.1 15.8 %collective-permute-start.1 = (bf16[64,384]{1,0:T(8,128)(2,1)S(1)}, bf16[64,384]{1,0:T(8,128)(2,1)S(1)}, u32[]{:S(2)}, u32[]{:S(2)}) collective-permute-start(bf16[64,384]{1,0:T(8,128)(2,1)S(1)} %pad_maximum_fusion.6), channel_id=1, source_target_pairs={{0,0},{1,8},{8,1},{9,9},{16,16},{17,24},{24,17},{25,25},{2,2},{3,1... | collective-permute-start | bytes 147464 | tf_op jit(solution)/shard_map/ppermute | solution.py:59
  12.6 14.9 %collective-permute-start.2 = (bf16[64,384]{1,0:T(8,128)(2,1)S(1)}, bf16[64,384]{1,0:T(8,128)(2,1)S(1)}, u32[]{:S(2)}, u32[]{:S(2)}) collective-permute-start(bf16[64,384]{1,0:T(8,128)(2,1)S(1)} %pad_maximum_fusion.6), channel_id=1, source_target_pairs={{0,17},{1,25},{8,0},{9,8},{16,1},{17,9},{24,16},{25,24},{2,19},{3,... | collective-permute-start | bytes 147464 | tf_op jit(solution)/shard_map/ppermute | solution.py:59
  12.7 16.8 %collective-permute-start.3 = (bf16[64,384]{1,0:T(8,128)(2,1)S(1)}, bf16[64,384]{1,0:T(8,128)(2,1)S(1)}, u32[]{:S(2)}, u32[]{:S(2)}) collective-permute-start(bf16[64,384]{1,0:T(8,128)(2,1)S(1)} %pad_maximum_fusion.6), channel_id=1, source_target_pairs={{0,16},{1,24},{8,17},{9,25},{16,0},{17,8},{24,1},{25,9},{2,18},{3,... | collective-permute-start | bytes 147464 | tf_op jit(solution)/shard_map/ppermute | solution.py:59
  14.3 15.2 %collective-permute-start.4 = (bf16[64,384]{1,0:T(8,128)(2,1)S(1)}, bf16[64,384]{1,0:T(8,128)(2,1)S(1)}, u32[]{:S(2)}, u32[]{:S(2)}) collective-permute-start(bf16[64,384]{1,0:T(8,128)(2,1)S(1)} %pad_maximum_fusion.6), channel_id=1, source_target_pairs={{0,1},{1,9},{8,16},{9,24},{16,17},{17,25},{24,0},{25,8},{2,3},{3,1... | collective-permute-start | bytes 147464 | tf_op jit(solution)/shard_map/ppermute | solution.py:59
  30.6 19.3 %collective-permute-start.10 = (bf16[2,64,1024]{2,1,0:T(8,128)(2,1)S(1)}, bf16[2,64,1024]{2,1,0:T(8,128)(2,1)S(1)}, u32[]{:S(2)}, u32[]{:S(2)}) collective-permute-start(bf16[2,64,1024]{2,1,0:T(8,128)(2,1)S(1)} %collective-permute-done.5), channel_id=1, source_target_pairs={{0,6},{2,0},{4,2},{6,4},{1,7},{3,1},{5,3},{7,5},{8,14},{10,8},{12,... | collective-permute-start | bytes 786440 | tf_op jit(solution)/shard_map/ppermute | solution.py:49
  34.5 15.5 %collective-permute-start.11 = (bf16[2,64,1024]{2,1,0:T(8,128)(2,1)S(1)}, bf16[2,64,1024]{2,1,0:T(8,128)(2,1)S(1)}, u32[]{:S(2)}, u32[]{:S(2)}) collective-permute-start(bf16[2,64,1024]{2,1,0:T(8,128)(2,1)S(1)} %collective-permute-done.5), channel_id=1, source_target_pairs={{0,4},{2,6},{4,0},{6,2},{1,5},{3,7},{5,1},{7,3},{8,12},{10,14},{12... | collective-permute-start | bytes 786440 | tf_op jit(solution)/shard_map/ppermute | solution.py:49
  34.5 15.5 %collective-permute-start.12 = (bf16[2,64,1024]{2,1,0:T(8,128)(2,1)S(1)}, bf16[2,64,1024]{2,1,0:T(8,128)(2,1)S(1)}, u32[]{:S(2)}, u32[]{:S(2)}) collective-permute-start(bf16[2,64,1024]{2,1,0:T(8,128)(2,1)S(1)} %collective-permute-done.5), channel_id=1, source_target_pairs={{0,2},{2,4},{4,6},{6,0},{1,3},{3,5},{5,7},{7,1},{8,10},{10,12},{12... | collective-permute-start | bytes 786440 | tf_op jit(solution)/shard_map/ppermute | solution.py:49
  50.2 23.8 %collective-permute-start.13 = (bf16[4,2,64,1024]{3,2,1,0:T(8,128)(2,1)S(1)}, bf16[4,2,64,1024]{3,2,1,0:T(8,128)(2,1)S(1)}, u32[]{:S(2)}, u32[]{:S(2)}) collective-permute-start(bf16[4,2,64,1024]{3,2,1,0:T(8,128)(2,1)S(1)} %pad_maximum_fusion.refs_0_), channel_id=1, source_target_pairs={{0,8},{8,0},{1,9},{9,1},{2,10},{10,2},{3,11},{11,3},{4,12},{12,4},... | collective-permute-start | bytes 3145736 | tf_op jit(solution)/shard_map/ppermute | solution.py:67
  60.5 27.2 %collective-permute-start.19 = (bf16[2,64,1024]{2,1,0:T(8,128)(2,1)S(1)}, bf16[2,64,1024]{2,1,0:T(8,128)(2,1)S(1)}, u32[]{:S(2)}, u32[]{:S(2)}) collective-permute-start(bf16[2,64,1024]{2,1,0:T(8,128)(2,1)S(1)} %collective-permute-done.17), channel_id=1, source_target_pairs={{0,4},{2,6},{4,0},{6,2},{1,5},{3,7},{5,1},{7,3},{8,12},{10,14},{12... | collective-permute-start | bytes 786440 | tf_op jit(solution)/shard_map/ppermute | solution.py:49
  62.5 25.2 %collective-permute-start.20 = (bf16[2,64,1024]{2,1,0:T(8,128)(2,1)S(1)}, bf16[2,64,1024]{2,1,0:T(8,128)(2,1)S(1)}, u32[]{:S(2)}, u32[]{:S(2)}) collective-permute-start(bf16[2,64,1024]{2,1,0:T(8,128)(2,1)S(1)} %collective-permute-done.17), channel_id=1, source_target_pairs={{0,2},{2,4},{4,6},{6,0},{1,3},{3,5},{5,7},{7,1},{8,10},{10,12},{12... | collective-permute-start | bytes 786440 | tf_op jit(solution)/shard_map/ppermute | solution.py:49
  63.5 24.3 %collective-permute-start.14 = (bf16[1024,128]{1,0:T(8,128)(2,1)S(1)}, bf16[1024,128]{1,0:T(8,128)(2,1)S(1)}, u32[]{:S(2)}, u32[]{:S(2)}) collective-permute-start(bf16[1024,128]{1,0:T(8,128)(2,1)S(1)} %pad_maximum_fusion.4), channel_id=1, source_target_pairs={{0,6},{2,0},{4,2},{6,4},{1,7},{3,1},{5,3},{7,5},{8,14},{10,8},{12,... | collective-permute-start | bytes 786440 | tf_op jit(solution)/shard_map/ppermute | solution.py:49
  67.4 20.4 %collective-permute-start.15 = (bf16[1024,128]{1,0:T(8,128)(2,1)S(1)}, bf16[1024,128]{1,0:T(8,128)(2,1)S(1)}, u32[]{:S(2)}, u32[]{:S(2)}) collective-permute-start(bf16[1024,128]{1,0:T(8,128)(2,1)S(1)} %pad_maximum_fusion.4), channel_id=1, source_target_pairs={{0,4},{2,6},{4,0},{6,2},{1,5},{3,7},{5,1},{7,3},{8,12},{10,14},{12... | collective-permute-start | bytes 786440 | tf_op jit(solution)/shard_map/ppermute | solution.py:49
  87.9 20.2 %collective-permute-start.28 = (bf16[4,1024,128]{2,1,0:T(8,128)(2,1)S(1)}, bf16[4,1024,128]{2,1,0:T(8,128)(2,1)S(1)}, u32[]{:S(2)}, u32[]{:S(2)}) collective-permute-start(bf16[4,1024,128]{2,1,0:T(8,128)(2,1)S(1)} %pad_maximum_fusion.1.refs_8_), channel_id=1, source_target_pairs={{0,8},{8,0},{1,9},{9,1},{2,10},{10,2},{3,11},{11,3},{4,12},{12,4},... | collective-permute-start | bytes 3145736 | tf_op jit(solution)/shard_map/ppermute | solution.py:67
  91.8 26.0 %collective-permute-start.29 = (bf16[4,2,64,1024]{3,2,1,0:T(8,128)(2,1)S(1)}, bf16[4,2,64,1024]{3,2,1,0:T(8,128)(2,1)}, u32[]{:S(2)}, u32[]{:S(2)}) collective-permute-start(bf16[4,2,64,1024]{3,2,1,0:T(8,128)(2,1)S(1)} %pad_maximum_fusion.2.refs_0_), channel_id=1, source_target_pairs={{0,8},{8,0},{1,9},{9,1},{2,10},{10,2},{3,11},{11,3},{4,12},{12,4},... | collective-permute-start | bytes 3145736 | tf_op jit(solution)/shard_map/ppermute | solution.py:67
  139.8 14.6 %collective-permute-start.31 = (bf16[2,64,1024]{2,1,0:T(8,128)(2,1)}, bf16[2,64,1024]{2,1,0:T(8,128)(2,1)S(1)}, u32[]{:S(2)}, u32[]{:S(2)}) collective-permute-start(bf16[2,64,1024]{2,1,0:T(8,128)(2,1)} %get-tuple-element.125), channel_id=1, source_target_pairs={{0,2},{2,4},{4,6},{6,0},{1,3},{3,5},{5,7},{7,1},{8,10},{10,12},{12... | collective-permute-start | bytes 786440 | tf_op jit(solution)/shard_map/ppermute | solution.py:49
  139.8 14.6 %collective-permute-start.32 = (bf16[2,64,1024]{2,1,0:T(8,128)(2,1)}, bf16[2,64,1024]{2,1,0:T(8,128)(2,1)S(1)}, u32[]{:S(2)}, u32[]{:S(2)}) collective-permute-start(bf16[2,64,1024]{2,1,0:T(8,128)(2,1)} %get-tuple-element.126), channel_id=1, source_target_pairs={{0,4},{2,6},{4,0},{6,2},{1,5},{3,7},{5,1},{7,3},{8,12},{10,14},{12... | collective-permute-start | bytes 786440 | tf_op jit(solution)/shard_map/ppermute | solution.py:49
  159.1 14.7 %collective-permute-start.36 = (bf16[2,64,1024]{2,1,0:T(8,128)(2,1)S(1)}, bf16[2,64,1024]{2,1,0:T(8,128)(2,1)S(1)}, u32[]{:S(2)}, u32[]{:S(2)}) collective-permute-start(bf16[2,64,1024]{2,1,0:T(8,128)(2,1)S(1)} %fusion.1.refs_0_), channel_id=1, source_target_pairs={{0,2},{2,4},{4,6},{6,0},{1,3},{3,5},{5,7},{7,1},{8,10},{10,12},{12... | collective-permute-start | bytes 786440 | tf_op jit(solution)/shard_map/ppermute | solution.py:49
  212.2 56.8 %all-to-all-start.1 = ((bf16[16,64,1728]{2,1,0:T(8,128)(2,1)}), bf16[16,64,1728]{2,1,0:T(8,128)(2,1)}, u32[]{:S(2)}, u32[]{:S(2)}) async-start(bf16[16,64,1728]{2,1,0:T(8,128)(2,1)} %bitcast.50), calls=%async_computation.1 | async-start | bytes 7340032 | tf_op jit(solution)/shard_map/all_to_all | solution.py:597
  226.6 15.5 %collective-permute-start.43 = (bf16[4,64,1024]{2,1,0:T(8,128)(2,1)}, bf16[4,64,1024]{2,1,0:T(8,128)(2,1)}, u32[]{:S(2)}, u32[]{:S(2)}) collective-permute-start(bf16[4,64,1024]{2,1,0:T(8,128)(2,1)} %get-tuple-element.149), channel_id=1, source_target_pairs={{0,2},{2,4},{4,6},{6,0},{1,3},{3,5},{5,7},{7,1},{8,10},{10,12},{12... | collective-permute-start | bytes 1572872 | tf_op jit(solution)/shard_map/ppermute | solution.py:49
  226.6 25.1 %collective-permute-start.44 = (bf16[4,64,1024]{2,1,0:T(8,128)(2,1)}, bf16[4,64,1024]{2,1,0:T(8,128)(2,1)}, u32[]{:S(2)}, u32[]{:S(2)}) collective-permute-start(bf16[4,64,1024]{2,1,0:T(8,128)(2,1)} %get-tuple-element.150), channel_id=1, source_target_pairs={{0,4},{2,6},{4,0},{6,2},{1,5},{3,7},{5,1},{7,3},{8,12},{10,14},{12... | collective-permute-start | bytes 1572872 | tf_op jit(solution)/shard_map/ppermute | solution.py:49
  228.4 24.4 %collective-permute-start.45 = (bf16[4,64,1024]{2,1,0:T(8,128)(2,1)}, bf16[4,64,1024]{2,1,0:T(8,128)(2,1)}, u32[]{:S(2)}, u32[]{:S(2)}) collective-permute-start(bf16[4,64,1024]{2,1,0:T(8,128)(2,1)} %get-tuple-element.151), channel_id=1, source_target_pairs={{0,6},{2,0},{4,2},{6,4},{1,7},{3,1},{5,3},{7,5},{8,14},{10,8},{12,... | collective-permute-start | bytes 1572872 | tf_op jit(solution)/shard_map/ppermute | solution.py:49
  275.2 19.3 %collective-permute-start.48 = (bf16[64,1728]{1,0:T(8,128)(2,1)}, bf16[64,1728]{1,0:T(8,128)(2,1)S(1)}, u32[]{:S(2)}, u32[]{:S(2)}) collective-permute-start(bf16[64,1728]{1,0:T(8,128)(2,1)} %reduce_sum.84), channel_id=1, source_target_pairs={{0,0},{1,8},{8,1},{9,9},{2,2},{3,10},{10,3},{11,11},{4,4},{5,12},{... | collective-permute-start | bytes 663560 | tf_op jit(solution)/shard_map/ppermute | solution.py:43
  281.1 14.3 %collective-permute-start.46 = (bf16[4,64,1024]{2,1,0:T(8,128)(2,1)S(1)}, bf16[4,64,1024]{2,1,0:T(8,128)(2,1)S(1)}, u32[]{:S(2)}, u32[]{:S(2)}) collective-permute-start(bf16[4,64,1024]{2,1,0:T(8,128)(2,1)S(1)} %pad_maximum_fusion.3), channel_id=1, source_target_pairs={{0,0},{1,8},{8,1},{9,9},{2,2},{3,10},{10,3},{11,11},{4,4},{5,12},{... | collective-permute-start | bytes 1572872 | tf_op jit(solution)/shard_map/ppermute | solution.py:43
  (67 other events, 560.5 us)
Sparse Core Ops, SparseCore 0:
  50.1 47.0 all-gather.1

commit v4 on v3

--- a/solution.py
+++ b/solution.py
@@ -489,7 +489,7 @@
             out((16, 80, 384), bf16),
         ],
         compiler_params=pltpu.CompilerParams(vmem_limit_bytes=VMEM),
-        cost_estimate=pl.CostEstimate(flops=15 * 10**9, bytes_accessed=10**7, transcendentals=10**6),
+        cost_estimate=pl.CostEstimate(flops=10**6, bytes_accessed=10**4, transcendentals=0),
         name="back",
     )(
         *(*state, normed, w_att, raw, query, keys, values, stat, mixed),
@@ -594,7 +594,7 @@
     got = [from_z(parts[k], -k) for k in (1, 2, 3)]
     grad_ffn = weights_back(second, upstream, gu_low, inner)
     grad_ffn, *got = tie(grad_ffn, *got)
-    grad_ffn = lax.all_to_all(grad_ffn.reshape(16, width // 16, -1), plane, 0, 0)
+    grad_ffn = lax.psum_scatter(grad_ffn, plane, scatter_dimension=0, tiled=True)
     grad_second = parts[0] + sum(piece.astype(f32) for piece in got)
     state_own = state.reshape(micro, 2, own, width)[:, 0]
     _, norm_pull = jax.vjp(rms_rows, state_own, ffn_gain)
@@ -615,7 +615,6 @@
     grad_resid_norm, _ = first_pull(total[:micro])
     input_grad = grad_state.astype(f32) + grad_resid_norm
     results = swap(jnp.concatenate([state_own + total[micro:], input_grad]).astype(bf16))
-    grad_ffn = jnp.sum(grad_ffn.astype(f32), axis=0)
     grad_att = jnp.sum(grad_att.astype(f32), axis=0)
     gains = group_sum(grad_att[64:70].reshape(-1))
     grad_att = swap(grad_att[:64])

time: 304 us -> 270 us (0.89)
  blocking collectives: 19.8 us -> 0 us
  waiting for transfers between devices: 95.9 us -> 87.8 us
  starting transfers between devices: 79.8 us -> 75.6 us
    all_to_all x1 -> x0, blocking collectives: 19.8 us -> none  [local(): grad_att = lax.all_to_all(grad_att, plane, 0, 0)]
    reduce_scatter x0 -> x1, waiting for transfers between devices: none -> 7.33 us  [local(): lax.psum_scatter(grad_ffn, plane, scatter_dimension=0, tiled=True)]
    all_to_all x1, waiting for transfers between devices: 16.2 us -> 9.44 us  [local(): grad_att = lax.all_to_all(grad_att, plane, 0, 0)]
    ppermute x24, waiting for transfers between devices: 54 us -> 49.3 us  [from_z(): return lax.ppermute(value, 'z', [(z, (z - k) % 4) for z in range(4)])]
    ppermute x15, waiting for transfers between devices: 9.99 us -> 5.95 us  [other_core(): return lax.ppermute(value, 'core', CORE)]
    reduce_sum x1 -> x0, other arithmetic: 3.31 us -> none  [local(): grad_ffn = jnp.sum(grad_ffn.astype(f32), axis=0)]
  transfers between devices with their start and end apart: 55 -> 56, of which waited for: 26 -> 25; matrix products, arithmetic and copies ran while one was open for 7% -> 7% of each run, Pallas kernels for 11% -> 17%
where the time goes in v4:
time: 270 us; the launch traced here: 269 us
  waiting for transfers between devices  87.8 us (33%)
  starting transfers between devices  75.6 us (28%)
  Pallas kernels  65.1 us (24%)
  between operations  14.8 us (5%)
  other arithmetic  13.4 us (5%)
  local copies, waits for them, and re-layouts  12.4 us (5%)
    ppermute x24, waiting for transfers between devices, from_z(): return lax.ppermute(value, 'z', [(z, (z - k) % 4) for z in range(4)])  49.3 us
    ppermute x24, starting transfers between devices, from_z(): return lax.ppermute(value, 'z', [(z, (z - k) % 4) for z in range(4)])  31.2 us
    ppermute x7, starting transfers between devices, swap(): lax.ppermute(value, ('core', 'xl'), [(a * 2 + b, b * 2 + a) for a in rang...  19.8 us
    pallas_call x1, Pallas kernels, feed(): pl.pallas_call(feed_kernel, grid=(steps,), in_specs=[rows(width), whole(w...  15.4 us
    pallas_call x1, Pallas kernels, back(): pl.pallas_call(back_kernel, grid=(micro,), in_specs=[part(p) for p in sta...  14.8 us
    pallas_call x1, Pallas kernels, attend(): pl.pallas_call(attend_kernel, grid_spec=pltpu.PrefetchScalarGridSpec(num_...  11.1 us
    ppermute x4, starting transfers between devices, swap_from_x(): return lax.ppermute(value, ('xh', 'core', 'xl'), perm)  9.65 us
    all_to_all x1, waiting for transfers between devices, local(): grad_att = lax.all_to_all(grad_att, plane, 0, 0)  9.44 us
  transfers between devices with their start and end apart: 56, of which 25 were waited for; matrix products, arithmetic and copies ran while one was open for 7% of the time, Pallas kernels for 17%

profile of v4, /device:TPU:1, one launch (start us, length us, event | category | flops | bytes accessed | tf_op | source)
XLA Modules:
  0.0 269.1 jit_solution(4912584114174892382)
XLA Ops:
  8.1 4.5 %collective-permute-start.1 = (bf16[64,384]{1,0:T(8,128)(2,1)S(1)}, bf16[64,384]{1,0:T(8,128)(2,1)S(1)}, u32[]{:S(2)}, u32[]{:S(2)}) collective-permute-start(bf16[64,384]{1,0:T(8,128)(2,1)S(1)} %pad_maximum_fusion.6), channel_id=1, source_target_pairs={{0,0},{1,8},{8,1},{9,9},{16,16},{17,24},{24,17},{25,25},{2,2},{3,1... | collective-permute-start | bytes 147464 | tf_op jit(solution)/shard_map/ppermute | solution.py:59
  14.3 3.4 %collective-permute-start.4 = (bf16[64,384]{1,0:T(8,128)(2,1)S(1)}, bf16[64,384]{1,0:T(8,128)(2,1)S(1)}, u32[]{:S(2)}, u32[]{:S(2)}) collective-permute-start(bf16[64,384]{1,0:T(8,128)(2,1)S(1)} %pad_maximum_fusion.6), channel_id=1, source_target_pairs={{0,1},{1,9},{8,16},{9,24},{16,17},{17,25},{24,0},{25,8},{2,3},{3,1... | collective-permute-start | bytes 147464 | tf_op jit(solution)/shard_map/ppermute | solution.py:59
  23.9 3.6 %collective-permute-start.6 = (s32[2,512]{1,0:T(2,128)}, s32[2,512]{1,0:T(2,128)S(1)}, u32[]{:S(2)}, u32[]{:S(2)}) collective-permute-start(s32[2,512]{1,0:T(2,128)} %param.15), channel_id=1, source_target_pairs={{0,0},{1,8},{8,1},{9,9},{2,2},{3,10},{10,3},{11,11},{4,4},{5,12},{... | collective-permute-start | bytes 12296 | tf_op jit(solution)/shard_map/ppermute | solution.py:43
  30.6 3.8 %collective-permute-start.10 = (bf16[2,64,1024]{2,1,0:T(8,128)(2,1)S(1)}, bf16[2,64,1024]{2,1,0:T(8,128)(2,1)S(1)}, u32[]{:S(2)}, u32[]{:S(2)}) collective-permute-start(bf16[2,64,1024]{2,1,0:T(8,128)(2,1)S(1)} %collective-permute-done.5), channel_id=1, source_target_pairs={{0,6},{2,0},{4,2},{6,4},{1,7},{3,1},{5,3},{7,5},{8,14},{10,8},{12,... | collective-permute-start | bytes 786440 | tf_op jit(solution)/shard_map/ppermute | solution.py:49
  40.3 3.5 %collective-permute-done.7.refs_3_ = bf16[256,384]{1,0:T(8,128)(2,1)S(1)} collective-permute-done((bf16[256,384]{1,0:T(8,128)(2,1)S(1)}, bf16[256,384]{1,0:T(8,128)(2,1)S(1)}, u32[]{:S(2)}, u32[]{:S(2)}) %collective-permute-start.7) | collective-permute-done | bytes 196640 | tf_op jit(solution)/shard_map/ppermute | solution.py:63
  50.3 4.0 %collective-permute-start.17 = (bf16[2,64,1024]{2,1,0:T(8,128)(2,1)S(1)}, bf16[2,64,1024]{2,1,0:T(8,128)(2,1)S(1)}, u32[]{:S(2)}, u32[]{:S(2)}) collective-permute-start(bf16[2,64,1024]{2,1,0:T(8,128)(2,1)S(1)} %copy-done.26), channel_id=1, source_target_pairs={{0,0},{1,8},{8,1},{9,9},{2,2},{3,10},{10,3},{11,11},{4,4},{5,12},{... | collective-permute-start | bytes 786440 | tf_op jit(solution)/shard_map/ppermute | solution.py:43
  54.3 4.3 %collective-permute-done.17 = bf16[2,64,1024]{2,1,0:T(8,128)(2,1)S(1)} collective-permute-done((bf16[2,64,1024]{2,1,0:T(8,128)(2,1)S(1)}, bf16[2,64,1024]{2,1,0:T(8,128)(2,1)S(1)}, u32[]{:S(2)}, u32[]{:S(2)}) %collective-permute-start.17) | collective-permute-done | bytes 262176 | tf_op jit(solution)/shard_map/ppermute | solution.py:43
  66.1 6.0 %collective-permute-done.18 = bf16[2,64,1024]{2,1,0:T(8,128)(2,1)S(1)} collective-permute-done((bf16[2,64,1024]{2,1,0:T(8,128)(2,1)S(1)}, bf16[2,64,1024]{2,1,0:T(8,128)(2,1)S(1)}, u32[]{:S(2)}, u32[]{:S(2)}) %collective-permute-start.18) | collective-permute-done | bytes 262176 | tf_op jit(solution)/shard_map/ppermute | solution.py:49
  76.9 11.1 %attend.1 = (bf16[1024,128]{1,0:T(8,128)(2,1)}, bf16[1024,1024]{1,0:T(8,128)(2,1)}, bf16[1024,1024]{1,0:T(8,128)(2,1)}, bf16[1024,384]{1,0:T(8,128)(2,1)}, f32[1...) custom-call(s32[4]{0:T(128)} %pad_add_fusion.at_ref, ...), custom_call_target="tpu_custom_call" | custom-call | flops 12000000000 | bytes 10000000 | tf_op jit(solution)/shard_map/attend/pallas_call | solution.py:186
  93.0 4.4 %collective-permute-done.21.refs_1_ = bf16[1024,128]{1,0:T(8,128)(2,1)S(1)} collective-permute-done((bf16[1024,128]{1,0:T(8,128)(2,1)S(1)}, bf16[1024,128]{1,0:T(8,128)(2,1)S(1)}, u32[]{:S(2)}, u32[]{:S(2)}) %collective-permute-start.21) | collective-permute-done | bytes 262176 | tf_op jit(solution)/shard_map/ppermute | solution.py:49
  98.7 6.4 %collective-permute-done.23.refs_3_ = bf16[1024,128]{1,0:T(8,128)(2,1)S(1)} collective-permute-done((bf16[1024,128]{1,0:T(8,128)(2,1)S(1)}, bf16[1024,128]{1,0:T(8,128)(2,1)S(1)}, u32[]{:S(2)}, u32[]{:S(2)}) %collective-permute-start.23) | collective-permute-done | bytes 262176 | tf_op jit(solution)/shard_map/ppermute | solution.py:49
  109.3 8.5 %second_norm.1 = (f32[256,1024]{1,0:T(8,128)}, bf16[1024,1024]{1,0:T(8,128)(2,1)}) custom-call(s32[4]{0:T(128)} %pad_add_fusion.at_ref, bf16[1024,128]{1,0:T(8,128)(2,1)} %get-tuple-element.103.refs_0_.refs_15_, bf16[1024,128]{1,0:T(8,128)(2,1)} %copy-done.27, bf16[1024,128]{1,0:T(8,128)(2,1)} %copy-done.28, bf16[1024,128]{1,0:T(8,128)(2,1)} %copy-done.29, ...), custom_call_target="tpu_custom_call" | custom-call | flops 3000000000 | bytes 10000000 | tf_op jit(solution)/shard_map/second_norm/pallas_call | solution.py:256
  117.9 15.4 %feed.1 = (bf16[1024,576]{1,0:T(8,128)(2,1)}, bf16[1024,1152]{1,0:T(8,128)(2,1)}, bf16[2,256,1024]{2,1,0:T(8,128)(2,1)}, bf16[2,256,1024]{2,1,0:T(8,128)(2,1)}, ...) custom-call(bf16[1024,1024]{1,0:T(8,128)(2,1)} %get-tuple-element.113.second_ref, ...), custom_call_target="tpu_custom_call" | custom-call | flops 8999999488 | bytes 10000000 | tf_op jit(solution)/shard_map/feed/pallas_call | solution.py:341
  143.4 8.8 %weights_back.1 = bf16[1024,1728]{1,0:T(8,128)(2,1)} custom-call(bf16[1024,1024]{1,0:T(8,128)(2,1)} %get-tuple-element.113.second_ref, bf16[1024,1024]{1,0:T(8,128)(2,1)} %get-tuple-element.122.up_ref, bf16[1024,1152]{1,0:T(8,128)(2,1)} %get-tuple-element.123.low_ref, bf16[1024,576]{1,0:T(8,128)(2,1)} %get-tuple-element.124.inner_ref), custom_call_target="tpu_custom_call" | custom-call | flops 4000000000 | bytes 10000000 | tf_op jit(solution)/shard_map/weights_back/pallas_call | solution.py:368
  160.0 10.0 %collective-permute-done.34.refs_1_ = bf16[2,64,1024]{2,1,0:T(8,128)(2,1)S(1)} collective-permute-done((bf16[2,64,1024]{2,1,0:T(8,128)(2,1)S(1)}, bf16[2,64,1024]{2,1,0:T(8,128)(2,1)S(1)}, u32[]{:S(2)}, u32[]{:S(2)}) %collective-permute-start.34) | collective-permute-done | bytes 262176 | tf_op jit(solution)/shard_map/ppermute | solution.py:49
  170.0 4.7 %collective-permute-done.36.refs_3_ = bf16[2,64,1024]{2,1,0:T(8,128)(2,1)S(1)} collective-permute-done((bf16[2,64,1024]{2,1,0:T(8,128)(2,1)S(1)}, bf16[2,64,1024]{2,1,0:T(8,128)(2,1)S(1)}, u32[]{:S(2)}, u32[]{:S(2)}) %collective-permute-start.36) | collective-permute-done | bytes 262176 | tf_op jit(solution)/shard_map/ppermute | solution.py:49
  178.5 14.8 %back.1 = (bf16[2,256,1024]{2,1,0:T(8,128)(2,1)}, bf16[2,256,1024]{2,1,0:T(8,128)(2,1)}, bf16[16,80,384]{2,1,0:T(8,128)(2,1)}) custom-call(bf16[2,64,1024]{2,1,0:T(8,128)(2,1)} %copy-done.1, bf16[2,64,1024]{2,1,0:T(8,128)(2,1)} %copy-done.11, bf16[2,64,1024]{2,1,0:T(8,128)(2,1)} %copy-done.12, bf16[2,64,1024]{2,1,0:T(8,128)(2,1)} %copy-done.13, ...), custom_call_target="tpu_custom_call" | custom-call | flops 1000000 | bytes 10000 | tf_op jit(solution)/shard_map/back/pallas_call | solution.py:471
  193.7 4.2 %all-to-all-start = ((bf16[16,80,384]{2,1,0:T(8,128)(2,1)}), bf16[16,80,384]{2,1,0:T(8,128)(2,1)S(1)}, u32[]{:S(2)}, u32[]{:S(2)}) async-start(bf16[16,80,384]{2,1,0:T(8,128)(2,1)} %get-tuple-element.147), calls=%async_computation | async-start | bytes 1966080 | tf_op jit(solution)/shard_map/all_to_all | solution.py:609
  198.9 3.9 %split.3 = (f32[4,64,1024]{2,1,0:T(8,128)}, bf16[4,64,1024]{2,1,0:T(8,128)(2,1)}, bf16[4,64,1024]{2,1,0:T(8,128)(2,1)}, bf16[4,64,1024]{2,1,0:T(8,128)(2,1)}) custom-call(bf16[2,256,1024]{2,1,0:T(8,128)(2,1)} %get-tuple-element.142.refs_0_, bf16[2,256,1024]{2,1,0:T(8,128)(2,1)} %collective-permute-done.41.refs_1_, ...), custom_call_target="tpu_custom_call" | custom-call | tf_op jit(solution)/shard_map/split/pallas_call | solution.py:515
  205.5 9.4 %all-to-all-done = bf16[16,80,384]{2,1,0:T(8,128)(2,1)S(1)} async-done(((bf16[16,80,384]{2,1,0:T(8,128)(2,1)}), bf16[16,80,384]{2,1,0:T(8,128)(2,1)S(1)}, u32[]{:S(2)}, u32[]{:S(2)}) %all-to-all-start) | async-done | bytes 983072 | tf_op jit(solution)/shard_map/all_to_all | solution.py:609
  218.0 9.6 %collective-permute-done.44 = bf16[4,64,1024]{2,1,0:T(8,128)(2,1)S(1)} collective-permute-done((bf16[4,64,1024]{2,1,0:T(8,128)(2,1)}, bf16[4,64,1024]{2,1,0:T(8,128)(2,1)S(1)}, u32[]{:S(2)}, u32[]{:S(2)}) %collective-permute-start.44) | collective-permute-done | bytes 524320 | tf_op jit(solution)/shard_map/ppermute | solution.py:49
  228.9 7.3 %reduce-scatter.2.cloned.1.call-done = bf16[64,1728]{1,0:T(8,128)(2,1)} async-done(((bf16[1024,1728]{1,0:T(8,128)(2,1)}), bf16[64,1728]{1,0:T(8,128)(2,1)}) %reduce-scatter.2.cloned.1.call-update) | async-done | bytes 221200 | tf_op jit(solution)/shard_map/reduce_scatter | solution.py:597
  247.6 3.7 %collective-permute-start.46 = (bf16[4,64,1024]{2,1,0:T(8,128)(2,1)S(1)}, bf16[4,64,1024]{2,1,0:T(8,128)(2,1)S(1)}, u32[]{:S(2)}, u32[]{:S(2)}) collective-permute-start(bf16[4,64,1024]{2,1,0:T(8,128)(2,1)S(1)} %pad_maximum_fusion.3), channel_id=1, source_target_pairs={{0,0},{1,8},{8,1},{9,9},{2,2},{3,10},{10,3},{11,11},{4,4},{5,12},{... | collective-permute-start | bytes 1572872 | tf_op jit(solution)/shard_map/ppermute | solution.py:43
  254.5 4.7 %collective-permute-done.47 = f32[64,384]{1,0:T(8,128)S(1)} collective-permute-done((f32[64,384]{1,0:T(8,128)S(1)}, f32[64,384]{1,0:T(8,128)S(1)}, u32[]{:S(2)}, u32[]{:S(2)}) %collective-permute-start.47) | collective-permute-done | bytes 98336 | tf_op jit(solution)/shard_map/ppermute | solution.py:43
  (228 shorter events, 94.2 us)
Async XLA Ops:
  7.2 110.7 %all-gather.2.cloned.1.call-start = ((), (), s32[]{:S(2)}) async-start(), calls=%async_computation.2 | async-start | bytes 3899392 | tf_op jit(solution)/shard_map/all_gather | solution.py:578
  8.1 15.8 %collective-permute-start.1 = (bf16[64,384]{1,0:T(8,128)(2,1)S(1)}, bf16[64,384]{1,0:T(8,128)(2,1)S(1)}, u32[]{:S(2)}, u32[]{:S(2)}) collective-permute-start(bf16[64,384]{1,0:T(8,128)(2,1)S(1)} %pad_maximum_fusion.6), channel_id=1, source_target_pairs={{0,0},{1,8},{8,1},{9,9},{16,16},{17,24},{24,17},{25,25},{2,2},{3,1... | collective-permute-start | bytes 147464 | tf_op jit(solution)/shard_map/ppermute | solution.py:59
  12.6 14.9 %collective-permute-start.2 = (bf16[64,384]{1,0:T(8,128)(2,1)S(1)}, bf16[64,384]{1,0:T(8,128)(2,1)S(1)}, u32[]{:S(2)}, u32[]{:S(2)}) collective-permute-start(bf16[64,384]{1,0:T(8,128)(2,1)S(1)} %pad_maximum_fusion.6), channel_id=1, source_target_pairs={{0,17},{1,25},{8,0},{9,8},{16,1},{17,9},{24,16},{25,24},{2,19},{3,... | collective-permute-start | bytes 147464 | tf_op jit(solution)/shard_map/ppermute | solution.py:59
  12.7 16.8 %collective-permute-start.3 = (bf16[64,384]{1,0:T(8,128)(2,1)S(1)}, bf16[64,384]{1,0:T(8,128)(2,1)S(1)}, u32[]{:S(2)}, u32[]{:S(2)}) collective-permute-start(bf16[64,384]{1,0:T(8,128)(2,1)S(1)} %pad_maximum_fusion.6), channel_id=1, source_target_pairs={{0,16},{1,24},{8,17},{9,25},{16,0},{17,8},{24,1},{25,9},{2,18},{3,... | collective-permute-start | bytes 147464 | tf_op jit(solution)/shard_map/ppermute | solution.py:59
  14.3 15.2 %collective-permute-start.4 = (bf16[64,384]{1,0:T(8,128)(2,1)S(1)}, bf16[64,384]{1,0:T(8,128)(2,1)S(1)}, u32[]{:S(2)}, u32[]{:S(2)}) collective-permute-start(bf16[64,384]{1,0:T(8,128)(2,1)S(1)} %pad_maximum_fusion.6), channel_id=1, source_target_pairs={{0,1},{1,9},{8,16},{9,24},{16,17},{17,25},{24,0},{25,8},{2,3},{3,1... | collective-permute-start | bytes 147464 | tf_op jit(solution)/shard_map/ppermute | solution.py:59
  30.6 19.3 %collective-permute-start.10 = (bf16[2,64,1024]{2,1,0:T(8,128)(2,1)S(1)}, bf16[2,64,1024]{2,1,0:T(8,128)(2,1)S(1)}, u32[]{:S(2)}, u32[]{:S(2)}) collective-permute-start(bf16[2,64,1024]{2,1,0:T(8,128)(2,1)S(1)} %collective-permute-done.5), channel_id=1, source_target_pairs={{0,6},{2,0},{4,2},{6,4},{1,7},{3,1},{5,3},{7,5},{8,14},{10,8},{12,... | collective-permute-start | bytes 786440 | tf_op jit(solution)/shard_map/ppermute | solution.py:49
  34.5 15.5 %collective-permute-start.11 = (bf16[2,64,1024]{2,1,0:T(8,128)(2,1)S(1)}, bf16[2,64,1024]{2,1,0:T(8,128)(2,1)S(1)}, u32[]{:S(2)}, u32[]{:S(2)}) collective-permute-start(bf16[2,64,1024]{2,1,0:T(8,128)(2,1)S(1)} %collective-permute-done.5), channel_id=1, source_target_pairs={{0,4},{2,6},{4,0},{6,2},{1,5},{3,7},{5,1},{7,3},{8,12},{10,14},{12... | collective-permute-start | bytes 786440 | tf_op jit(solution)/shard_map/ppermute | solution.py:49
  34.5 15.5 %collective-permute-start.12 = (bf16[2,64,1024]{2,1,0:T(8,128)(2,1)S(1)}, bf16[2,64,1024]{2,1,0:T(8,128)(2,1)S(1)}, u32[]{:S(2)}, u32[]{:S(2)}) collective-permute-start(bf16[2,64,1024]{2,1,0:T(8,128)(2,1)S(1)} %collective-permute-done.5), channel_id=1, source_target_pairs={{0,2},{2,4},{4,6},{6,0},{1,3},{3,5},{5,7},{7,1},{8,10},{10,12},{12... | collective-permute-start | bytes 786440 | tf_op jit(solution)/shard_map/ppermute | solution.py:49
  50.0 186.2 %reduce-scatter.2.cloned.1.call-start = ((), (), s32[]{:S(2)}) async-start(), calls=%async_computation.3 | async-start | bytes 3899392 | tf_op jit(solution)/shard_map/reduce_scatter | solution.py:597
  50.2 22.9 %collective-permute-start.13 = (bf16[4,2,64,1024]{3,2,1,0:T(8,128)(2,1)S(1)}, bf16[4,2,64,1024]{3,2,1,0:T(8,128)(2,1)S(1)}, u32[]{:S(2)}, u32[]{:S(2)}) collective-permute-start(bf16[4,2,64,1024]{3,2,1,0:T(8,128)(2,1)S(1)} %pad_maximum_fusion.refs_0_), channel_id=1, source_target_pairs={{0,8},{8,0},{1,9},{9,1},{2,10},{10,2},{3,11},{11,3},{4,12},{12,4},... | collective-permute-start | bytes 3145736 | tf_op jit(solution)/shard_map/ppermute | solution.py:67
  60.4 27.6 %collective-permute-start.19 = (bf16[2,64,1024]{2,1,0:T(8,128)(2,1)S(1)}, bf16[2,64,1024]{2,1,0:T(8,128)(2,1)S(1)}, u32[]{:S(2)}, u32[]{:S(2)}) collective-permute-start(bf16[2,64,1024]{2,1,0:T(8,128)(2,1)S(1)} %collective-permute-done.17), channel_id=1, source_target_pairs={{0,4},{2,6},{4,0},{6,2},{1,5},{3,7},{5,1},{7,3},{8,12},{10,14},{12... | collective-permute-start | bytes 786440 | tf_op jit(solution)/shard_map/ppermute | solution.py:49
  62.4 25.6 %collective-permute-start.20 = (bf16[2,64,1024]{2,1,0:T(8,128)(2,1)S(1)}, bf16[2,64,1024]{2,1,0:T(8,128)(2,1)S(1)}, u32[]{:S(2)}, u32[]{:S(2)}) collective-permute-start(bf16[2,64,1024]{2,1,0:T(8,128)(2,1)S(1)} %collective-permute-done.17), channel_id=1, source_target_pairs={{0,2},{2,4},{4,6},{6,0},{1,3},{3,5},{5,7},{7,1},{8,10},{10,12},{12... | collective-permute-start | bytes 786440 | tf_op jit(solution)/shard_map/ppermute | solution.py:49
  63.3 24.7 %collective-permute-start.14 = (bf16[1024,128]{1,0:T(8,128)(2,1)S(1)}, bf16[1024,128]{1,0:T(8,128)(2,1)S(1)}, u32[]{:S(2)}, u32[]{:S(2)}) collective-permute-start(bf16[1024,128]{1,0:T(8,128)(2,1)S(1)} %pad_maximum_fusion.4), channel_id=1, source_target_pairs={{0,6},{2,0},{4,2},{6,4},{1,7},{3,1},{5,3},{7,5},{8,14},{10,8},{12,... | collective-permute-start | bytes 786440 | tf_op jit(solution)/shard_map/ppermute | solution.py:49
  72.0 16.0 %collective-permute-start.15 = (bf16[1024,128]{1,0:T(8,128)(2,1)S(1)}, bf16[1024,128]{1,0:T(8,128)(2,1)}, u32[]{:S(2)}, u32[]{:S(2)}) collective-permute-start(bf16[1024,128]{1,0:T(8,128)(2,1)S(1)} %pad_maximum_fusion.4), channel_id=1, source_target_pairs={{0,4},{2,6},{4,0},{6,2},{1,5},{3,7},{5,1},{7,3},{8,12},{10,14},{12... | collective-permute-start | bytes 786440 | tf_op jit(solution)/shard_map/ppermute | solution.py:49
  89.2 19.0 %collective-permute-start.28 = (bf16[4,1024,128]{2,1,0:T(8,128)(2,1)S(1)}, bf16[4,1024,128]{2,1,0:T(8,128)(2,1)S(1)}, u32[]{:S(2)}, u32[]{:S(2)}) collective-permute-start(bf16[4,1024,128]{2,1,0:T(8,128)(2,1)S(1)} %pad_maximum_fusion.1.refs_8_), channel_id=1, source_target_pairs={{0,8},{8,0},{1,9},{9,1},{2,10},{10,2},{3,11},{11,3},{4,12},{12,4},... | collective-permute-start | bytes 3145736 | tf_op jit(solution)/shard_map/ppermute | solution.py:67
  91.8 26.0 %collective-permute-start.29 = (bf16[4,2,64,1024]{3,2,1,0:T(8,128)(2,1)S(1)}, bf16[4,2,64,1024]{3,2,1,0:T(8,128)(2,1)}, u32[]{:S(2)}, u32[]{:S(2)}) collective-permute-start(bf16[4,2,64,1024]{3,2,1,0:T(8,128)(2,1)S(1)} %pad_maximum_fusion.2.refs_0_), channel_id=1, source_target_pairs={{0,8},{8,0},{1,9},{9,1},{2,10},{10,2},{3,11},{11,3},{4,12},{12,4},... | collective-permute-start | bytes 3145736 | tf_op jit(solution)/shard_map/ppermute | solution.py:67
  156.0 14.0 %collective-permute-start.34 = (bf16[2,64,1024]{2,1,0:T(8,128)(2,1)S(1)}, bf16[2,64,1024]{2,1,0:T(8,128)(2,1)S(1)}, u32[]{:S(2)}, u32[]{:S(2)}) collective-permute-start(bf16[2,64,1024]{2,1,0:T(8,128)(2,1)S(1)} %fusion.1.refs_0_), channel_id=1, source_target_pairs={{0,6},{2,0},{4,2},{6,4},{1,7},{3,1},{5,3},{7,5},{8,14},{10,8},{12,... | collective-permute-start | bytes 786440 | tf_op jit(solution)/shard_map/ppermute | solution.py:49
  159.6 15.1 %collective-permute-start.36 = (bf16[2,64,1024]{2,1,0:T(8,128)(2,1)S(1)}, bf16[2,64,1024]{2,1,0:T(8,128)(2,1)S(1)}, u32[]{:S(2)}, u32[]{:S(2)}) collective-permute-start(bf16[2,64,1024]{2,1,0:T(8,128)(2,1)S(1)} %fusion.1.refs_0_), channel_id=1, source_target_pairs={{0,2},{2,4},{4,6},{6,0},{1,3},{3,5},{5,7},{7,1},{8,10},{10,12},{12... | collective-permute-start | bytes 786440 | tf_op jit(solution)/shard_map/ppermute | solution.py:49
  175.7 22.2 %collective-permute-start.42 = (bf16[2,256,1024]{2,1,0:T(8,128)(2,1)}, bf16[2,256,1024]{2,1,0:T(8,128)(2,1)S(1)}, u32[]{:S(2)}, u32[]{:S(2)}) collective-permute-start(bf16[2,256,1024]{2,1,0:T(8,128)(2,1)} %get-tuple-element.145), channel_id=1, source_target_pairs={{0,8},{8,0},{1,9},{9,1},{2,10},{10,2},{3,11},{11,3},{4,12},{12,4},... | collective-permute-start | bytes 3145736 | tf_op jit(solution)/shard_map/ppermute | solution.py:67
  193.7 21.2 %all-to-all-start = ((bf16[16,80,384]{2,1,0:T(8,128)(2,1)}), bf16[16,80,384]{2,1,0:T(8,128)(2,1)S(1)}, u32[]{:S(2)}, u32[]{:S(2)}) async-start(bf16[16,80,384]{2,1,0:T(8,128)(2,1)} %get-tuple-element.147), calls=%async_computation | async-start | bytes 1966080 | tf_op jit(solution)/shard_map/all_to_all | solution.py:609
  202.8 15.2 %collective-permute-start.43 = (bf16[4,64,1024]{2,1,0:T(8,128)(2,1)}, bf16[4,64,1024]{2,1,0:T(8,128)(2,1)S(1)}, u32[]{:S(2)}, u32[]{:S(2)}) collective-permute-start(bf16[4,64,1024]{2,1,0:T(8,128)(2,1)} %get-tuple-element.149), channel_id=1, source_target_pairs={{0,2},{2,4},{4,6},{6,0},{1,3},{3,5},{5,7},{7,1},{8,10},{10,12},{12... | collective-permute-start | bytes 1572872 | tf_op jit(solution)/shard_map/ppermute | solution.py:49
  202.8 24.9 %collective-permute-start.44 = (bf16[4,64,1024]{2,1,0:T(8,128)(2,1)}, bf16[4,64,1024]{2,1,0:T(8,128)(2,1)S(1)}, u32[]{:S(2)}, u32[]{:S(2)}) collective-permute-start(bf16[4,64,1024]{2,1,0:T(8,128)(2,1)} %get-tuple-element.150), channel_id=1, source_target_pairs={{0,4},{2,6},{4,0},{6,2},{1,5},{3,7},{5,1},{7,3},{8,12},{10,14},{12... | collective-permute-start | bytes 1572872 | tf_op jit(solution)/shard_map/ppermute | solution.py:49
  204.6 24.4 %collective-permute-start.45 = (bf16[4,64,1024]{2,1,0:T(8,128)(2,1)}, bf16[4,64,1024]{2,1,0:T(8,128)(2,1)}, u32[]{:S(2)}, u32[]{:S(2)}) collective-permute-start(bf16[4,64,1024]{2,1,0:T(8,128)(2,1)} %get-tuple-element.151), channel_id=1, source_target_pairs={{0,6},{2,0},{4,2},{6,4},{1,7},{3,1},{5,3},{7,5},{8,14},{10,8},{12,... | collective-permute-start | bytes 1572872 | tf_op jit(solution)/shard_map/ppermute | solution.py:49
  238.9 21.7 %collective-permute-start.48 = (bf16[64,1728]{1,0:T(8,128)(2,1)}, bf16[64,1728]{1,0:T(8,128)(2,1)S(1)}, u32[]{:S(2)}, u32[]{:S(2)}) collective-permute-start(bf16[64,1728]{1,0:T(8,128)(2,1)} %reduce-scatter.2.cloned.1.call-done), channel_id=1, source_target_pairs={{0,0},{1,8},{8,1},{9,9},{2,2},{3,10},{10,3},{11,11},{4,4},{5,12},{... | collective-permute-start | bytes 663560 | tf_op jit(solution)/shard_map/ppermute | solution.py:43
  (66 other events, 537.3 us)
Sparse Core Ops, SparseCore 0:
  50.1 47.1 all-gather.1
  154.9 81.2 reduce-scatter.1

commit v5 on v4

--- a/solution.py
+++ b/solution.py
@@ -88,11 +88,6 @@
     v = lax.dynamic_slice_in_dim(jnp.concatenate([v, v], axis), z, 4, axis)
     v = lax.dynamic_slice_in_dim(jnp.concatenate([v, v], axis + 1), core, 2, axis + 1)
     return jnp.swapaxes(v, axis, axis + 1).reshape(shape)
-
-
-def group_sum(value):
-    value = value + other_core(value)
-    return value + sum(from_z(value, k) for k in (1, 2, 3))
 
 
 def tie(*values):
@@ -572,9 +567,9 @@
     bias = jnp.where(allowed, 0.0, -1e30).astype(bf16)
     qk_gain = jnp.stack([jnp.tile(query_gain, 2), jnp.tile(key_gain, 2)])
 
-    w_ffn, *pieces = tie(w_ffn, *w_att, *x_pieces, cosine, sine, bias, qk_gain, at)
+    w_ffn, *pieces = tie(w_ffn, *w_att, *x_pieces, cosine, sine, bias, qk_gain, at, cotangent_own)
     w_att, x_pieces = pieces[:4], pieces[4:8]
-    cosine, sine, bias, qk_gain, at = pieces[8:]
+    cosine, sine, bias, qk_gain, at, cotangent_own = pieces[8:]
     w_ffn = lax.all_gather(w_ffn, plane, axis=0, tiled=True)
     w_out_chain = from_chain(jnp.concatenate([w[:, nq + 2 * nk :] for w in w_att], axis=0))
     x_chain, x_other = gather_chains(x_pieces)
@@ -609,14 +604,15 @@
     grad_att = lax.all_to_all(grad_att, plane, 0, 0)
     parts = split(grad_own, grad_other, down_own, down_got)
     got = [from_z(parts[k], -k) for k in (1, 2, 3)]
-    grad_att, grad_ffn, *got = tie(grad_att, grad_ffn, *got)
+    grad_att = jnp.sum(grad_att.astype(f32), axis=0)
+    gains = grad_att[64:70].reshape(-1)
+    gains, grad_ffn, *got = tie(gains + other_core(gains), grad_ffn, *got)
     total = parts[0] + sum(piece.astype(f32) for piece in got)
     _, first_pull = jax.vjp(rms_rows, x_own.astype(f32), norm_gain)
     grad_resid_norm, _ = first_pull(total[:micro])
     input_grad = grad_state.astype(f32) + grad_resid_norm
     results = swap(jnp.concatenate([state_own + total[micro:], input_grad]).astype(bf16))
-    grad_att = jnp.sum(grad_att.astype(f32), axis=0)
-    gains = group_sum(grad_att[64:70].reshape(-1))
+    gains = gains + sum(from_z(gains, k) for k in (1, 2, 3))
     grad_att = swap(grad_att[:64])
     grad_ffn = swap(grad_ffn.astype(bf16)).astype(f32)
     both = nq + nk

time: 270 us -> 275 us (1.019)
  waiting for transfers between devices: 87.8 us -> 91.9 us
    reduce_scatter x1, waiting for transfers between devices: 7.33 us -> 0.01 us  [local(): lax.psum_scatter(grad_ffn, plane, scatter_dimension=0, tiled=True)]
    ppermute x24, waiting for transfers between devices: 49.3 us -> 56.4 us  [from_z(): return lax.ppermute(value, 'z', [(z, (z - k) % 4) for z in range(4)])]
    all_to_all x1, waiting for transfers between devices: 9.44 us -> 16 us  [local(): grad_att = lax.all_to_all(grad_att, plane, 0, 0)]
    ppermute x7, waiting for transfers between devices: 9.09 us -> 4.79 us  [swap(): lax.ppermute(value, ('core', 'xl'), [(a * 2 + b, b * 2 + a) for a in rang...]
    unnamed x68 -> x70, local copies, waits for them, and re-layouts: 4.86 us -> 5.51 us
where the time goes in v5:
time: 275 us
  waiting for transfers between devices  91.9 us (33%)
  starting transfers between devices  77.5 us (28%)
  Pallas kernels  65 us (24%)
  between operations  14.7 us (5%)
  other arithmetic  13.4 us (5%)
  local copies, waits for them, and re-layouts  12.2 us (4%)
    ppermute x24, waiting for transfers between devices, from_z(): return lax.ppermute(value, 'z', [(z, (z - k) % 4) for z in range(4)])  56.4 us
    ppermute x24, starting transfers between devices, from_z(): return lax.ppermute(value, 'z', [(z, (z - k) % 4) for z in range(4)])  30.1 us
    ppermute x7, starting transfers between devices, swap(): lax.ppermute(value, ('core', 'xl'), [(a * 2 + b, b * 2 + a) for a in rang...  20.4 us
    all_to_all x1, waiting for transfers between devices, local(): grad_att = lax.all_to_all(grad_att, plane, 0, 0)  16 us
    pallas_call x1, Pallas kernels, feed(): pl.pallas_call(feed_kernel, grid=(steps,), in_specs=[rows(width), whole(w...  15.4 us
    pallas_call x1, Pallas kernels, back(): pl.pallas_call(back_kernel, grid=(micro,), in_specs=[part(p) for p in sta...  14.8 us
    pallas_call x1, Pallas kernels, attend(): pl.pallas_call(attend_kernel, grid_spec=pltpu.PrefetchScalarGridSpec(num_...  11 us
    ppermute x4, starting transfers between devices, swap_from_x(): return lax.ppermute(value, ('xh', 'core', 'xl'), perm)  9.65 us
  transfers between devices with their start and end apart: 56, of which 25 were waited for; matrix products, arithmetic and copies ran while one was open for 7% of the time, Pallas kernels for 17%

profile of v5, /device:TPU:1, one launch (start us, length us, event | category | flops | bytes accessed | tf_op | source)
XLA Modules:
  0.0 274.7 jit_solution(7786286941229278572)
XLA Ops:
  8.1 4.5 %collective-permute-start.1 = (bf16[64,384]{1,0:T(8,128)(2,1)S(1)}, bf16[64,384]{1,0:T(8,128)(2,1)S(1)}, u32[]{:S(2)}, u32[]{:S(2)}) collective-permute-start(bf16[64,384]{1,0:T(8,128)(2,1)S(1)} %pad_maximum_fusion.6), channel_id=1, source_target_pairs={{0,0},{1,8},{8,1},{9,9},{16,16},{17,24},{24,17},{25,25},{2,2},{3,1... | collective-permute-start | bytes 147464 | tf_op jit(solution)/shard_map/ppermute | solution.py:59
  14.3 3.4 %collective-permute-start.4 = (bf16[64,384]{1,0:T(8,128)(2,1)S(1)}, bf16[64,384]{1,0:T(8,128)(2,1)S(1)}, u32[]{:S(2)}, u32[]{:S(2)}) collective-permute-start(bf16[64,384]{1,0:T(8,128)(2,1)S(1)} %pad_maximum_fusion.6), channel_id=1, source_target_pairs={{0,1},{1,9},{8,16},{9,24},{16,17},{17,25},{24,0},{25,8},{2,3},{3,1... | collective-permute-start | bytes 147464 | tf_op jit(solution)/shard_map/ppermute | solution.py:59
  23.9 3.6 %collective-permute-start.6 = (s32[2,512]{1,0:T(2,128)}, s32[2,512]{1,0:T(2,128)S(1)}, u32[]{:S(2)}, u32[]{:S(2)}) collective-permute-start(s32[2,512]{1,0:T(2,128)} %param.15), channel_id=1, source_target_pairs={{0,0},{1,8},{8,1},{9,9},{2,2},{3,10},{10,3},{11,11},{4,4},{5,12},{... | collective-permute-start | bytes 12296 | tf_op jit(solution)/shard_map/ppermute | solution.py:43
  29.5 3.6 %collective-permute-start.13 = (bf16[2,64,1024]{2,1,0:T(8,128)(2,1)}, bf16[2,64,1024]{2,1,0:T(8,128)(2,1)S(1)}, u32[]{:S(2)}, u32[]{:S(2)}) collective-permute-start(bf16[2,64,1024]{2,1,0:T(8,128)(2,1)} %param.16), channel_id=1, source_target_pairs={{0,0},{1,8},{8,1},{9,9},{2,2},{3,10},{10,3},{11,11},{4,4},{5,12},{... | collective-permute-start | bytes 786440 | tf_op jit(solution)/shard_map/ppermute | solution.py:43
  34.3 3.8 %collective-permute-start.10 = (bf16[2,64,1024]{2,1,0:T(8,128)(2,1)S(1)}, bf16[2,64,1024]{2,1,0:T(8,128)(2,1)S(1)}, u32[]{:S(2)}, u32[]{:S(2)}) collective-permute-start(bf16[2,64,1024]{2,1,0:T(8,128)(2,1)S(1)} %collective-permute-done.5), channel_id=1, source_target_pairs={{0,6},{2,0},{4,2},{6,4},{1,7},{3,1},{5,3},{7,5},{8,14},{10,8},{12,... | collective-permute-start | bytes 786440 | tf_op jit(solution)/shard_map/ppermute | solution.py:49
  43.9 4.3 %collective-permute-done.7.refs_3_ = bf16[256,384]{1,0:T(8,128)(2,1)S(1)} collective-permute-done((bf16[256,384]{1,0:T(8,128)(2,1)S(1)}, bf16[256,384]{1,0:T(8,128)(2,1)S(1)}, u32[]{:S(2)}, u32[]{:S(2)}) %collective-permute-start.7) | collective-permute-done | bytes 196640 | tf_op jit(solution)/shard_map/ppermute | solution.py:63
  67.0 11.0 %attend.1 = (bf16[1024,128]{1,0:T(8,128)(2,1)}, bf16[1024,1024]{1,0:T(8,128)(2,1)}, bf16[1024,1024]{1,0:T(8,128)(2,1)}, bf16[1024,384]{1,0:T(8,128)(2,1)}, f32[1...) custom-call(s32[4]{0:T(128)} %pad_add_fusion.at_ref, ...), custom_call_target="tpu_custom_call" | custom-call | flops 12000000000 | bytes 10000000 | tf_op jit(solution)/shard_map/attend/pallas_call | solution.py:181
  78.1 4.7 %collective-permute-done.20 = bf16[2,64,1024]{2,1,0:T(8,128)(2,1)S(1)} collective-permute-done((bf16[2,64,1024]{2,1,0:T(8,128)(2,1)S(1)}, bf16[2,64,1024]{2,1,0:T(8,128)(2,1)S(1)}, u32[]{:S(2)}, u32[]{:S(2)}) %collective-permute-start.20) | collective-permute-done | bytes 262176 | tf_op jit(solution)/shard_map/ppermute | solution.py:49
  84.6 3.8 %collective-permute-start.28 = (bf16[4,1024,128]{2,1,0:T(8,128)(2,1)S(1)}, bf16[4,1024,128]{2,1,0:T(8,128)(2,1)S(1)}, u32[]{:S(2)}, u32[]{:S(2)}) collective-permute-start(bf16[4,1024,128]{2,1,0:T(8,128)(2,1)S(1)} %pad_maximum_fusion.1.refs_8_), channel_id=1, source_target_pairs={{0,8},{8,0},{1,9},{9,1},{2,10},{10,2},{3,11},{11,3},{4,12},{12,4},... | collective-permute-start | bytes 3145736 | tf_op jit(solution)/shard_map/ppermute | solution.py:67
  92.4 3.8 %collective-permute-done.21.refs_1_ = bf16[1024,128]{1,0:T(8,128)(2,1)S(1)} collective-permute-done((bf16[1024,128]{1,0:T(8,128)(2,1)S(1)}, bf16[1024,128]{1,0:T(8,128)(2,1)S(1)}, u32[]{:S(2)}, u32[]{:S(2)}) %collective-permute-start.21) | collective-permute-done | bytes 262176 | tf_op jit(solution)/shard_map/ppermute | solution.py:49
  97.7 6.5 %collective-permute-done.23.refs_3_ = bf16[1024,128]{1,0:T(8,128)(2,1)S(1)} collective-permute-done((bf16[1024,128]{1,0:T(8,128)(2,1)S(1)}, bf16[1024,128]{1,0:T(8,128)(2,1)S(1)}, u32[]{:S(2)}, u32[]{:S(2)}) %collective-permute-start.23) | collective-permute-done | bytes 262176 | tf_op jit(solution)/shard_map/ppermute | solution.py:49
  108.5 8.5 %second_norm.1 = (f32[256,1024]{1,0:T(8,128)}, bf16[1024,1024]{1,0:T(8,128)(2,1)}) custom-call(s32[4]{0:T(128)} %pad_add_fusion.at_ref, bf16[1024,128]{1,0:T(8,128)(2,1)} %get-tuple-element.105.refs_0_.refs_15_, bf16[1024,128]{1,0:T(8,128)(2,1)} %copy-done.28, bf16[1024,128]{1,0:T(8,128)(2,1)} %copy-done.29, bf16[1024,128]{1,0:T(8,128)(2,1)} %copy-done.30, ...), custom_call_target="tpu_custom_call" | custom-call | flops 3000000000 | bytes 10000000 | tf_op jit(solution)/shard_map/second_norm/pallas_call | solution.py:251
  117.0 15.4 %feed.1 = (bf16[1024,576]{1,0:T(8,128)(2,1)}, bf16[1024,1152]{1,0:T(8,128)(2,1)}, bf16[2,256,1024]{2,1,0:T(8,128)(2,1)}, bf16[2,256,1024]{2,1,0:T(8,128)(2,1)}, ...) custom-call(bf16[1024,1024]{1,0:T(8,128)(2,1)} %get-tuple-element.115.second_ref, ...), custom_call_target="tpu_custom_call" | custom-call | flops 8999999488 | bytes 10000000 | tf_op jit(solution)/shard_map/feed/pallas_call | solution.py:336
  142.4 8.8 %weights_back.1 = bf16[1024,1728]{1,0:T(8,128)(2,1)} custom-call(bf16[1024,1024]{1,0:T(8,128)(2,1)} %get-tuple-element.115.second_ref, bf16[1024,1024]{1,0:T(8,128)(2,1)} %get-tuple-element.124.up_ref, bf16[1024,1152]{1,0:T(8,128)(2,1)} %get-tuple-element.125.low_ref, bf16[1024,576]{1,0:T(8,128)(2,1)} %get-tuple-element.126.inner_ref), custom_call_target="tpu_custom_call" | custom-call | flops 4000000000 | bytes 10000000 | tf_op jit(solution)/shard_map/weights_back/pallas_call | solution.py:363
  159.2 10.0 %collective-permute-done.34.refs_1_ = bf16[2,64,1024]{2,1,0:T(8,128)(2,1)S(1)} collective-permute-done((bf16[2,64,1024]{2,1,0:T(8,128)(2,1)S(1)}, bf16[2,64,1024]{2,1,0:T(8,128)(2,1)S(1)}, u32[]{:S(2)}, u32[]{:S(2)}) %collective-permute-start.34) | collective-permute-done | bytes 262176 | tf_op jit(solution)/shard_map/ppermute | solution.py:49
  169.2 4.4 %collective-permute-done.36.refs_3_ = bf16[2,64,1024]{2,1,0:T(8,128)(2,1)S(1)} collective-permute-done((bf16[2,64,1024]{2,1,0:T(8,128)(2,1)S(1)}, bf16[2,64,1024]{2,1,0:T(8,128)(2,1)S(1)}, u32[]{:S(2)}, u32[]{:S(2)}) %collective-permute-start.36) | collective-permute-done | bytes 262176 | tf_op jit(solution)/shard_map/ppermute | solution.py:49
  177.2 14.8 %back.1 = (bf16[2,256,1024]{2,1,0:T(8,128)(2,1)}, bf16[2,256,1024]{2,1,0:T(8,128)(2,1)}, bf16[16,80,384]{2,1,0:T(8,128)(2,1)}) custom-call(bf16[2,64,1024]{2,1,0:T(8,128)(2,1)} %copy-done.1, bf16[2,64,1024]{2,1,0:T(8,128)(2,1)} %copy-done.11, bf16[2,64,1024]{2,1,0:T(8,128)(2,1)} %copy-done.12, bf16[2,64,1024]{2,1,0:T(8,128)(2,1)} %copy-done.13, ...), custom_call_target="tpu_custom_call" | custom-call | flops 1000000 | bytes 10000 | tf_op jit(solution)/shard_map/back/pallas_call | solution.py:466
  192.0 5.3 %all-to-all-start = ((bf16[16,80,384]{2,1,0:T(8,128)(2,1)}), bf16[16,80,384]{2,1,0:T(8,128)(2,1)S(1)}, u32[]{:S(2)}, u32[]{:S(2)}) async-start(bf16[16,80,384]{2,1,0:T(8,128)(2,1)} %get-tuple-element.149), calls=%async_computation | async-start | bytes 1966080 | tf_op jit(solution)/shard_map/all_to_all | solution.py:604
  198.1 16.0 %all-to-all-done = bf16[16,80,384]{2,1,0:T(8,128)(2,1)S(1)} async-done(((bf16[16,80,384]{2,1,0:T(8,128)(2,1)}), bf16[16,80,384]{2,1,0:T(8,128)(2,1)S(1)}, u32[]{:S(2)}, u32[]{:S(2)}) %all-to-all-start) | async-done | bytes 983072 | tf_op jit(solution)/shard_map/all_to_all | solution.py:604
  214.3 3.7 %collective-permute-start.48 = (f32[64,384]{1,0:T(8,128)S(1)}, f32[64,384]{1,0:T(8,128)S(1)}, u32[]{:S(2)}, u32[]{:S(2)}) collective-permute-start(f32[64,384]{1,0:T(8,128)S(1)} %slice.119), channel_id=1, source_target_pairs={{0,0},{1,8},{8,1},{9,9},{2,2},{3,10},{10,3},{11,11},{4,4},{5,12},{... | collective-permute-start | bytes 294920 | tf_op jit(solution)/shard_map/ppermute | solution.py:43
  219.0 3.8 %split.3 = (f32[4,64,1024]{2,1,0:T(8,128)}, bf16[4,64,1024]{2,1,0:T(8,128)(2,1)}, bf16[4,64,1024]{2,1,0:T(8,128)(2,1)}, bf16[4,64,1024]{2,1,0:T(8,128)(2,1)}) custom-call(bf16[2,256,1024]{2,1,0:T(8,128)(2,1)} %get-tuple-element.144.refs_0_, bf16[2,256,1024]{2,1,0:T(8,128)(2,1)} %collective-permute-done.41.refs_1_, ...), custom_call_target="tpu_custom_call" | custom-call | tf_op jit(solution)/shard_map/split/pallas_call | solution.py:510
  228.3 20.0 %collective-permute-done.44 = bf16[4,64,1024]{2,1,0:T(8,128)(2,1)S(1)} collective-permute-done((bf16[4,64,1024]{2,1,0:T(8,128)(2,1)}, bf16[4,64,1024]{2,1,0:T(8,128)(2,1)S(1)}, u32[]{:S(2)}, u32[]{:S(2)}) %collective-permute-start.44) | collective-permute-done | bytes 524320 | tf_op jit(solution)/shard_map/ppermute | solution.py:49
  256.5 3.6 %collective-permute-start.47 = (bf16[4,64,1024]{2,1,0:T(8,128)(2,1)S(1)}, bf16[4,64,1024]{2,1,0:T(8,128)(2,1)S(1)}, u32[]{:S(2)}, u32[]{:S(2)}) collective-permute-start(bf16[4,64,1024]{2,1,0:T(8,128)(2,1)S(1)} %pad_maximum_fusion.3), channel_id=1, source_target_pairs={{0,0},{1,8},{8,1},{9,9},{2,2},{3,10},{10,3},{11,11},{4,4},{5,12},{... | collective-permute-start | bytes 1572872 | tf_op jit(solution)/shard_map/ppermute | solution.py:43
  262.2 4.8 %collective-permute-done.47 = bf16[4,64,1024]{2,1,0:T(8,128)(2,1)S(1)} collective-permute-done((bf16[4,64,1024]{2,1,0:T(8,128)(2,1)S(1)}, bf16[4,64,1024]{2,1,0:T(8,128)(2,1)S(1)}, u32[]{:S(2)}, u32[]{:S(2)}) %collective-permute-start.47) | collective-permute-done | bytes 524320 | tf_op jit(solution)/shard_map/ppermute | solution.py:43
  (230 shorter events, 87.7 us)
Async XLA Ops:
  7.2 109.8 %all-gather.2.cloned.1.call-start = ((), (), s32[]{:S(2)}) async-start(), calls=%async_computation.2 | async-start | bytes 3899392 | tf_op jit(solution)/shard_map/all_gather | solution.py:573
  8.1 15.8 %collective-permute-start.1 = (bf16[64,384]{1,0:T(8,128)(2,1)S(1)}, bf16[64,384]{1,0:T(8,128)(2,1)S(1)}, u32[]{:S(2)}, u32[]{:S(2)}) collective-permute-start(bf16[64,384]{1,0:T(8,128)(2,1)S(1)} %pad_maximum_fusion.6), channel_id=1, source_target_pairs={{0,0},{1,8},{8,1},{9,9},{16,16},{17,24},{24,17},{25,25},{2,2},{3,1... | collective-permute-start | bytes 147464 | tf_op jit(solution)/shard_map/ppermute | solution.py:59
  12.6 14.9 %collective-permute-start.2 = (bf16[64,384]{1,0:T(8,128)(2,1)S(1)}, bf16[64,384]{1,0:T(8,128)(2,1)S(1)}, u32[]{:S(2)}, u32[]{:S(2)}) collective-permute-start(bf16[64,384]{1,0:T(8,128)(2,1)S(1)} %pad_maximum_fusion.6), channel_id=1, source_target_pairs={{0,17},{1,25},{8,0},{9,8},{16,1},{17,9},{24,16},{25,24},{2,19},{3,... | collective-permute-start | bytes 147464 | tf_op jit(solution)/shard_map/ppermute | solution.py:59
  12.7 16.8 %collective-permute-start.3 = (bf16[64,384]{1,0:T(8,128)(2,1)S(1)}, bf16[64,384]{1,0:T(8,128)(2,1)S(1)}, u32[]{:S(2)}, u32[]{:S(2)}) collective-permute-start(bf16[64,384]{1,0:T(8,128)(2,1)S(1)} %pad_maximum_fusion.6), channel_id=1, source_target_pairs={{0,16},{1,24},{8,17},{9,25},{16,0},{17,8},{24,1},{25,9},{2,18},{3,... | collective-permute-start | bytes 147464 | tf_op jit(solution)/shard_map/ppermute | solution.py:59
  14.3 18.8 %collective-permute-start.4 = (bf16[64,384]{1,0:T(8,128)(2,1)S(1)}, bf16[64,384]{1,0:T(8,128)(2,1)S(1)}, u32[]{:S(2)}, u32[]{:S(2)}) collective-permute-start(bf16[64,384]{1,0:T(8,128)(2,1)S(1)} %pad_maximum_fusion.6), channel_id=1, source_target_pairs={{0,1},{1,9},{8,16},{9,24},{16,17},{17,25},{24,0},{25,8},{2,3},{3,1... | collective-permute-start | bytes 147464 | tf_op jit(solution)/shard_map/ppermute | solution.py:59
  17.7 15.5 %collective-permute-start.5 = (bf16[2,64,1024]{2,1,0:T(8,128)(2,1)}, bf16[2,64,1024]{2,1,0:T(8,128)(2,1)S(1)}, u32[]{:S(2)}, u32[]{:S(2)}) collective-permute-start(bf16[2,64,1024]{2,1,0:T(8,128)(2,1)} %param.14), channel_id=1, source_target_pairs={{0,0},{1,8},{8,1},{9,9},{2,2},{3,10},{10,3},{11,11},{4,4},{5,12},{... | collective-permute-start | bytes 786440 | tf_op jit(solution)/shard_map/ppermute | solution.py:43
  34.3 20.1 %collective-permute-start.10 = (bf16[2,64,1024]{2,1,0:T(8,128)(2,1)S(1)}, bf16[2,64,1024]{2,1,0:T(8,128)(2,1)S(1)}, u32[]{:S(2)}, u32[]{:S(2)}) collective-permute-start(bf16[2,64,1024]{2,1,0:T(8,128)(2,1)S(1)} %collective-permute-done.5), channel_id=1, source_target_pairs={{0,6},{2,0},{4,2},{6,4},{1,7},{3,1},{5,3},{7,5},{8,14},{10,8},{12,... | collective-permute-start | bytes 786440 | tf_op jit(solution)/shard_map/ppermute | solution.py:49
  38.1 16.2 %collective-permute-start.11 = (bf16[2,64,1024]{2,1,0:T(8,128)(2,1)S(1)}, bf16[2,64,1024]{2,1,0:T(8,128)(2,1)S(1)}, u32[]{:S(2)}, u32[]{:S(2)}) collective-permute-start(bf16[2,64,1024]{2,1,0:T(8,128)(2,1)S(1)} %collective-permute-done.5), channel_id=1, source_target_pairs={{0,4},{2,6},{4,0},{6,2},{1,5},{3,7},{5,1},{7,3},{8,12},{10,14},{12... | collective-permute-start | bytes 786440 | tf_op jit(solution)/shard_map/ppermute | solution.py:49
  38.1 16.2 %collective-permute-start.12 = (bf16[2,64,1024]{2,1,0:T(8,128)(2,1)S(1)}, bf16[2,64,1024]{2,1,0:T(8,128)(2,1)S(1)}, u32[]{:S(2)}, u32[]{:S(2)}) collective-permute-start(bf16[2,64,1024]{2,1,0:T(8,128)(2,1)S(1)} %collective-permute-done.5), channel_id=1, source_target_pairs={{0,2},{2,4},{4,6},{6,0},{1,3},{3,5},{5,7},{7,1},{8,10},{10,12},{12... | collective-permute-start | bytes 786440 | tf_op jit(solution)/shard_map/ppermute | solution.py:49
  54.4 194.9 %reduce-scatter.2.cloned.1.call-start = ((), (), s32[]{:S(2)}) async-start(), calls=%async_computation.3 | async-start | bytes 3899392 | tf_op jit(solution)/shard_map/reduce_scatter | solution.py:592
  56.9 21.2 %collective-permute-start.16 = (bf16[1024,128]{1,0:T(8,128)(2,1)S(1)}, bf16[1024,128]{1,0:T(8,128)(2,1)}, u32[]{:S(2)}, u32[]{:S(2)}) collective-permute-start(bf16[1024,128]{1,0:T(8,128)(2,1)S(1)} %pad_maximum_fusion.4), channel_id=1, source_target_pairs={{0,4},{2,6},{4,0},{6,2},{1,5},{3,7},{5,1},{7,3},{8,12},{10,14},{12... | collective-permute-start | bytes 786440 | tf_op jit(solution)/shard_map/ppermute | solution.py:49
  58.6 19.4 %collective-permute-start.17 = (bf16[1024,128]{1,0:T(8,128)(2,1)S(1)}, bf16[1024,128]{1,0:T(8,128)(2,1)}, u32[]{:S(2)}, u32[]{:S(2)}) collective-permute-start(bf16[1024,128]{1,0:T(8,128)(2,1)S(1)} %pad_maximum_fusion.4), channel_id=1, source_target_pairs={{0,2},{2,4},{4,6},{6,0},{1,3},{3,5},{5,7},{7,1},{8,10},{10,12},{12... | collective-permute-start | bytes 786440 | tf_op jit(solution)/shard_map/ppermute | solution.py:49
  58.6 19.4 %collective-permute-start.18 = (bf16[2,64,1024]{2,1,0:T(8,128)(2,1)S(1)}, bf16[2,64,1024]{2,1,0:T(8,128)(2,1)S(1)}, u32[]{:S(2)}, u32[]{:S(2)}) collective-permute-start(bf16[2,64,1024]{2,1,0:T(8,128)(2,1)S(1)} %collective-permute-done.13), channel_id=1, source_target_pairs={{0,6},{2,0},{4,2},{6,4},{1,7},{3,1},{5,3},{7,5},{8,14},{10,8},{12,... | collective-permute-start | bytes 786440 | tf_op jit(solution)/shard_map/ppermute | solution.py:49
  63.2 14.9 %collective-permute-start.19 = (bf16[2,64,1024]{2,1,0:T(8,128)(2,1)S(1)}, bf16[2,64,1024]{2,1,0:T(8,128)(2,1)S(1)}, u32[]{:S(2)}, u32[]{:S(2)}) collective-permute-start(bf16[2,64,1024]{2,1,0:T(8,128)(2,1)S(1)} %collective-permute-done.13), channel_id=1, source_target_pairs={{0,4},{2,6},{4,0},{6,2},{1,5},{3,7},{5,1},{7,3},{8,12},{10,14},{12... | collective-permute-start | bytes 786440 | tf_op jit(solution)/shard_map/ppermute | solution.py:49
  65.6 17.1 %collective-permute-start.20 = (bf16[2,64,1024]{2,1,0:T(8,128)(2,1)S(1)}, bf16[2,64,1024]{2,1,0:T(8,128)(2,1)S(1)}, u32[]{:S(2)}, u32[]{:S(2)}) collective-permute-start(bf16[2,64,1024]{2,1,0:T(8,128)(2,1)S(1)} %collective-permute-done.13), channel_id=1, source_target_pairs={{0,2},{2,4},{4,6},{6,0},{1,3},{3,5},{5,7},{7,1},{8,10},{10,12},{12... | collective-permute-start | bytes 786440 | tf_op jit(solution)/shard_map/ppermute | solution.py:49
  84.6 22.8 %collective-permute-start.28 = (bf16[4,1024,128]{2,1,0:T(8,128)(2,1)S(1)}, bf16[4,1024,128]{2,1,0:T(8,128)(2,1)S(1)}, u32[]{:S(2)}, u32[]{:S(2)}) collective-permute-start(bf16[4,1024,128]{2,1,0:T(8,128)(2,1)S(1)} %pad_maximum_fusion.1.refs_8_), channel_id=1, source_target_pairs={{0,8},{8,0},{1,9},{9,1},{2,10},{10,2},{3,11},{11,3},{4,12},{12,4},... | collective-permute-start | bytes 3145736 | tf_op jit(solution)/shard_map/ppermute | solution.py:67
  91.2 25.8 %collective-permute-start.29 = (bf16[4,2,64,1024]{3,2,1,0:T(8,128)(2,1)S(1)}, bf16[4,2,64,1024]{3,2,1,0:T(8,128)(2,1)}, u32[]{:S(2)}, u32[]{:S(2)}) collective-permute-start(bf16[4,2,64,1024]{3,2,1,0:T(8,128)(2,1)S(1)} %pad_maximum_fusion.2.refs_0_), channel_id=1, source_target_pairs={{0,8},{8,0},{1,9},{9,1},{2,10},{10,2},{3,11},{11,3},{4,12},{12,4},... | collective-permute-start | bytes 3145736 | tf_op jit(solution)/shard_map/ppermute | solution.py:67
  158.7 14.9 %collective-permute-start.36 = (bf16[2,64,1024]{2,1,0:T(8,128)(2,1)S(1)}, bf16[2,64,1024]{2,1,0:T(8,128)(2,1)S(1)}, u32[]{:S(2)}, u32[]{:S(2)}) collective-permute-start(bf16[2,64,1024]{2,1,0:T(8,128)(2,1)S(1)} %fusion.1.refs_0_), channel_id=1, source_target_pairs={{0,2},{2,4},{4,6},{6,0},{1,3},{3,5},{5,7},{7,1},{8,10},{10,12},{12... | collective-permute-start | bytes 786440 | tf_op jit(solution)/shard_map/ppermute | solution.py:49
  192.0 22.1 %all-to-all-start = ((bf16[16,80,384]{2,1,0:T(8,128)(2,1)}), bf16[16,80,384]{2,1,0:T(8,128)(2,1)S(1)}, u32[]{:S(2)}, u32[]{:S(2)}) async-start(bf16[16,80,384]{2,1,0:T(8,128)(2,1)} %get-tuple-element.149), calls=%async_computation | async-start | bytes 1966080 | tf_op jit(solution)/shard_map/all_to_all | solution.py:604
  197.3 20.7 %collective-permute-start.42 = (bf16[2,256,1024]{2,1,0:T(8,128)(2,1)}, bf16[2,256,1024]{2,1,0:T(8,128)(2,1)S(1)}, u32[]{:S(2)}, u32[]{:S(2)}) collective-permute-start(bf16[2,256,1024]{2,1,0:T(8,128)(2,1)} %get-tuple-element.147), channel_id=1, source_target_pairs={{0,8},{8,0},{1,9},{9,1},{2,10},{10,2},{3,11},{11,3},{4,12},{12,4},... | collective-permute-start | bytes 3145736 | tf_op jit(solution)/shard_map/ppermute | solution.py:67
  198.0 20.0 %collective-permute-start.41 = (bf16[2,256,1024]{2,1,0:T(8,128)(2,1)}, bf16[2,256,1024]{2,1,0:T(8,128)(2,1)}, u32[]{:S(2)}, u32[]{:S(2)}) collective-permute-start(bf16[2,256,1024]{2,1,0:T(8,128)(2,1)} %get-tuple-element.145), channel_id=1, source_target_pairs={{0,8},{8,0},{1,9},{9,1},{2,10},{10,2},{3,11},{11,3},{4,12},{12,4},... | collective-permute-start | bytes 3145736 | tf_op jit(solution)/shard_map/ppermute | solution.py:67
  222.9 25.5 %collective-permute-start.44 = (bf16[4,64,1024]{2,1,0:T(8,128)(2,1)}, bf16[4,64,1024]{2,1,0:T(8,128)(2,1)S(1)}, u32[]{:S(2)}, u32[]{:S(2)}) collective-permute-start(bf16[4,64,1024]{2,1,0:T(8,128)(2,1)} %get-tuple-element.151), channel_id=1, source_target_pairs={{0,2},{2,4},{4,6},{6,0},{1,3},{3,5},{5,7},{7,1},{8,10},{10,12},{12... | collective-permute-start | bytes 1572872 | tf_op jit(solution)/shard_map/ppermute | solution.py:49
  222.9 25.5 %collective-permute-start.45 = (bf16[4,64,1024]{2,1,0:T(8,128)(2,1)}, bf16[4,64,1024]{2,1,0:T(8,128)(2,1)S(1)}, u32[]{:S(2)}, u32[]{:S(2)}) collective-permute-start(bf16[4,64,1024]{2,1,0:T(8,128)(2,1)} %get-tuple-element.152), channel_id=1, source_target_pairs={{0,4},{2,6},{4,0},{6,2},{1,5},{3,7},{5,1},{7,3},{8,12},{10,14},{12... | collective-permute-start | bytes 1572872 | tf_op jit(solution)/shard_map/ppermute | solution.py:49
  225.1 24.1 %collective-permute-start.46 = (bf16[4,64,1024]{2,1,0:T(8,128)(2,1)}, bf16[4,64,1024]{2,1,0:T(8,128)(2,1)S(1)}, u32[]{:S(2)}, u32[]{:S(2)}) collective-permute-start(bf16[4,64,1024]{2,1,0:T(8,128)(2,1)} %get-tuple-element.153), channel_id=1, source_target_pairs={{0,6},{2,0},{4,2},{6,4},{1,7},{3,1},{5,3},{7,5},{8,14},{10,8},{12,... | collective-permute-start | bytes 1572872 | tf_op jit(solution)/shard_map/ppermute | solution.py:49
  (67 other events, 526.7 us)
Sparse Core Ops, SparseCore 0:
  54.5 48.1 all-gather.1
  154.1 81.6 reduce-scatter.1

commit v6 on v4

--- a/solution.py
+++ b/solution.py
@@ -572,9 +572,9 @@
     bias = jnp.where(allowed, 0.0, -1e30).astype(bf16)
     qk_gain = jnp.stack([jnp.tile(query_gain, 2), jnp.tile(key_gain, 2)])
 
-    w_ffn, *pieces = tie(w_ffn, *w_att, *x_pieces, cosine, sine, bias, qk_gain, at)
+    w_ffn, *pieces = tie(w_ffn, *w_att, *x_pieces, cosine, sine, bias, qk_gain, at, cotangent_own)
     w_att, x_pieces = pieces[:4], pieces[4:8]
-    cosine, sine, bias, qk_gain, at = pieces[8:]
+    cosine, sine, bias, qk_gain, at, cotangent_own = pieces[8:]
     w_ffn = lax.all_gather(w_ffn, plane, axis=0, tiled=True)
     w_out_chain = from_chain(jnp.concatenate([w[:, nq + 2 * nk :] for w in w_att], axis=0))
     x_chain, x_other = gather_chains(x_pieces)

time: 270 us -> 270 us (level)
  starting transfers between devices: 75.6 us -> 79.3 us
  waiting for transfers between devices: 87.8 us -> 84.2 us
    ppermute x7, waiting for transfers between devices: 9.09 us -> 4.76 us  [swap(): lax.ppermute(value, ('core', 'xl'), [(a * 2 + b, b * 2 + a) for a in rang...]
    ppermute x15, starting transfers between devices: 7.53 us -> 11.2 us  [other_core(): return lax.ppermute(value, 'core', CORE)]
    unnamed x68 -> x70, local copies, waits for them, and re-layouts: 4.86 us -> 5.54 us
where the time goes in v6:
time: 270 us; the launch traced here: 269 us
  waiting for transfers between devices  84.2 us (31%)
  starting transfers between devices  79.3 us (29%)
  Pallas kernels  65.1 us (24%)
  between operations  14.8 us (5%)
  other arithmetic  13.4 us (5%)
  local copies, waits for them, and re-layouts  12.3 us (5%)
    ppermute x24, waiting for transfers between devices, from_z(): return lax.ppermute(value, 'z', [(z, (z - k) % 4) for z in range(4)])  49.3 us
    ppermute x24, starting transfers between devices, from_z(): return lax.ppermute(value, 'z', [(z, (z - k) % 4) for z in range(4)])  30.5 us
    ppermute x7, starting transfers between devices, swap(): lax.ppermute(value, ('core', 'xl'), [(a * 2 + b, b * 2 + a) for a in rang...  19.4 us
    pallas_call x1, Pallas kernels, feed(): pl.pallas_call(feed_kernel, grid=(steps,), in_specs=[rows(width), whole(w...  15.4 us
    pallas_call x1, Pallas kernels, back(): pl.pallas_call(back_kernel, grid=(micro,), in_specs=[part(p) for p in sta...  14.8 us
    ppermute x15, starting transfers between devices, other_core(): return lax.ppermute(value, 'core', CORE)  11.2 us
    pallas_call x1, Pallas kernels, attend(): pl.pallas_call(attend_kernel, grid_spec=pltpu.PrefetchScalarGridSpec(num_...  11 us
    ppermute x4, starting transfers between devices, swap_from_x(): return lax.ppermute(value, ('xh', 'core', 'xl'), perm)  9.65 us
  transfers between devices with their start and end apart: 56, of which 25 were waited for; matrix products, arithmetic and copies ran while one was open for 7% of the time, Pallas kernels for 17%

profile of v6, /device:TPU:1, one launch (start us, length us, event | category | flops | bytes accessed | tf_op | source)
XLA Modules:
  0.0 269.0 jit_solution(13818418008829880329)
XLA Ops:
  8.1 4.5 %collective-permute-start.1 = (bf16[64,384]{1,0:T(8,128)(2,1)S(1)}, bf16[64,384]{1,0:T(8,128)(2,1)S(1)}, u32[]{:S(2)}, u32[]{:S(2)}) collective-permute-start(bf16[64,384]{1,0:T(8,128)(2,1)S(1)} %pad_maximum_fusion.6), channel_id=1, source_target_pairs={{0,0},{1,8},{8,1},{9,9},{16,16},{17,24},{24,17},{25,25},{2,2},{3,1... | collective-permute-start | bytes 147464 | tf_op jit(solution)/shard_map/ppermute | solution.py:59
  14.3 3.4 %collective-permute-start.4 = (bf16[64,384]{1,0:T(8,128)(2,1)S(1)}, bf16[64,384]{1,0:T(8,128)(2,1)S(1)}, u32[]{:S(2)}, u32[]{:S(2)}) collective-permute-start(bf16[64,384]{1,0:T(8,128)(2,1)S(1)} %pad_maximum_fusion.6), channel_id=1, source_target_pairs={{0,1},{1,9},{8,16},{9,24},{16,17},{17,25},{24,0},{25,8},{2,3},{3,1... | collective-permute-start | bytes 147464 | tf_op jit(solution)/shard_map/ppermute | solution.py:59
  23.9 3.6 %collective-permute-start.6 = (s32[2,512]{1,0:T(2,128)}, s32[2,512]{1,0:T(2,128)S(1)}, u32[]{:S(2)}, u32[]{:S(2)}) collective-permute-start(s32[2,512]{1,0:T(2,128)} %param.15), channel_id=1, source_target_pairs={{0,0},{1,8},{8,1},{9,9},{2,2},{3,10},{10,3},{11,11},{4,4},{5,12},{... | collective-permute-start | bytes 12296 | tf_op jit(solution)/shard_map/ppermute | solution.py:43
  29.5 3.6 %collective-permute-start.13 = (bf16[2,64,1024]{2,1,0:T(8,128)(2,1)}, bf16[2,64,1024]{2,1,0:T(8,128)(2,1)S(1)}, u32[]{:S(2)}, u32[]{:S(2)}) collective-permute-start(bf16[2,64,1024]{2,1,0:T(8,128)(2,1)} %param.16), channel_id=1, source_target_pairs={{0,0},{1,8},{8,1},{9,9},{2,2},{3,10},{10,3},{11,11},{4,4},{5,12},{... | collective-permute-start | bytes 786440 | tf_op jit(solution)/shard_map/ppermute | solution.py:43
  34.3 3.8 %collective-permute-start.10 = (bf16[2,64,1024]{2,1,0:T(8,128)(2,1)S(1)}, bf16[2,64,1024]{2,1,0:T(8,128)(2,1)S(1)}, u32[]{:S(2)}, u32[]{:S(2)}) collective-permute-start(bf16[2,64,1024]{2,1,0:T(8,128)(2,1)S(1)} %collective-permute-done.5), channel_id=1, source_target_pairs={{0,6},{2,0},{4,2},{6,4},{1,7},{3,1},{5,3},{7,5},{8,14},{10,8},{12,... | collective-permute-start | bytes 786440 | tf_op jit(solution)/shard_map/ppermute | solution.py:49
  43.9 4.3 %collective-permute-done.7.refs_3_ = bf16[256,384]{1,0:T(8,128)(2,1)S(1)} collective-permute-done((bf16[256,384]{1,0:T(8,128)(2,1)S(1)}, bf16[256,384]{1,0:T(8,128)(2,1)S(1)}, u32[]{:S(2)}, u32[]{:S(2)}) %collective-permute-start.7) | collective-permute-done | bytes 196640 | tf_op jit(solution)/shard_map/ppermute | solution.py:63
  67.0 11.0 %attend.1 = (bf16[1024,128]{1,0:T(8,128)(2,1)}, bf16[1024,1024]{1,0:T(8,128)(2,1)}, bf16[1024,1024]{1,0:T(8,128)(2,1)}, bf16[1024,384]{1,0:T(8,128)(2,1)}, f32[1...) custom-call(s32[4]{0:T(128)} %pad_add_fusion.at_ref, ...), custom_call_target="tpu_custom_call" | custom-call | flops 12000000000 | bytes 10000000 | tf_op jit(solution)/shard_map/attend/pallas_call | solution.py:186
  78.0 4.7 %collective-permute-done.20 = bf16[2,64,1024]{2,1,0:T(8,128)(2,1)S(1)} collective-permute-done((bf16[2,64,1024]{2,1,0:T(8,128)(2,1)S(1)}, bf16[2,64,1024]{2,1,0:T(8,128)(2,1)S(1)}, u32[]{:S(2)}, u32[]{:S(2)}) %collective-permute-start.20) | collective-permute-done | bytes 262176 | tf_op jit(solution)/shard_map/ppermute | solution.py:49
  84.5 3.8 %collective-permute-start.28 = (bf16[4,1024,128]{2,1,0:T(8,128)(2,1)S(1)}, bf16[4,1024,128]{2,1,0:T(8,128)(2,1)S(1)}, u32[]{:S(2)}, u32[]{:S(2)}) collective-permute-start(bf16[4,1024,128]{2,1,0:T(8,128)(2,1)S(1)} %pad_maximum_fusion.1.refs_8_), channel_id=1, source_target_pairs={{0,8},{8,0},{1,9},{9,1},{2,10},{10,2},{3,11},{11,3},{4,12},{12,4},... | collective-permute-start | bytes 3145736 | tf_op jit(solution)/shard_map/ppermute | solution.py:67
  92.3 3.8 %collective-permute-done.21.refs_1_ = bf16[1024,128]{1,0:T(8,128)(2,1)S(1)} collective-permute-done((bf16[1024,128]{1,0:T(8,128)(2,1)S(1)}, bf16[1024,128]{1,0:T(8,128)(2,1)S(1)}, u32[]{:S(2)}, u32[]{:S(2)}) %collective-permute-start.21) | collective-permute-done | bytes 262176 | tf_op jit(solution)/shard_map/ppermute | solution.py:49
  97.6 6.5 %collective-permute-done.23.refs_3_ = bf16[1024,128]{1,0:T(8,128)(2,1)S(1)} collective-permute-done((bf16[1024,128]{1,0:T(8,128)(2,1)S(1)}, bf16[1024,128]{1,0:T(8,128)(2,1)S(1)}, u32[]{:S(2)}, u32[]{:S(2)}) %collective-permute-start.23) | collective-permute-done | bytes 262176 | tf_op jit(solution)/shard_map/ppermute | solution.py:49
  108.4 8.5 %second_norm.1 = (f32[256,1024]{1,0:T(8,128)}, bf16[1024,1024]{1,0:T(8,128)(2,1)}) custom-call(s32[4]{0:T(128)} %pad_add_fusion.at_ref, bf16[1024,128]{1,0:T(8,128)(2,1)} %get-tuple-element.105.refs_0_.refs_15_, bf16[1024,128]{1,0:T(8,128)(2,1)} %copy-done.28, bf16[1024,128]{1,0:T(8,128)(2,1)} %copy-done.29, bf16[1024,128]{1,0:T(8,128)(2,1)} %copy-done.30, ...), custom_call_target="tpu_custom_call" | custom-call | flops 3000000000 | bytes 10000000 | tf_op jit(solution)/shard_map/second_norm/pallas_call | solution.py:256
  117.0 15.4 %feed.1 = (bf16[1024,576]{1,0:T(8,128)(2,1)}, bf16[1024,1152]{1,0:T(8,128)(2,1)}, bf16[2,256,1024]{2,1,0:T(8,128)(2,1)}, bf16[2,256,1024]{2,1,0:T(8,128)(2,1)}, ...) custom-call(bf16[1024,1024]{1,0:T(8,128)(2,1)} %get-tuple-element.115.second_ref, ...), custom_call_target="tpu_custom_call" | custom-call | flops 8999999488 | bytes 10000000 | tf_op jit(solution)/shard_map/feed/pallas_call | solution.py:341
  142.3 8.8 %weights_back.1 = bf16[1024,1728]{1,0:T(8,128)(2,1)} custom-call(bf16[1024,1024]{1,0:T(8,128)(2,1)} %get-tuple-element.115.second_ref, bf16[1024,1024]{1,0:T(8,128)(2,1)} %get-tuple-element.124.up_ref, bf16[1024,1152]{1,0:T(8,128)(2,1)} %get-tuple-element.125.low_ref, bf16[1024,576]{1,0:T(8,128)(2,1)} %get-tuple-element.126.inner_ref), custom_call_target="tpu_custom_call" | custom-call | flops 4000000000 | bytes 10000000 | tf_op jit(solution)/shard_map/weights_back/pallas_call | solution.py:368
  159.1 10.0 %collective-permute-done.34.refs_1_ = bf16[2,64,1024]{2,1,0:T(8,128)(2,1)S(1)} collective-permute-done((bf16[2,64,1024]{2,1,0:T(8,128)(2,1)S(1)}, bf16[2,64,1024]{2,1,0:T(8,128)(2,1)S(1)}, u32[]{:S(2)}, u32[]{:S(2)}) %collective-permute-start.34) | collective-permute-done | bytes 262176 | tf_op jit(solution)/shard_map/ppermute | solution.py:49
  169.1 4.4 %collective-permute-done.36.refs_3_ = bf16[2,64,1024]{2,1,0:T(8,128)(2,1)S(1)} collective-permute-done((bf16[2,64,1024]{2,1,0:T(8,128)(2,1)S(1)}, bf16[2,64,1024]{2,1,0:T(8,128)(2,1)S(1)}, u32[]{:S(2)}, u32[]{:S(2)}) %collective-permute-start.36) | collective-permute-done | bytes 262176 | tf_op jit(solution)/shard_map/ppermute | solution.py:49
  177.5 14.8 %back.1 = (bf16[2,256,1024]{2,1,0:T(8,128)(2,1)}, bf16[2,256,1024]{2,1,0:T(8,128)(2,1)}, bf16[16,80,384]{2,1,0:T(8,128)(2,1)}) custom-call(bf16[2,64,1024]{2,1,0:T(8,128)(2,1)} %copy-done.1, bf16[2,64,1024]{2,1,0:T(8,128)(2,1)} %copy-done.11, bf16[2,64,1024]{2,1,0:T(8,128)(2,1)} %copy-done.12, bf16[2,64,1024]{2,1,0:T(8,128)(2,1)} %copy-done.13, ...), custom_call_target="tpu_custom_call" | custom-call | flops 1000000 | bytes 10000 | tf_op jit(solution)/shard_map/back/pallas_call | solution.py:471
  192.7 5.3 %all-to-all-start = ((bf16[16,80,384]{2,1,0:T(8,128)(2,1)}), bf16[16,80,384]{2,1,0:T(8,128)(2,1)S(1)}, u32[]{:S(2)}, u32[]{:S(2)}) async-start(bf16[16,80,384]{2,1,0:T(8,128)(2,1)} %get-tuple-element.149), calls=%async_computation | async-start | bytes 1966080 | tf_op jit(solution)/shard_map/all_to_all | solution.py:609
  199.1 3.9 %split.3 = (f32[4,64,1024]{2,1,0:T(8,128)}, bf16[4,64,1024]{2,1,0:T(8,128)(2,1)}, bf16[4,64,1024]{2,1,0:T(8,128)(2,1)}, bf16[4,64,1024]{2,1,0:T(8,128)(2,1)}) custom-call(bf16[2,256,1024]{2,1,0:T(8,128)(2,1)} %get-tuple-element.144.refs_0_, bf16[2,256,1024]{2,1,0:T(8,128)(2,1)} %collective-permute-done.41.refs_1_, ...), custom_call_target="tpu_custom_call" | custom-call | tf_op jit(solution)/shard_map/split/pallas_call | solution.py:515
  205.7 9.4 %all-to-all-done = bf16[16,80,384]{2,1,0:T(8,128)(2,1)S(1)} async-done(((bf16[16,80,384]{2,1,0:T(8,128)(2,1)}), bf16[16,80,384]{2,1,0:T(8,128)(2,1)S(1)}, u32[]{:S(2)}, u32[]{:S(2)}) %all-to-all-start) | async-done | bytes 983072 | tf_op jit(solution)/shard_map/all_to_all | solution.py:609
  215.1 13.7 %collective-permute-done.43 = bf16[4,64,1024]{2,1,0:T(8,128)(2,1)S(1)} collective-permute-done((bf16[4,64,1024]{2,1,0:T(8,128)(2,1)}, bf16[4,64,1024]{2,1,0:T(8,128)(2,1)S(1)}, u32[]{:S(2)}, u32[]{:S(2)}) %collective-permute-start.43) | collective-permute-done | bytes 524320 | tf_op jit(solution)/shard_map/ppermute | solution.py:49
  229.1 7.3 %reduce-scatter.2.cloned.1.call-done = bf16[64,1728]{1,0:T(8,128)(2,1)} async-done(((bf16[1024,1728]{1,0:T(8,128)(2,1)}), bf16[64,1728]{1,0:T(8,128)(2,1)}) %reduce-scatter.2.cloned.1.call-update) | async-done | bytes 221200 | tf_op jit(solution)/shard_map/reduce_scatter | solution.py:597
  247.5 3.7 %collective-permute-start.46 = (bf16[4,64,1024]{2,1,0:T(8,128)(2,1)S(1)}, bf16[4,64,1024]{2,1,0:T(8,128)(2,1)S(1)}, u32[]{:S(2)}, u32[]{:S(2)}) collective-permute-start(bf16[4,64,1024]{2,1,0:T(8,128)(2,1)S(1)} %pad_maximum_fusion.3), channel_id=1, source_target_pairs={{0,0},{1,8},{8,1},{9,9},{2,2},{3,10},{10,3},{11,11},{4,4},{5,12},{... | collective-permute-start | bytes 1572872 | tf_op jit(solution)/shard_map/ppermute | solution.py:43
  254.4 4.7 %collective-permute-done.47 = f32[64,384]{1,0:T(8,128)S(1)} collective-permute-done((f32[64,384]{1,0:T(8,128)S(1)}, f32[64,384]{1,0:T(8,128)S(1)}, u32[]{:S(2)}, u32[]{:S(2)}) %collective-permute-start.47) | collective-permute-done | bytes 98336 | tf_op jit(solution)/shard_map/ppermute | solution.py:43
  (230 shorter events, 91.2 us)
Async XLA Ops:
  7.2 109.8 %all-gather.2.cloned.1.call-start = ((), (), s32[]{:S(2)}) async-start(), calls=%async_computation.2 | async-start | bytes 3899392 | tf_op jit(solution)/shard_map/all_gather | solution.py:578
  8.1 15.8 %collective-permute-start.1 = (bf16[64,384]{1,0:T(8,128)(2,1)S(1)}, bf16[64,384]{1,0:T(8,128)(2,1)S(1)}, u32[]{:S(2)}, u32[]{:S(2)}) collective-permute-start(bf16[64,384]{1,0:T(8,128)(2,1)S(1)} %pad_maximum_fusion.6), channel_id=1, source_target_pairs={{0,0},{1,8},{8,1},{9,9},{16,16},{17,24},{24,17},{25,25},{2,2},{3,1... | collective-permute-start | bytes 147464 | tf_op jit(solution)/shard_map/ppermute | solution.py:59
  12.6 14.9 %collective-permute-start.2 = (bf16[64,384]{1,0:T(8,128)(2,1)S(1)}, bf16[64,384]{1,0:T(8,128)(2,1)S(1)}, u32[]{:S(2)}, u32[]{:S(2)}) collective-permute-start(bf16[64,384]{1,0:T(8,128)(2,1)S(1)} %pad_maximum_fusion.6), channel_id=1, source_target_pairs={{0,17},{1,25},{8,0},{9,8},{16,1},{17,9},{24,16},{25,24},{2,19},{3,... | collective-permute-start | bytes 147464 | tf_op jit(solution)/shard_map/ppermute | solution.py:59
  12.7 16.8 %collective-permute-start.3 = (bf16[64,384]{1,0:T(8,128)(2,1)S(1)}, bf16[64,384]{1,0:T(8,128)(2,1)S(1)}, u32[]{:S(2)}, u32[]{:S(2)}) collective-permute-start(bf16[64,384]{1,0:T(8,128)(2,1)S(1)} %pad_maximum_fusion.6), channel_id=1, source_target_pairs={{0,16},{1,24},{8,17},{9,25},{16,0},{17,8},{24,1},{25,9},{2,18},{3,... | collective-permute-start | bytes 147464 | tf_op jit(solution)/shard_map/ppermute | solution.py:59
  14.3 18.8 %collective-permute-start.4 = (bf16[64,384]{1,0:T(8,128)(2,1)S(1)}, bf16[64,384]{1,0:T(8,128)(2,1)S(1)}, u32[]{:S(2)}, u32[]{:S(2)}) collective-permute-start(bf16[64,384]{1,0:T(8,128)(2,1)S(1)} %pad_maximum_fusion.6), channel_id=1, source_target_pairs={{0,1},{1,9},{8,16},{9,24},{16,17},{17,25},{24,0},{25,8},{2,3},{3,1... | collective-permute-start | bytes 147464 | tf_op jit(solution)/shard_map/ppermute | solution.py:59
  17.7 15.5 %collective-permute-start.5 = (bf16[2,64,1024]{2,1,0:T(8,128)(2,1)}, bf16[2,64,1024]{2,1,0:T(8,128)(2,1)S(1)}, u32[]{:S(2)}, u32[]{:S(2)}) collective-permute-start(bf16[2,64,1024]{2,1,0:T(8,128)(2,1)} %param.14), channel_id=1, source_target_pairs={{0,0},{1,8},{8,1},{9,9},{2,2},{3,10},{10,3},{11,11},{4,4},{5,12},{... | collective-permute-start | bytes 786440 | tf_op jit(solution)/shard_map/ppermute | solution.py:43
  34.3 20.1 %collective-permute-start.10 = (bf16[2,64,1024]{2,1,0:T(8,128)(2,1)S(1)}, bf16[2,64,1024]{2,1,0:T(8,128)(2,1)S(1)}, u32[]{:S(2)}, u32[]{:S(2)}) collective-permute-start(bf16[2,64,1024]{2,1,0:T(8,128)(2,1)S(1)} %collective-permute-done.5), channel_id=1, source_target_pairs={{0,6},{2,0},{4,2},{6,4},{1,7},{3,1},{5,3},{7,5},{8,14},{10,8},{12,... | collective-permute-start | bytes 786440 | tf_op jit(solution)/shard_map/ppermute | solution.py:49
  38.1 16.2 %collective-permute-start.11 = (bf16[2,64,1024]{2,1,0:T(8,128)(2,1)S(1)}, bf16[2,64,1024]{2,1,0:T(8,128)(2,1)S(1)}, u32[]{:S(2)}, u32[]{:S(2)}) collective-permute-start(bf16[2,64,1024]{2,1,0:T(8,128)(2,1)S(1)} %collective-permute-done.5), channel_id=1, source_target_pairs={{0,4},{2,6},{4,0},{6,2},{1,5},{3,7},{5,1},{7,3},{8,12},{10,14},{12... | collective-permute-start | bytes 786440 | tf_op jit(solution)/shard_map/ppermute | solution.py:49
  38.1 16.2 %collective-permute-start.12 = (bf16[2,64,1024]{2,1,0:T(8,128)(2,1)S(1)}, bf16[2,64,1024]{2,1,0:T(8,128)(2,1)S(1)}, u32[]{:S(2)}, u32[]{:S(2)}) collective-permute-start(bf16[2,64,1024]{2,1,0:T(8,128)(2,1)S(1)} %collective-permute-done.5), channel_id=1, source_target_pairs={{0,2},{2,4},{4,6},{6,0},{1,3},{3,5},{5,7},{7,1},{8,10},{10,12},{12... | collective-permute-start | bytes 786440 | tf_op jit(solution)/shard_map/ppermute | solution.py:49
  54.4 182.0 %reduce-scatter.2.cloned.1.call-start = ((), (), s32[]{:S(2)}) async-start(), calls=%async_computation.3 | async-start | bytes 3899392 | tf_op jit(solution)/shard_map/reduce_scatter | solution.py:597
  56.9 21.1 %collective-permute-start.16 = (bf16[1024,128]{1,0:T(8,128)(2,1)S(1)}, bf16[1024,128]{1,0:T(8,128)(2,1)S(1)}, u32[]{:S(2)}, u32[]{:S(2)}) collective-permute-start(bf16[1024,128]{1,0:T(8,128)(2,1)S(1)} %pad_maximum_fusion.4), channel_id=1, source_target_pairs={{0,4},{2,6},{4,0},{6,2},{1,5},{3,7},{5,1},{7,3},{8,12},{10,14},{12... | collective-permute-start | bytes 786440 | tf_op jit(solution)/shard_map/ppermute | solution.py:49
  58.6 19.4 %collective-permute-start.17 = (bf16[1024,128]{1,0:T(8,128)(2,1)S(1)}, bf16[1024,128]{1,0:T(8,128)(2,1)}, u32[]{:S(2)}, u32[]{:S(2)}) collective-permute-start(bf16[1024,128]{1,0:T(8,128)(2,1)S(1)} %pad_maximum_fusion.4), channel_id=1, source_target_pairs={{0,2},{2,4},{4,6},{6,0},{1,3},{3,5},{5,7},{7,1},{8,10},{10,12},{12... | collective-permute-start | bytes 786440 | tf_op jit(solution)/shard_map/ppermute | solution.py:49
  58.6 19.4 %collective-permute-start.18 = (bf16[2,64,1024]{2,1,0:T(8,128)(2,1)S(1)}, bf16[2,64,1024]{2,1,0:T(8,128)(2,1)S(1)}, u32[]{:S(2)}, u32[]{:S(2)}) collective-permute-start(bf16[2,64,1024]{2,1,0:T(8,128)(2,1)S(1)} %collective-permute-done.13), channel_id=1, source_target_pairs={{0,6},{2,0},{4,2},{6,4},{1,7},{3,1},{5,3},{7,5},{8,14},{10,8},{12,... | collective-permute-start | bytes 786440 | tf_op jit(solution)/shard_map/ppermute | solution.py:49
  63.1 15.0 %collective-permute-start.19 = (bf16[2,64,1024]{2,1,0:T(8,128)(2,1)S(1)}, bf16[2,64,1024]{2,1,0:T(8,128)(2,1)S(1)}, u32[]{:S(2)}, u32[]{:S(2)}) collective-permute-start(bf16[2,64,1024]{2,1,0:T(8,128)(2,1)S(1)} %collective-permute-done.13), channel_id=1, source_target_pairs={{0,4},{2,6},{4,0},{6,2},{1,5},{3,7},{5,1},{7,3},{8,12},{10,14},{12... | collective-permute-start | bytes 786440 | tf_op jit(solution)/shard_map/ppermute | solution.py:49
  65.5 17.2 %collective-permute-start.20 = (bf16[2,64,1024]{2,1,0:T(8,128)(2,1)S(1)}, bf16[2,64,1024]{2,1,0:T(8,128)(2,1)S(1)}, u32[]{:S(2)}, u32[]{:S(2)}) collective-permute-start(bf16[2,64,1024]{2,1,0:T(8,128)(2,1)S(1)} %collective-permute-done.13), channel_id=1, source_target_pairs={{0,2},{2,4},{4,6},{6,0},{1,3},{3,5},{5,7},{7,1},{8,10},{10,12},{12... | collective-permute-start | bytes 786440 | tf_op jit(solution)/shard_map/ppermute | solution.py:49
  84.5 22.8 %collective-permute-start.28 = (bf16[4,1024,128]{2,1,0:T(8,128)(2,1)S(1)}, bf16[4,1024,128]{2,1,0:T(8,128)(2,1)S(1)}, u32[]{:S(2)}, u32[]{:S(2)}) collective-permute-start(bf16[4,1024,128]{2,1,0:T(8,128)(2,1)S(1)} %pad_maximum_fusion.1.refs_8_), channel_id=1, source_target_pairs={{0,8},{8,0},{1,9},{9,1},{2,10},{10,2},{3,11},{11,3},{4,12},{12,4},... | collective-permute-start | bytes 3145736 | tf_op jit(solution)/shard_map/ppermute | solution.py:67
  91.1 25.8 %collective-permute-start.29 = (bf16[4,2,64,1024]{3,2,1,0:T(8,128)(2,1)S(1)}, bf16[4,2,64,1024]{3,2,1,0:T(8,128)(2,1)}, u32[]{:S(2)}, u32[]{:S(2)}) collective-permute-start(bf16[4,2,64,1024]{3,2,1,0:T(8,128)(2,1)S(1)} %pad_maximum_fusion.2.refs_0_), channel_id=1, source_target_pairs={{0,8},{8,0},{1,9},{9,1},{2,10},{10,2},{3,11},{11,3},{4,12},{12,4},... | collective-permute-start | bytes 3145736 | tf_op jit(solution)/shard_map/ppermute | solution.py:67
  158.6 14.9 %collective-permute-start.36 = (bf16[2,64,1024]{2,1,0:T(8,128)(2,1)S(1)}, bf16[2,64,1024]{2,1,0:T(8,128)(2,1)S(1)}, u32[]{:S(2)}, u32[]{:S(2)}) collective-permute-start(bf16[2,64,1024]{2,1,0:T(8,128)(2,1)S(1)} %fusion.1.refs_0_), channel_id=1, source_target_pairs={{0,2},{2,4},{4,6},{6,0},{1,3},{3,5},{5,7},{7,1},{8,10},{10,12},{12... | collective-permute-start | bytes 786440 | tf_op jit(solution)/shard_map/ppermute | solution.py:49
  174.6 23.4 %collective-permute-start.42 = (bf16[2,256,1024]{2,1,0:T(8,128)(2,1)}, bf16[2,256,1024]{2,1,0:T(8,128)(2,1)S(1)}, u32[]{:S(2)}, u32[]{:S(2)}) collective-permute-start(bf16[2,256,1024]{2,1,0:T(8,128)(2,1)} %get-tuple-element.147), channel_id=1, source_target_pairs={{0,8},{8,0},{1,9},{9,1},{2,10},{10,2},{3,11},{11,3},{4,12},{12,4},... | collective-permute-start | bytes 3145736 | tf_op jit(solution)/shard_map/ppermute | solution.py:67
  192.7 22.4 %all-to-all-start = ((bf16[16,80,384]{2,1,0:T(8,128)(2,1)}), bf16[16,80,384]{2,1,0:T(8,128)(2,1)S(1)}, u32[]{:S(2)}, u32[]{:S(2)}) async-start(bf16[16,80,384]{2,1,0:T(8,128)(2,1)} %get-tuple-element.149), calls=%async_computation | async-start | bytes 1966080 | tf_op jit(solution)/shard_map/all_to_all | solution.py:609
  203.0 25.8 %collective-permute-start.43 = (bf16[4,64,1024]{2,1,0:T(8,128)(2,1)}, bf16[4,64,1024]{2,1,0:T(8,128)(2,1)S(1)}, u32[]{:S(2)}, u32[]{:S(2)}) collective-permute-start(bf16[4,64,1024]{2,1,0:T(8,128)(2,1)} %get-tuple-element.151), channel_id=1, source_target_pairs={{0,2},{2,4},{4,6},{6,0},{1,3},{3,5},{5,7},{7,1},{8,10},{10,12},{12... | collective-permute-start | bytes 1572872 | tf_op jit(solution)/shard_map/ppermute | solution.py:49
  203.0 25.8 %collective-permute-start.44 = (bf16[4,64,1024]{2,1,0:T(8,128)(2,1)}, bf16[4,64,1024]{2,1,0:T(8,128)(2,1)S(1)}, u32[]{:S(2)}, u32[]{:S(2)}) collective-permute-start(bf16[4,64,1024]{2,1,0:T(8,128)(2,1)} %get-tuple-element.152), channel_id=1, source_target_pairs={{0,4},{2,6},{4,0},{6,2},{1,5},{3,7},{5,1},{7,3},{8,12},{10,14},{12... | collective-permute-start | bytes 1572872 | tf_op jit(solution)/shard_map/ppermute | solution.py:49
  204.6 24.6 %collective-permute-start.45 = (bf16[4,64,1024]{2,1,0:T(8,128)(2,1)}, bf16[4,64,1024]{2,1,0:T(8,128)(2,1)}, u32[]{:S(2)}, u32[]{:S(2)}) collective-permute-start(bf16[4,64,1024]{2,1,0:T(8,128)(2,1)} %get-tuple-element.153), channel_id=1, source_target_pairs={{0,6},{2,0},{4,2},{6,4},{1,7},{3,1},{5,3},{7,5},{8,14},{10,8},{12,... | collective-permute-start | bytes 1572872 | tf_op jit(solution)/shard_map/ppermute | solution.py:49
  238.8 21.6 %collective-permute-start.48 = (bf16[64,1728]{1,0:T(8,128)(2,1)}, bf16[64,1728]{1,0:T(8,128)(2,1)S(1)}, u32[]{:S(2)}, u32[]{:S(2)}) collective-permute-start(bf16[64,1728]{1,0:T(8,128)(2,1)} %reduce-scatter.2.cloned.1.call-done), channel_id=1, source_target_pairs={{0,0},{1,8},{8,1},{9,9},{2,2},{3,10},{10,3},{11,11},{4,4},{5,12},{... | collective-permute-start | bytes 663560 | tf_op jit(solution)/shard_map/ppermute | solution.py:43
  (67 other events, 492.4 us)
Sparse Core Ops, SparseCore 0:
  54.5 48.1 all-gather.1
  154.0 82.3 reduce-scatter.1
